TPU v7x, 512 devices: a whole 4x8x8 slice. The times are simulated.
512 devices in a mesh: grp: 16 (over z, core), ang: 32 (over x, y).
Axes of the slice: x: 4, y: 8, z: 8, core: 2. Of those that a mesh axis runs over, the one named last changes fastest.
Arguments:
- slab_views: bfloat16 [16, 32, 1024, 1024], P('grp', None, 'ang'), may hold values from -6 to 6
- footprint: int32 [16, 32, 8], P('grp'), may hold values from -1 to 31, as said below
- row_shift: float32 [16, 32], P('grp'), may hold values from 0 to 16
- stretch: float32 [16, 32], P('grp'), may hold values from 0.8 to 0.95
- projections: bfloat16 [32, 2, 2048, 1024], P('ang', None, 'grp'), may hold values from -6 to 6
Outputs:
- row_grad: bfloat16 [32, 2, 2048, 1024], P('ang', None, 'grp')
- filter_grad: float32 [2, 16, 512], P(None, 'grp')
Inputs may be any that keep to these rules, and one draw needn't show every extreme that they name: `footprint`: each list starts with 4 to 8 consecutive tile numbers and is padded with -1 after them; in every draw one list is full and ends at the last tile.
All inputs are finite; a program needn't handle non-finite values.
Results may differ from a plain program's by a relative error of at most 0.0065.
Values may be sent and summed in bfloat16 or wider, within the bound.
No kernel may reach another device: no remote copies, remote signals or barrier semaphores. Data moves between devices by JAX's collectives and lax.ppermute only.
A program may use at most 128 MiB of HBM per device.

v0:
```python
import math

import jax
import jax.numpy as jnp
from jax import lax
from jax.sharding import PartitionSpec as P

TR = 128
KF = 8
SZ = 1024
TPO = 2


angle_block = 2


def footprint_weights(counts, offsets, stretch, entries):
    magnify = (TR * counts).astype(jnp.float32) * stretch / SZ
    row_pos = jnp.arange(TR, dtype=jnp.float32)
    depth_pos = jnp.arange(SZ, dtype=jnp.float32)
    band_pos = (TR * entries).astype(jnp.float32)[:, :, None, None] + row_pos[None, None, :, None]
    voxel_pos = (
        offsets[:, None, None, None] + magnify[:, None, None, None] * depth_pos[None, None, None, :]
    )
    weights = jnp.maximum(1.0 - jnp.abs(band_pos - voxel_pos) / magnify[:, None, None, None], 0.0)
    live = (entries < counts[:, None])[:, :, None, None]
    return jnp.where(live, weights, 0.0).astype(jnp.bfloat16)


def dft_basis(columns):
    column_idx = jnp.arange(columns, dtype=jnp.int32)[:, None]
    freq_idx = jnp.arange(columns // 2, dtype=jnp.int32)[None, :]
    phases = (column_idx * freq_idx % columns).astype(jnp.float32) * (2.0 * math.pi / columns)
    return jnp.concatenate([jnp.cos(phases), jnp.sin(phases)], axis=1).astype(jnp.bfloat16)


def body(slab_views, footprint, row_shift, stretch, projections):
    n_grp = lax.axis_size("grp")
    owner = lax.axis_index("grp")
    slab_view = slab_views[0]
    lists = footprint[0]
    offsets = row_shift[0]
    stretches = stretch[0]
    angles = lists.shape[0]
    narrow = slab_view.shape[1]
    slots_per = (KF + n_grp - 1) // n_grp
    owned_tiles = jnp.arange(TPO, dtype=jnp.int32) * n_grp + owner
    counts_all = jnp.sum((lists >= 0).astype(jnp.int32), axis=-1)
    blocks = angles // angle_block
    padded = slots_per * n_grp

    def one_block(carry, block_id):
        first_angle = block_id * angle_block
        block_view = lax.dynamic_slice_in_dim(slab_view, first_angle, angle_block, 0)
        block_lists = lax.dynamic_slice_in_dim(lists, first_angle, angle_block, 0)
        block_counts = lax.dynamic_slice_in_dim(counts_all, first_angle, angle_block, 0)
        block_shift = lax.dynamic_slice_in_dim(offsets, first_angle, angle_block, 0)
        block_stretch = lax.dynamic_slice_in_dim(stretches, first_angle, angle_block, 0)
        entries = jnp.broadcast_to(jnp.arange(KF, dtype=jnp.int32)[None, :], (angle_block, KF))
        weights = footprint_weights(block_counts, block_shift, block_stretch, entries)
        contrib = jnp.einsum(
            "akrz,acz->akrc", weights, block_view, preferred_element_type=jnp.float32
        ).astype(jnp.bfloat16)
        contrib = jnp.pad(contrib, ((0, 0), (0, padded - KF), (0, 0), (0, 0)))
        contrib = contrib.reshape(angle_block, slots_per, n_grp, TR, narrow)
        tile_ids = jnp.pad(block_lists, ((0, 0), (0, padded - KF)), constant_values=-1)
        tile_ids = tile_ids.reshape(angle_block, slots_per, n_grp)
        first_tile = block_lists[:, 0]
        rotation = (jnp.arange(n_grp, dtype=jnp.int32)[None, :] - first_tile[:, None]) % n_grp
        permute = (
            jnp.arange(n_grp, dtype=jnp.int32)[None, None, :] == rotation[:, :, None]
        ).astype(jnp.bfloat16)
        sending = jnp.einsum(
            "aom,acmrw->oacrw", permute, contrib, preferred_element_type=jnp.float32
        ).astype(jnp.bfloat16)
        gather_idx = rotation[:, None, :]
        send_ids = jnp.transpose(jnp.take_along_axis(tile_ids, gather_idx, axis=2), (2, 0, 1))
        received, recv_ids = (
            lax.all_to_all(sending, "grp", split_axis=0, concat_axis=0, tiled=True),
            lax.all_to_all(send_ids, "grp", split_axis=0, concat_axis=0, tiled=True),
        )
        select = (recv_ids[:, :, :, None] == owned_tiles[None, None, None, :]).astype(jnp.bfloat16)
        partial_value = jnp.einsum(
            "sacp,sacrw->aprw", select, received, preferred_element_type=jnp.float32
        )
        return (carry, partial_value)

    _, parts = lax.scan(one_block, jnp.zeros((), jnp.float32), jnp.arange(blocks, dtype=jnp.int32))
    detector = parts.reshape(angles, TPO, TR, narrow)
    summed = detector.astype(jnp.bfloat16)
    row_grad = lax.all_to_all(summed, "ang", split_axis=0, concat_axis=3, tiled=True)
    columns = row_grad.shape[3]
    basis = dft_basis(columns)
    n_freq = columns // 2
    spec_grad = jnp.dot(row_grad.reshape(-1, columns), basis, preferred_element_type=jnp.float32)
    spec_proj = jnp.dot(projections.reshape(-1, columns), basis, preferred_element_type=jnp.float32)
    product = (
        spec_grad[:, :n_freq] * spec_proj[:, :n_freq]
        + spec_grad[:, n_freq:] * spec_proj[:, n_freq:]
    )
    local_angles = row_grad.shape[0]
    partial_grad = jnp.sum(product.reshape(local_angles, TPO, TR, n_freq), axis=(0, 2))
    total_grad = lax.psum(partial_grad, "ang")
    filter_grad = (total_grad * (1.0 / (columns * angles)))[:, None, :]
    return (row_grad, filter_grad)


def solution(mesh):
    return jax.shard_map(
        body,
        mesh=mesh,
        in_specs=(
            P("grp", None, "ang", None),
            P("grp", None, None),
            P("grp", None),
            P("grp", None),
            P("ang", None, "grp", None),
        ),
        out_specs=(P("ang", None, "grp", None), P(None, "grp", None)),
        check_vma=False,
    )
```

profile of v0, /device:TPU:8, one launch (start us, length us, event | category | flops | bytes accessed | tf_op | source)
XLA Modules:
  0.0 617.6 jit_solution(6685439340431644844)
XLA Ops:
  1.4 512.8 %while.13 = (s32[]{:T(128)}, bf16[16,2,2,128,32]{3,2,4,1,0:T(2,128)(2,1)S(1)}, s32[16]{0:T(128)S(1)}, s32[32,8]{0,1:T(8,128)}, s32[32]{0:T(128)S(1)}, /*index=5*...) while((s32[]{:T(128)}, ...), condition=%wide.region_2.3_spmd.clone, body=%wide.region_1.2_spmd.clone.sunk | while | flops 153821392 | bytes 2609731 | solution.py:88
  5.2 10.4 %all-to-all-start.1 = ((s32[16,2,1]{1,2,0:T(1,128)}), s32[16,2,1]{1,2,0:T(1,128)S(1)}, u32[]{:S(2)}, u32[]{:S(2)}) async-start(s32[16,2,1]{1,2,0:T(1,128)} %copy.44), calls=%async_computation.1 | async-start | bytes 16384 | tf_op jit(solution)/shard_map/while/body/eval_jaxpr/all_to_all | solution.py:80
  28.7 11.1 %all-to-all-done = bf16[16,2,1,128,32]{3,4,1,2,0:T(8,128)(2,1)S(1)} async-done(((bf16[16,2,1,128,32]{3,4,1,2,0:T(8,128)(2,1)}), bf16[16,2,1,128,32]{3,4,1,2,0:T(8,128)(2,1)S(1)}, u32[]{:S(2)}, u32[]{:S(2)}) %all-to-all-start) | async-done | bytes 262176 | tf_op jit(solution)/shard_map/while/body/eval_jaxpr/all_to_all | solution.py:79
  60.3 11.1 %all-to-all-done = bf16[16,2,1,128,32]{3,4,1,2,0:T(8,128)(2,1)S(1)} async-done(((bf16[16,2,1,128,32]{3,4,1,2,0:T(8,128)(2,1)}), bf16[16,2,1,128,32]{3,4,1,2,0:T(8,128)(2,1)S(1)}, u32[]{:S(2)}, u32[]{:S(2)}) %all-to-all-start) | async-done | bytes 262176 | tf_op jit(solution)/shard_map/while/body/eval_jaxpr/all_to_all | solution.py:79
  91.9 11.1 %all-to-all-done = bf16[16,2,1,128,32]{3,4,1,2,0:T(8,128)(2,1)S(1)} async-done(((bf16[16,2,1,128,32]{3,4,1,2,0:T(8,128)(2,1)}), bf16[16,2,1,128,32]{3,4,1,2,0:T(8,128)(2,1)S(1)}, u32[]{:S(2)}, u32[]{:S(2)}) %all-to-all-start) | async-done | bytes 262176 | tf_op jit(solution)/shard_map/while/body/eval_jaxpr/all_to_all | solution.py:79
  123.5 11.1 %all-to-all-done = bf16[16,2,1,128,32]{3,4,1,2,0:T(8,128)(2,1)S(1)} async-done(((bf16[16,2,1,128,32]{3,4,1,2,0:T(8,128)(2,1)}), bf16[16,2,1,128,32]{3,4,1,2,0:T(8,128)(2,1)S(1)}, u32[]{:S(2)}, u32[]{:S(2)}) %all-to-all-start) | async-done | bytes 262176 | tf_op jit(solution)/shard_map/while/body/eval_jaxpr/all_to_all | solution.py:79
  155.1 11.1 %all-to-all-done = bf16[16,2,1,128,32]{3,4,1,2,0:T(8,128)(2,1)S(1)} async-done(((bf16[16,2,1,128,32]{3,4,1,2,0:T(8,128)(2,1)}), bf16[16,2,1,128,32]{3,4,1,2,0:T(8,128)(2,1)S(1)}, u32[]{:S(2)}, u32[]{:S(2)}) %all-to-all-start) | async-done | bytes 262176 | tf_op jit(solution)/shard_map/while/body/eval_jaxpr/all_to_all | solution.py:79
  186.7 11.1 %all-to-all-done = bf16[16,2,1,128,32]{3,4,1,2,0:T(8,128)(2,1)S(1)} async-done(((bf16[16,2,1,128,32]{3,4,1,2,0:T(8,128)(2,1)}), bf16[16,2,1,128,32]{3,4,1,2,0:T(8,128)(2,1)S(1)}, u32[]{:S(2)}, u32[]{:S(2)}) %all-to-all-start) | async-done | bytes 262176 | tf_op jit(solution)/shard_map/while/body/eval_jaxpr/all_to_all | solution.py:79
  218.4 11.1 %all-to-all-done = bf16[16,2,1,128,32]{3,4,1,2,0:T(8,128)(2,1)S(1)} async-done(((bf16[16,2,1,128,32]{3,4,1,2,0:T(8,128)(2,1)}), bf16[16,2,1,128,32]{3,4,1,2,0:T(8,128)(2,1)S(1)}, u32[]{:S(2)}, u32[]{:S(2)}) %all-to-all-start) | async-done | bytes 262176 | tf_op jit(solution)/shard_map/while/body/eval_jaxpr/all_to_all | solution.py:79
  250.0 11.1 %all-to-all-done = bf16[16,2,1,128,32]{3,4,1,2,0:T(8,128)(2,1)S(1)} async-done(((bf16[16,2,1,128,32]{3,4,1,2,0:T(8,128)(2,1)}), bf16[16,2,1,128,32]{3,4,1,2,0:T(8,128)(2,1)S(1)}, u32[]{:S(2)}, u32[]{:S(2)}) %all-to-all-start) | async-done | bytes 262176 | tf_op jit(solution)/shard_map/while/body/eval_jaxpr/all_to_all | solution.py:79
  281.6 11.1 %all-to-all-done = bf16[16,2,1,128,32]{3,4,1,2,0:T(8,128)(2,1)S(1)} async-done(((bf16[16,2,1,128,32]{3,4,1,2,0:T(8,128)(2,1)}), bf16[16,2,1,128,32]{3,4,1,2,0:T(8,128)(2,1)S(1)}, u32[]{:S(2)}, u32[]{:S(2)}) %all-to-all-start) | async-done | bytes 262176 | tf_op jit(solution)/shard_map/while/body/eval_jaxpr/all_to_all | solution.py:79
  307.7 5.4 all-to-all-start
  313.2 11.1 %all-to-all-done = bf16[16,2,1,128,32]{3,4,1,2,0:T(8,128)(2,1)S(1)} async-done(((bf16[16,2,1,128,32]{3,4,1,2,0:T(8,128)(2,1)}), bf16[16,2,1,128,32]{3,4,1,2,0:T(8,128)(2,1)S(1)}, u32[]{:S(2)}, u32[]{:S(2)}) %all-to-all-start) | async-done | bytes 262176 | tf_op jit(solution)/shard_map/while/body/eval_jaxpr/all_to_all | solution.py:79
  344.8 11.1 %all-to-all-done = bf16[16,2,1,128,32]{3,4,1,2,0:T(8,128)(2,1)S(1)} async-done(((bf16[16,2,1,128,32]{3,4,1,2,0:T(8,128)(2,1)}), bf16[16,2,1,128,32]{3,4,1,2,0:T(8,128)(2,1)S(1)}, u32[]{:S(2)}, u32[]{:S(2)}) %all-to-all-start) | async-done | bytes 262176 | tf_op jit(solution)/shard_map/while/body/eval_jaxpr/all_to_all | solution.py:79
  370.9 5.4 all-to-all-start
  376.4 11.1 %all-to-all-done = bf16[16,2,1,128,32]{3,4,1,2,0:T(8,128)(2,1)S(1)} async-done(((bf16[16,2,1,128,32]{3,4,1,2,0:T(8,128)(2,1)}), bf16[16,2,1,128,32]{3,4,1,2,0:T(8,128)(2,1)S(1)}, u32[]{:S(2)}, u32[]{:S(2)}) %all-to-all-start) | async-done | bytes 262176 | tf_op jit(solution)/shard_map/while/body/eval_jaxpr/all_to_all | solution.py:79
  408.1 11.1 %all-to-all-done = bf16[16,2,1,128,32]{3,4,1,2,0:T(8,128)(2,1)S(1)} async-done(((bf16[16,2,1,128,32]{3,4,1,2,0:T(8,128)(2,1)}), bf16[16,2,1,128,32]{3,4,1,2,0:T(8,128)(2,1)S(1)}, u32[]{:S(2)}, u32[]{:S(2)}) %all-to-all-start) | async-done | bytes 262176 | tf_op jit(solution)/shard_map/while/body/eval_jaxpr/all_to_all | solution.py:79
  439.7 11.1 %all-to-all-done = bf16[16,2,1,128,32]{3,4,1,2,0:T(8,128)(2,1)S(1)} async-done(((bf16[16,2,1,128,32]{3,4,1,2,0:T(8,128)(2,1)}), bf16[16,2,1,128,32]{3,4,1,2,0:T(8,128)(2,1)S(1)}, u32[]{:S(2)}, u32[]{:S(2)}) %all-to-all-start) | async-done | bytes 262176 | tf_op jit(solution)/shard_map/while/body/eval_jaxpr/all_to_all | solution.py:79
  471.3 11.1 %all-to-all-done = bf16[16,2,1,128,32]{3,4,1,2,0:T(8,128)(2,1)S(1)} async-done(((bf16[16,2,1,128,32]{3,4,1,2,0:T(8,128)(2,1)}), bf16[16,2,1,128,32]{3,4,1,2,0:T(8,128)(2,1)S(1)}, u32[]{:S(2)}, u32[]{:S(2)}) %all-to-all-start) | async-done | bytes 262176 | tf_op jit(solution)/shard_map/while/body/eval_jaxpr/all_to_all | solution.py:79
  502.9 11.1 %all-to-all-done = bf16[16,2,1,128,32]{3,4,1,2,0:T(8,128)(2,1)S(1)} async-done(((bf16[16,2,1,128,32]{3,4,1,2,0:T(8,128)(2,1)}), bf16[16,2,1,128,32]{3,4,1,2,0:T(8,128)(2,1)S(1)}, u32[]{:S(2)}, u32[]{:S(2)}) %all-to-all-start) | async-done | bytes 262176 | tf_op jit(solution)/shard_map/while/body/eval_jaxpr/all_to_all | solution.py:79
  515.2 10.2 %all-to-all-start.2 = ((bf16[32,2,128,32]{2,3,1,0:T(8,128)(2,1)}), bf16[32,2,128,32]{2,3,1,0:T(8,128)(2,1)S(1)}, u32[]{:S(2)}, u32[]{:S(2)}) async-start(bf16[32,2,128,32]{2,3,1,0:T(8,128)(2,1)} %bitcast.4), calls=%async_computation.2 | async-start | bytes 1048576 | tf_op jit(solution)/shard_map/all_to_all | solution.py:91
  525.4 8.5 %sine_convert_fusion = (bf16[1024,512]{1,0:T(8,128)(2,1)S(1)}, bf16[1024,512]{1,0:T(8,128)(2,1)S(1)}) fusion(), kind=kLoop, calls=%fused_computation.60 | loop fusion | flops 8388608 | bytes 2097152 | tf_op jit(solution)/shard_map/convert.1
  535.9 8.0 %all-to-all-done.2 = bf16[32,2,128,32]{2,3,1,0:T(8,128)(2,1)S(1)} async-done(((bf16[32,2,128,32]{2,3,1,0:T(8,128)(2,1)}), bf16[32,2,128,32]{2,3,1,0:T(8,128)(2,1)S(1)}, u32[]{:S(2)}, u32[]{:S(2)}) %all-to-all-start.2) | async-done | bytes 524320 | tf_op jit(solution)/shard_map/all_to_all | solution.py:91
  548.0 69.0 %psum.7 = f32[2,512]{1,0:T(2,128)S(1)} all-reduce(f32[2,512]{1,0:T(2,128)S(1)} %bitcast_reduce_fusion), channel_id=1, replica_groups=mesh['grp'=16,'ang'=32] {'ang'}, use_global_device_ids=true, to_apply=%region_4.5 | all-reduce | flops 1024 | bytes 8192 | tf_op jit(solution)/shard_map/psum | solution.py:103
  (447 shorter events, 311.1 us)
Async XLA Ops:
  5.2 18.0 %all-to-all-start.1 = ((s32[16,2,1]{1,2,0:T(1,128)}), s32[16,2,1]{1,2,0:T(1,128)S(1)}, u32[]{:S(2)}, u32[]{:S(2)}) async-start(s32[16,2,1]{1,2,0:T(1,128)} %copy.44), calls=%async_computation.1 | async-start | bytes 16384 | tf_op jit(solution)/shard_map/while/body/eval_jaxpr/all_to_all | solution.py:80
  23.2 16.6 %all-to-all-start = ((bf16[16,2,1,128,32]{3,4,1,2,0:T(8,128)(2,1)}), bf16[16,2,1,128,32]{3,4,1,2,0:T(8,128)(2,1)S(1)}, u32[]{:S(2)}, u32[]{:S(2)}) async-start(bf16[16,2,1,128,32]{3,4,1,2,0:T(8,128)(2,1)} %copy.43), calls=%async_computation | async-start | bytes 524288 | tf_op jit(solution)/shard_map/while/body/eval_jaxpr/all_to_all | solution.py:79
  54.8 16.6 %all-to-all-start = ((bf16[16,2,1,128,32]{3,4,1,2,0:T(8,128)(2,1)}), bf16[16,2,1,128,32]{3,4,1,2,0:T(8,128)(2,1)S(1)}, u32[]{:S(2)}, u32[]{:S(2)}) async-start(bf16[16,2,1,128,32]{3,4,1,2,0:T(8,128)(2,1)} %copy.43), calls=%async_computation | async-start | bytes 524288 | tf_op jit(solution)/shard_map/while/body/eval_jaxpr/all_to_all | solution.py:79
  75.4 11.0 %all-to-all-start.1 = ((s32[16,2,1]{1,2,0:T(1,128)}), s32[16,2,1]{1,2,0:T(1,128)S(1)}, u32[]{:S(2)}, u32[]{:S(2)}) async-start(s32[16,2,1]{1,2,0:T(1,128)} %copy.44), calls=%async_computation.1 | async-start | bytes 16384 | tf_op jit(solution)/shard_map/while/body/eval_jaxpr/all_to_all | solution.py:80
  86.4 16.6 %all-to-all-start = ((bf16[16,2,1,128,32]{3,4,1,2,0:T(8,128)(2,1)}), bf16[16,2,1,128,32]{3,4,1,2,0:T(8,128)(2,1)S(1)}, u32[]{:S(2)}, u32[]{:S(2)}) async-start(bf16[16,2,1,128,32]{3,4,1,2,0:T(8,128)(2,1)} %copy.43), calls=%async_computation | async-start | bytes 524288 | tf_op jit(solution)/shard_map/while/body/eval_jaxpr/all_to_all | solution.py:79
  118.0 16.6 %all-to-all-start = ((bf16[16,2,1,128,32]{3,4,1,2,0:T(8,128)(2,1)}), bf16[16,2,1,128,32]{3,4,1,2,0:T(8,128)(2,1)S(1)}, u32[]{:S(2)}, u32[]{:S(2)}) async-start(bf16[16,2,1,128,32]{3,4,1,2,0:T(8,128)(2,1)} %copy.43), calls=%async_computation | async-start | bytes 524288 | tf_op jit(solution)/shard_map/while/body/eval_jaxpr/all_to_all | solution.py:79
  138.6 11.0 %all-to-all-start.1 = ((s32[16,2,1]{1,2,0:T(1,128)}), s32[16,2,1]{1,2,0:T(1,128)S(1)}, u32[]{:S(2)}, u32[]{:S(2)}) async-start(s32[16,2,1]{1,2,0:T(1,128)} %copy.44), calls=%async_computation.1 | async-start | bytes 16384 | tf_op jit(solution)/shard_map/while/body/eval_jaxpr/all_to_all | solution.py:80
  149.6 16.6 %all-to-all-start = ((bf16[16,2,1,128,32]{3,4,1,2,0:T(8,128)(2,1)}), bf16[16,2,1,128,32]{3,4,1,2,0:T(8,128)(2,1)S(1)}, u32[]{:S(2)}, u32[]{:S(2)}) async-start(bf16[16,2,1,128,32]{3,4,1,2,0:T(8,128)(2,1)} %copy.43), calls=%async_computation | async-start | bytes 524288 | tf_op jit(solution)/shard_map/while/body/eval_jaxpr/all_to_all | solution.py:79
  170.3 11.0 %all-to-all-start.1 = ((s32[16,2,1]{1,2,0:T(1,128)}), s32[16,2,1]{1,2,0:T(1,128)S(1)}, u32[]{:S(2)}, u32[]{:S(2)}) async-start(s32[16,2,1]{1,2,0:T(1,128)} %copy.44), calls=%async_computation.1 | async-start | bytes 16384 | tf_op jit(solution)/shard_map/while/body/eval_jaxpr/all_to_all | solution.py:80
  181.2 16.6 %all-to-all-start = ((bf16[16,2,1,128,32]{3,4,1,2,0:T(8,128)(2,1)}), bf16[16,2,1,128,32]{3,4,1,2,0:T(8,128)(2,1)S(1)}, u32[]{:S(2)}, u32[]{:S(2)}) async-start(bf16[16,2,1,128,32]{3,4,1,2,0:T(8,128)(2,1)} %copy.43), calls=%async_computation | async-start | bytes 524288 | tf_op jit(solution)/shard_map/while/body/eval_jaxpr/all_to_all | solution.py:79
  212.9 16.6 %all-to-all-start = ((bf16[16,2,1,128,32]{3,4,1,2,0:T(8,128)(2,1)}), bf16[16,2,1,128,32]{3,4,1,2,0:T(8,128)(2,1)S(1)}, u32[]{:S(2)}, u32[]{:S(2)}) async-start(bf16[16,2,1,128,32]{3,4,1,2,0:T(8,128)(2,1)} %copy.43), calls=%async_computation | async-start | bytes 524288 | tf_op jit(solution)/shard_map/while/body/eval_jaxpr/all_to_all | solution.py:79
  244.5 16.6 %all-to-all-start = ((bf16[16,2,1,128,32]{3,4,1,2,0:T(8,128)(2,1)}), bf16[16,2,1,128,32]{3,4,1,2,0:T(8,128)(2,1)S(1)}, u32[]{:S(2)}, u32[]{:S(2)}) async-start(bf16[16,2,1,128,32]{3,4,1,2,0:T(8,128)(2,1)} %copy.43), calls=%async_computation | async-start | bytes 524288 | tf_op jit(solution)/shard_map/while/body/eval_jaxpr/all_to_all | solution.py:79
  265.1 11.0 %all-to-all-start.1 = ((s32[16,2,1]{1,2,0:T(1,128)}), s32[16,2,1]{1,2,0:T(1,128)S(1)}, u32[]{:S(2)}, u32[]{:S(2)}) async-start(s32[16,2,1]{1,2,0:T(1,128)} %copy.44), calls=%async_computation.1 | async-start | bytes 16384 | tf_op jit(solution)/shard_map/while/body/eval_jaxpr/all_to_all | solution.py:80
  276.1 16.6 %all-to-all-start = ((bf16[16,2,1,128,32]{3,4,1,2,0:T(8,128)(2,1)}), bf16[16,2,1,128,32]{3,4,1,2,0:T(8,128)(2,1)S(1)}, u32[]{:S(2)}, u32[]{:S(2)}) async-start(bf16[16,2,1,128,32]{3,4,1,2,0:T(8,128)(2,1)} %copy.43), calls=%async_computation | async-start | bytes 524288 | tf_op jit(solution)/shard_map/while/body/eval_jaxpr/all_to_all | solution.py:79
  307.7 16.6 %all-to-all-start = ((bf16[16,2,1,128,32]{3,4,1,2,0:T(8,128)(2,1)}), bf16[16,2,1,128,32]{3,4,1,2,0:T(8,128)(2,1)S(1)}, u32[]{:S(2)}, u32[]{:S(2)}) async-start(bf16[16,2,1,128,32]{3,4,1,2,0:T(8,128)(2,1)} %copy.43), calls=%async_computation | async-start | bytes 524288 | tf_op jit(solution)/shard_map/while/body/eval_jaxpr/all_to_all | solution.py:79
  339.3 16.6 %all-to-all-start = ((bf16[16,2,1,128,32]{3,4,1,2,0:T(8,128)(2,1)}), bf16[16,2,1,128,32]{3,4,1,2,0:T(8,128)(2,1)S(1)}, u32[]{:S(2)}, u32[]{:S(2)}) async-start(bf16[16,2,1,128,32]{3,4,1,2,0:T(8,128)(2,1)} %copy.43), calls=%async_computation | async-start | bytes 524288 | tf_op jit(solution)/shard_map/while/body/eval_jaxpr/all_to_all | solution.py:79
  359.9 11.0 %all-to-all-start.1 = ((s32[16,2,1]{1,2,0:T(1,128)}), s32[16,2,1]{1,2,0:T(1,128)S(1)}, u32[]{:S(2)}, u32[]{:S(2)}) async-start(s32[16,2,1]{1,2,0:T(1,128)} %copy.44), calls=%async_computation.1 | async-start | bytes 16384 | tf_op jit(solution)/shard_map/while/body/eval_jaxpr/all_to_all | solution.py:80
  370.9 16.6 %all-to-all-start = ((bf16[16,2,1,128,32]{3,4,1,2,0:T(8,128)(2,1)}), bf16[16,2,1,128,32]{3,4,1,2,0:T(8,128)(2,1)S(1)}, u32[]{:S(2)}, u32[]{:S(2)}) async-start(bf16[16,2,1,128,32]{3,4,1,2,0:T(8,128)(2,1)} %copy.43), calls=%async_computation | async-start | bytes 524288 | tf_op jit(solution)/shard_map/while/body/eval_jaxpr/all_to_all | solution.py:79
  402.5 16.6 %all-to-all-start = ((bf16[16,2,1,128,32]{3,4,1,2,0:T(8,128)(2,1)}), bf16[16,2,1,128,32]{3,4,1,2,0:T(8,128)(2,1)S(1)}, u32[]{:S(2)}, u32[]{:S(2)}) async-start(bf16[16,2,1,128,32]{3,4,1,2,0:T(8,128)(2,1)} %copy.43), calls=%async_computation | async-start | bytes 524288 | tf_op jit(solution)/shard_map/while/body/eval_jaxpr/all_to_all | solution.py:79
  434.2 16.6 %all-to-all-start = ((bf16[16,2,1,128,32]{3,4,1,2,0:T(8,128)(2,1)}), bf16[16,2,1,128,32]{3,4,1,2,0:T(8,128)(2,1)S(1)}, u32[]{:S(2)}, u32[]{:S(2)}) async-start(bf16[16,2,1,128,32]{3,4,1,2,0:T(8,128)(2,1)} %copy.43), calls=%async_computation | async-start | bytes 524288 | tf_op jit(solution)/shard_map/while/body/eval_jaxpr/all_to_all | solution.py:79
  454.8 11.0 %all-to-all-start.1 = ((s32[16,2,1]{1,2,0:T(1,128)}), s32[16,2,1]{1,2,0:T(1,128)S(1)}, u32[]{:S(2)}, u32[]{:S(2)}) async-start(s32[16,2,1]{1,2,0:T(1,128)} %copy.44), calls=%async_computation.1 | async-start | bytes 16384 | tf_op jit(solution)/shard_map/while/body/eval_jaxpr/all_to_all | solution.py:80
  465.8 16.6 %all-to-all-start = ((bf16[16,2,1,128,32]{3,4,1,2,0:T(8,128)(2,1)}), bf16[16,2,1,128,32]{3,4,1,2,0:T(8,128)(2,1)S(1)}, u32[]{:S(2)}, u32[]{:S(2)}) async-start(bf16[16,2,1,128,32]{3,4,1,2,0:T(8,128)(2,1)} %copy.43), calls=%async_computation | async-start | bytes 524288 | tf_op jit(solution)/shard_map/while/body/eval_jaxpr/all_to_all | solution.py:79
  497.4 16.6 %all-to-all-start = ((bf16[16,2,1,128,32]{3,4,1,2,0:T(8,128)(2,1)}), bf16[16,2,1,128,32]{3,4,1,2,0:T(8,128)(2,1)S(1)}, u32[]{:S(2)}, u32[]{:S(2)}) async-start(bf16[16,2,1,128,32]{3,4,1,2,0:T(8,128)(2,1)} %copy.43), calls=%async_computation | async-start | bytes 524288 | tf_op jit(solution)/shard_map/while/body/eval_jaxpr/all_to_all | solution.py:79
  515.2 28.7 %all-to-all-start.2 = ((bf16[32,2,128,32]{2,3,1,0:T(8,128)(2,1)}), bf16[32,2,128,32]{2,3,1,0:T(8,128)(2,1)S(1)}, u32[]{:S(2)}, u32[]{:S(2)}) async-start(bf16[32,2,128,32]{2,3,1,0:T(8,128)(2,1)} %bitcast.4), calls=%async_computation.2 | async-start | bytes 1048576 | tf_op jit(solution)/shard_map/all_to_all | solution.py:91
  (12 other events, 634.4 us)
where the time goes:
time: 622 us; the launch traced here: 618 us
  waiting for transfers between devices  214 us (34%)
  starting transfers between devices  159 us (26%)
  local copies, waits for them, and re-layouts  77.3 us (12%)
  blocking collectives  69 us (11%)
  matrix products  57.5 us (9%)
  other arithmetic  28.8 us (5%)
  loops' own time  11.6 us (2%)
    all_to_all x16, waiting for transfers between devices, one_block(): lax.all_to_all(sending, 'grp', split_axis=0, concat_axis=0, tiled=True)  177 us
    all_to_all x16, starting transfers between devices, one_block(): lax.all_to_all(sending, 'grp', split_axis=0, concat_axis=0, tiled=True)  86.5 us
    psum x1, blocking collectives, body(): total_grad = lax.psum(partial_grad, 'ang')  69 us
    all_to_all x16, starting transfers between devices, one_block(): lax.all_to_all(send_ids, 'grp', split_axis=0, concat_axis=0, tiled=True)  62.1 us
    dot_general x16, matrix products, one_block(): jnp.einsum('akrz,acz->akrc', weights, block_view, preferred_element_type=...  45.7 us
    all_to_all x16, waiting for transfers between devices, one_block(): lax.all_to_all(send_ids, 'grp', split_axis=0, concat_axis=0, tiled=True)  28.6 us
    gather x48, local copies, waits for them, and re-layouts, one_block(): jnp.take_along_axis(tile_ids, gather_idx, axis=2)  14.1 us
  transfers between devices with their start and end apart: 33, of which 33 were waited for; matrix products, arithmetic and copies ran while one was open for 17% of the time, Pallas kernels for 0%

commit v1 on v0

v1 whole, which is shorter than its diff:
```python
import functools
import math

import jax
import jax.numpy as jnp
import numpy as np
from jax import lax
from jax.experimental import pallas as pl
from jax.experimental.pallas import tpu as pltpu
from jax.sharding import PartitionSpec as P

TR = 128
KF = 8
SZ = 1024
TPO = 2
WINDOW = 512
PIECE = 16
GROUPS = 2
PER_SLAB = KF // 2


def dft_basis(columns):
    column_idx = np.arange(columns, dtype=np.int64)[:, None]
    freq_idx = np.arange(columns // 2, dtype=np.int64)[None, :]
    phases = ((column_idx * freq_idx) % columns).astype(np.float64) * (2.0 * math.pi / columns)
    return np.concatenate([np.cos(phases), np.sin(phases)], axis=1).astype(jnp.bfloat16)


def contrib_kernel(place, start, slope, own, other, out):
    angles = own.shape[0]
    out[...] = jnp.zeros_like(out)
    row = lax.broadcasted_iota(jnp.int32, (PIECE, TR), 1).astype(jnp.float32)
    depth = lax.broadcasted_iota(jnp.int32, (PIECE, TR), 0).astype(jnp.float32)

    def one_angle(a, carry):
        for s, views in enumerate((own, other)):
            step = row * slope[s, a] - depth
            for j in range(PER_SLAB):
                where = place[s, a * PER_SLAB + j]
                slot = where // 8
                z0 = pl.multiple_of((where % 8) * 128, 128)
                ahead = step + start[s, a * PER_SLAB + j]
                pieces = []
                for i in range(WINDOW // PIECE):
                    away = jnp.abs(ahead - float(i * PIECE))
                    pieces.append(jnp.maximum(1.0 - away, 0.0).astype(jnp.bfloat16))
                weights = jnp.concatenate(pieces, axis=0)
                tile = jnp.dot(
                    views[a, :, pl.ds(z0, WINDOW)], weights, preferred_element_type=jnp.float32
                )
                old = out[slot // 2, a, slot % 2].astype(jnp.float32)
                out[slot // 2, a, slot % 2] = (old + tile).astype(jnp.bfloat16)
        return carry

    lax.fori_loop(0, angles, one_angle, 0)


def contributions(place, start, slope, own, other, chips):
    angles, narrow, _ = own.shape
    smem = pl.BlockSpec(memory_space=pltpu.SMEM)
    vmem = pl.BlockSpec(memory_space=pltpu.VMEM)
    return pl.pallas_call(
        contrib_kernel,
        out_shape=jax.ShapeDtypeStruct((chips, angles, TPO, narrow, TR), jnp.bfloat16),
        in_specs=[smem, smem, smem, vmem, vmem],
        out_specs=vmem,
        compiler_params=pltpu.CompilerParams(vmem_limit_bytes=32 * 1024 * 1024),
        cost_estimate=pl.CostEstimate(
            flops=2 * angles * 2 * PER_SLAB * narrow * WINDOW * TR * 8,
            bytes_accessed=angles * narrow * SZ * 4 + chips * angles * TPO * narrow * TR * 2,
            transcendentals=0,
        ),
    )(place, start, slope, own, other)


def add(*terms):
    total = terms[0].astype(jnp.float32)
    for term in terms[1:]:
        total = total + term.astype(jnp.float32)
    return total.astype(jnp.bfloat16)


def body(slab_views, footprint, row_shift, stretch, projections):
    n_grp = lax.axis_size("grp")
    n_ang = lax.axis_size("ang")
    chips = n_grp // 2
    owner = lax.axis_index("grp")
    chip, core = owner // 2, owner % 2
    views = slab_views[0]
    angles = views.shape[0]
    part = angles // GROUPS

    swap = [(i, i ^ 1) for i in range(n_grp)]
    up = [(i, (i + 2) % n_grp) for i in range(n_grp)]
    down = [(i, (i - 2) % n_grp) for i in range(n_grp)]

    counts = jnp.sum((footprint[0] >= 0).astype(jnp.int32), axis=-1)
    mine = jnp.stack(
        [
            counts.astype(jnp.float32),
            footprint[0, :, 0].astype(jnp.float32),
            row_shift[0],
            stretch[0],
        ]
    )
    both = jnp.stack([mine, lax.ppermute(mine, "grp", swap)])
    count, first = both[:, 0].astype(jnp.int32), both[:, 1].astype(jnp.int32)
    magnify = (TR * count).astype(jnp.float32) * both[:, 3] / SZ
    slope = 1.0 / magnify
    entry = ((core - first) & 1)[:, :, None] + 2 * jnp.arange(PER_SLAB, dtype=jnp.int32)
    tile = first[:, :, None] + entry
    begin = ((TR * entry).astype(jnp.float32) - both[:, 2, :, None]) * slope[:, :, None]
    block = jnp.clip(jnp.floor((begin - 1.0) / 128.0).astype(jnp.int32), 0, (SZ - WINDOW) // 128)
    start = jnp.where(entry < count[:, :, None], begin - 128.0 * block.astype(jnp.float32), -1e6)
    slot = ((((tile % n_grp) // 2) - chip) % chips) * TPO + (tile // n_grp) % TPO
    place = slot * 8 + block

    parts = []
    for g in range(GROUPS):
        own = views[g * part : (g + 1) * part]
        other = lax.ppermute(own, "grp", swap)
        at = slice(g * part, (g + 1) * part)
        parts.append(
            contributions(
                place[:, at].reshape(2, -1), start[:, at].reshape(2, -1), slope[:, at], own, other, chips
            )
        )

    def ring(held, perm, order):
        moving = lax.ppermute(held[order[0]], "grp", perm)
        for at in order[1:]:
            moving = lax.ppermute(add(moving, held[at]), "grp", perm)
        return moving

    a_up = ring(parts[0], up, (4, 3, 2, 1))
    a_down = ring(parts[0], down, (5, 6, 7))
    b_up = ring(parts[1], up, (3, 2, 1))
    b_down = ring(parts[1], down, (4, 5, 6, 7))
    summed = jnp.concatenate(
        [add(parts[0][0], a_up, a_down), add(parts[1][0], b_up, b_down)], axis=0
    )

    got = lax.all_to_all(summed, "ang", split_axis=0, concat_axis=0, tiled=True)
    columns = got.shape[0] * got.shape[2]
    rows = jnp.transpose(got, (1, 3, 0, 2)).reshape(TPO * TR, columns)
    basis = jnp.asarray(dft_basis(columns))
    n_freq = columns // 2
    spec_proj = jnp.dot(projections.reshape(-1, columns), basis, preferred_element_type=jnp.float32)
    spec_grad = jnp.dot(rows, basis, preferred_element_type=jnp.float32)
    product = (
        spec_grad[:, :n_freq] * spec_proj[:, :n_freq]
        + spec_grad[:, n_freq:] * spec_proj[:, n_freq:]
    )
    share = jnp.sum(product.reshape(TPO, TR, n_freq), axis=1).reshape(-1, 128)
    shares = lax.all_to_all(
        jnp.broadcast_to(share[None], (n_ang,) + share.shape), "ang", split_axis=0, concat_axis=0, tiled=True
    )
    filter_grad = (jnp.sum(shares, axis=0) * (1.0 / (columns * angles))).reshape(TPO, 1, n_freq)
    return rows.reshape(1, TPO, TR, columns), filter_grad


def solution(mesh):
    return jax.shard_map(
        body,
        mesh=mesh,
        in_specs=(
            P("grp", None, "ang", None),
            P("grp", None, None),
            P("grp", None),
            P("grp", None),
            P("ang", None, "grp", None),
        ),
        out_specs=(P("ang", None, "grp", None), P(None, "grp", None)),
        check_vma=False,
    )
```

time: 622 us -> 137 us (0.22)
  waiting for transfers between devices: 214 us -> 27.8 us
  starting transfers between devices: 159 us -> 75.2 us
  local copies, waits for them, and re-layouts: 77.3 us -> 4.98 us
  blocking collectives: 69 us -> 0 us
  matrix products: 57.5 us -> 2.46 us
  other arithmetic: 28.8 us -> 5.28 us
  Pallas kernels: 0 us -> 19.5 us
  loops' own time: 11.6 us -> 0 us
    all_to_all x33 -> x2, waiting for transfers between devices: 214 us -> 20.8 us  [the longest x1 12.2 us: body(): got = lax.all_to_all(summed, 'ang', split_axis=0, concat_axis=0, tiled=True)]
    all_to_all x33 -> x2, starting transfers between devices: 159 us -> 14.8 us  [the longest x1 10.2 us: body(): got = lax.all_to_all(summed, 'ang', split_axis=0, concat_axis=0, tiled=True)]
    psum x1 -> x0, blocking collectives: 69 us -> none  [body(): total_grad = lax.psum(partial_grad, 'ang')]
    ppermute x0 -> x17, starting transfers between devices: none -> 60.3 us  [the longest x10 35.4 us: ring(): moving = lax.ppermute(add(moving, held[at]), 'grp', perm)]
    dot_general x49 -> x1, matrix products: 56.8 us -> 0.74 us  [body(): spec_grad = jnp.dot(rows, basis, preferred_element_type=jnp.float32)]
    dynamic_slice x48 -> x0, local copies, waits for them, and re-layouts: 33.2 us -> none  [the longest x16 12.2 us: one_block(): block_lists = lax.dynamic_slice_in_dim(lists, first_angle, angle_block, 0)]
    pallas_call x0 -> x2, Pallas kernels: none -> 19.5 us  [contributions(): pl.pallas_call(contrib_kernel, out_shape=jax.ShapeDtypeStruct((chips, ang...]
    gather x48 -> x0, local copies, waits for them, and re-layouts: 14.1 us -> none  [one_block(): jnp.take_along_axis(tile_ids, gather_idx, axis=2)]
  transfers between devices with their start and end apart: 33 -> 19, of which waited for: 33 -> 5; matrix products, arithmetic and copies ran while one was open for 17% -> 5% of each run, Pallas kernels for 0% -> 14%
where the time goes in v1:
time: 137 us; the launch traced here: 136 us
  starting transfers between devices  75.2 us (55%)
  waiting for transfers between devices  27.8 us (20%)
  Pallas kernels  19.5 us (14%)
  other arithmetic  5.28 us (4%)
  local copies, waits for them, and re-layouts  4.98 us (4%)
  matrix products  2.46 us (2%)
    ppermute x10, starting transfers between devices, ring(): moving = lax.ppermute(add(moving, held[at]), 'grp', perm)  35.4 us
    pallas_call x2, Pallas kernels, contributions(): pl.pallas_call(contrib_kernel, out_shape=jax.ShapeDtypeStruct((chips, ang...  19.5 us
    ppermute x4, starting transfers between devices, ring(): moving = lax.ppermute(held[order[0]], 'grp', perm)  18.7 us
    all_to_all x1, waiting for transfers between devices, body(): got = lax.all_to_all(summed, 'ang', split_axis=0, concat_axis=0, tiled=True)  12.2 us
    all_to_all x1, starting transfers between devices, body(): got = lax.all_to_all(summed, 'ang', split_axis=0, concat_axis=0, tiled=True)  10.2 us
    all_to_all x1, waiting for transfers between devices, body(): lax.all_to_all(jnp.broadcast_to(share[None], (n_ang,) + share.shape), 'an...  8.61 us
    ppermute x10, waiting for transfers between devices, ring(): moving = lax.ppermute(add(moving, held[at]), 'grp', perm)  6.97 us
    all_to_all x1, starting transfers between devices, body(): lax.all_to_all(jnp.broadcast_to(share[None], (n_ang,) + share.shape), 'an...  4.66 us
  transfers between devices with their start and end apart: 19, of which 5 were waited for; matrix products, arithmetic and copies ran while one was open for 5% of the time, Pallas kernels for 14%

profile of v1, /device:TPU:8, one launch (start us, length us, event | category | flops | bytes accessed | tf_op | source)
XLA Modules:
  0.0 136.4 jit_solution(2193964783460971993)
XLA Ops:
  6.5 2.4 %collective-permute-start.1 = (bf16[16,32,1024]{2,1,0:T(8,128)(2,1)S(1)}, bf16[16,32,1024]{2,1,0:T(8,128)(2,1)}, u32[]{:S(2)}, u32[]{:S(2)}) collective-permute-start(bf16[16,32,1024]{2,1,0:T(8,128)(2,1)S(1)} %get-tuple-element.12.own), channel_id=1, source_target_pairs={{0,32},{32,0},{64,96},{96,64},{128,160},{160,128},{192,224},{224,1... | collective-permute-start | bytes 3145736 | tf_op jit(solution)/shard_map/ppermute | solution.py:121
  8.9 1.9 %collective-permute-start.9 = (bf16[16,32,1024]{2,1,0:T(8,128)(2,1)S(1)}, bf16[16,32,1024]{2,1,0:T(8,128)(2,1)}, u32[]{:S(2)}, u32[]{:S(2)}) collective-permute-start(bf16[16,32,1024]{2,1,0:T(8,128)(2,1)S(1)} %get-tuple-element.13.own), channel_id=1, source_target_pairs={{0,32},{32,0},{64,96},{96,64},{128,160},{160,128},{192,224},{224,1... | collective-permute-start | bytes 3145736 | tf_op jit(solution)/shard_map/ppermute | solution.py:121
  11.7 9.8 %shard_map.77 = bf16[8,16,2,32,128]{4,3,2,1,0:T(8,128)(2,1)S(1)} custom-call(s32[2,64]{1,0:T(2,128)S(1)} %reshape.121.place, f32[2,64]{1,0:T(2,128)S(1)} %reshape.122.start, f32[2,16]{1,0:T(2,128)S(1)} %get-tuple-element.30.slope, bf16[16,32,1024]{2,1,0:T(8,128)(2,1)S(1)} %get-tuple-element.12.own, bf16[16,32,1024]{2,1,0:T(8,128)(2,1)} %collective-permute-done.1.other), custom_call_target="tpu_custom_call" | custom-call | flops 4294967296 | bytes 4194304 | tf_op jit(solution)/shard_map/pallas_call | solution.py:62
  21.5 4.3 %collective-permute-start.2 = (bf16[16,2,32,128]{3,2,1,0:T(8,128)(2,1)S(1)}, bf16[16,2,32,128]{3,2,1,0:T(8,128)(2,1)S(1)}, u32[]{:S(2)}, u32[]{:S(2)}) collective-permute-start(bf16[16,2,32,128]{3,2,1,0:T(8,128)(2,1)S(1)} %get-tuple-element.10), channel_id=1, source_target_pairs={{0,64},{32,96},{64,128},{96,160},{128,192},{160,224},{192,256},{22... | collective-permute-start | bytes 786440 | tf_op jit(solution)/shard_map/ppermute | solution.py:130
  25.8 9.8 %shard_map.78 = bf16[8,16,2,32,128]{4,3,2,1,0:T(8,128)(2,1)S(1)} custom-call(s32[2,64]{1,0:T(2,128)S(1)} %reshape.123.place, f32[2,64]{1,0:T(2,128)S(1)} %reshape.124.start, f32[2,16]{1,0:T(2,128)S(1)} %get-tuple-element.31.slope, bf16[16,32,1024]{2,1,0:T(8,128)(2,1)S(1)} %get-tuple-element.13.own, bf16[16,32,1024]{2,1,0:T(8,128)(2,1)} %collective-permute-done.9.other), custom_call_target="tpu_custom_call" | custom-call | flops 4294967296 | bytes 4194304 | tf_op jit(solution)/shard_map/pallas_call | solution.py:62
  35.6 8.6 %collective-permute-start.13 = (bf16[16,2,32,128]{3,2,1,0:T(8,128)(2,1)S(1)}, bf16[16,2,32,128]{3,2,1,0:T(8,128)(2,1)S(1)}, u32[]{:S(2)}, u32[]{:S(2)}) collective-permute-start(bf16[16,2,32,128]{3,2,1,0:T(8,128)(2,1)S(1)} %get-tuple-element.19), channel_id=1, source_target_pairs={{0,448},{32,480},{64,0},{96,32},{128,64},{160,96},{192,128},{224,1... | collective-permute-start | bytes 786440 | tf_op jit(solution)/shard_map/ppermute | solution.py:130
  44.2 3.9 %collective-permute-start.6 = (bf16[16,2,32,128]{3,2,1,0:T(8,128)(2,1)S(1)}, bf16[16,2,32,128]{3,2,1,0:T(8,128)(2,1)S(1)}, u32[]{:S(2)}, u32[]{:S(2)}) collective-permute-start(bf16[16,2,32,128]{3,2,1,0:T(8,128)(2,1)S(1)} %get-tuple-element.11), channel_id=1, source_target_pairs={{0,448},{32,480},{64,0},{96,32},{128,64},{160,96},{192,128},{224,1... | collective-permute-start | bytes 786440 | tf_op jit(solution)/shard_map/ppermute | solution.py:130
  48.2 1.9 %collective-permute-start.3 = (bf16[16,2,32,128]{3,2,1,0:T(8,128)(2,1)S(1)}, bf16[16,2,32,128]{3,2,1,0:T(8,128)(2,1)S(1)}, u32[]{:S(2)}, u32[]{:S(2)}) collective-permute-start(bf16[16,2,32,128]{3,2,1,0:T(8,128)(2,1)S(1)} %fusion.15), channel_id=1, source_target_pairs={{0,64},{32,96},{64,128},{96,160},{128,192},{160,224},{192,256},{22... | collective-permute-start | bytes 786440 | tf_op jit(solution)/shard_map/ppermute | solution.py:132
  50.1 1.9 %collective-permute-start.10 = (bf16[16,2,32,128]{3,2,1,0:T(8,128)(2,1)S(1)}, bf16[16,2,32,128]{3,2,1,0:T(8,128)(2,1)S(1)}, u32[]{:S(2)}, u32[]{:S(2)}) collective-permute-start(bf16[16,2,32,128]{3,2,1,0:T(8,128)(2,1)S(1)} %get-tuple-element.18), channel_id=1, source_target_pairs={{0,64},{32,96},{64,128},{96,160},{128,192},{160,224},{192,256},{22... | collective-permute-start | bytes 786440 | tf_op jit(solution)/shard_map/ppermute | solution.py:130
  52.1 5.1 %collective-permute-start.14 = (bf16[16,2,32,128]{3,2,1,0:T(8,128)(2,1)S(1)}, bf16[16,2,32,128]{3,2,1,0:T(8,128)(2,1)S(1)}, u32[]{:S(2)}, u32[]{:S(2)}) collective-permute-start(bf16[16,2,32,128]{3,2,1,0:T(8,128)(2,1)S(1)} %fusion.6), channel_id=1, source_target_pairs={{0,448},{32,480},{64,0},{96,32},{128,64},{160,96},{192,128},{224,1... | collective-permute-start | bytes 786440 | tf_op jit(solution)/shard_map/ppermute | solution.py:132
  57.3 3.2 %collective-permute-done.3 = bf16[16,2,32,128]{3,2,1,0:T(8,128)(2,1)S(1)} collective-permute-done((bf16[16,2,32,128]{3,2,1,0:T(8,128)(2,1)S(1)}, bf16[16,2,32,128]{3,2,1,0:T(8,128)(2,1)S(1)}, u32[]{:S(2)}, u32[]{:S(2)}) %collective-permute-start.3) | collective-permute-done | bytes 262176 | tf_op jit(solution)/shard_map/ppermute | solution.py:132
  60.7 1.9 %collective-permute-start.4 = (bf16[16,2,32,128]{3,2,1,0:T(8,128)(2,1)S(1)}, bf16[16,2,32,128]{3,2,1,0:T(8,128)(2,1)S(1)}, u32[]{:S(2)}, u32[]{:S(2)}) collective-permute-start(bf16[16,2,32,128]{3,2,1,0:T(8,128)(2,1)S(1)} %get-tuple-element.8), channel_id=1, source_target_pairs={{0,64},{32,96},{64,128},{96,160},{128,192},{160,224},{192,256},{22... | collective-permute-start | bytes 786440 | tf_op jit(solution)/shard_map/ppermute | solution.py:132
  62.6 5.1 %collective-permute-start.7 = (bf16[16,2,32,128]{3,2,1,0:T(8,128)(2,1)S(1)}, bf16[16,2,32,128]{3,2,1,0:T(8,128)(2,1)S(1)}, u32[]{:S(2)}, u32[]{:S(2)}) collective-permute-start(bf16[16,2,32,128]{3,2,1,0:T(8,128)(2,1)S(1)} %get-tuple-element.9), channel_id=1, source_target_pairs={{0,448},{32,480},{64,0},{96,32},{128,64},{160,96},{192,128},{224,1... | collective-permute-start | bytes 786440 | tf_op jit(solution)/shard_map/ppermute | solution.py:132
  68.0 1.9 %collective-permute-start.11 = (bf16[16,2,32,128]{3,2,1,0:T(8,128)(2,1)S(1)}, bf16[16,2,32,128]{3,2,1,0:T(8,128)(2,1)S(1)}, u32[]{:S(2)}, u32[]{:S(2)}) collective-permute-start(bf16[16,2,32,128]{3,2,1,0:T(8,128)(2,1)S(1)} %get-tuple-element.16), channel_id=1, source_target_pairs={{0,64},{32,96},{64,128},{96,160},{128,192},{160,224},{192,256},{22... | collective-permute-start | bytes 786440 | tf_op jit(solution)/shard_map/ppermute | solution.py:132
  69.9 5.1 %collective-permute-start.15 = (bf16[16,2,32,128]{3,2,1,0:T(8,128)(2,1)S(1)}, bf16[16,2,32,128]{3,2,1,0:T(8,128)(2,1)S(1)}, u32[]{:S(2)}, u32[]{:S(2)}) collective-permute-start(bf16[16,2,32,128]{3,2,1,0:T(8,128)(2,1)S(1)} %get-tuple-element.17), channel_id=1, source_target_pairs={{0,448},{32,480},{64,0},{96,32},{128,64},{160,96},{192,128},{224,1... | collective-permute-start | bytes 786440 | tf_op jit(solution)/shard_map/ppermute | solution.py:132
  75.3 1.9 %collective-permute-start.5 = (bf16[16,2,32,128]{3,2,1,0:T(8,128)(2,1)S(1)}, bf16[16,2,32,128]{3,2,1,0:T(8,128)(2,1)S(1)}, u32[]{:S(2)}, u32[]{:S(2)}) collective-permute-start(bf16[16,2,32,128]{3,2,1,0:T(8,128)(2,1)S(1)} %get-tuple-element.6), channel_id=1, source_target_pairs={{0,64},{32,96},{64,128},{96,160},{128,192},{160,224},{192,256},{22... | collective-permute-start | bytes 786440 | tf_op jit(solution)/shard_map/ppermute | solution.py:132
  77.2 5.1 %collective-permute-start.8 = (bf16[16,2,32,128]{3,2,1,0:T(8,128)(2,1)S(1)}, bf16[16,2,32,128]{3,2,1,0:T(8,128)(2,1)S(1)}, u32[]{:S(2)}, u32[]{:S(2)}) collective-permute-start(bf16[16,2,32,128]{3,2,1,0:T(8,128)(2,1)S(1)} %get-tuple-element.7), channel_id=1, source_target_pairs={{0,448},{32,480},{64,0},{96,32},{128,64},{160,96},{192,128},{224,1... | collective-permute-start | bytes 786440 | tf_op jit(solution)/shard_map/ppermute | solution.py:132
  82.6 1.9 %collective-permute-start.12 = (bf16[16,2,32,128]{3,2,1,0:T(8,128)(2,1)S(1)}, bf16[16,2,32,128]{3,2,1,0:T(8,128)(2,1)S(1)}, u32[]{:S(2)}, u32[]{:S(2)}) collective-permute-start(bf16[16,2,32,128]{3,2,1,0:T(8,128)(2,1)S(1)} %get-tuple-element.14), channel_id=1, source_target_pairs={{0,64},{32,96},{64,128},{96,160},{128,192},{160,224},{192,256},{22... | collective-permute-start | bytes 786440 | tf_op jit(solution)/shard_map/ppermute | solution.py:132
  84.5 5.3 %collective-permute-start.16 = (bf16[16,2,32,128]{3,2,1,0:T(8,128)(2,1)S(1)}, bf16[16,2,32,128]{3,2,1,0:T(8,128)(2,1)S(1)}, u32[]{:S(2)}, u32[]{:S(2)}) collective-permute-start(bf16[16,2,32,128]{3,2,1,0:T(8,128)(2,1)S(1)} %get-tuple-element.15), channel_id=1, source_target_pairs={{0,448},{32,480},{64,0},{96,32},{128,64},{160,96},{192,128},{224,1... | collective-permute-start | bytes 786440 | tf_op jit(solution)/shard_map/ppermute | solution.py:132
  89.9 2.1 %collective-permute-done.12 = bf16[16,2,32,128]{3,2,1,0:T(8,128)(2,1)S(1)} collective-permute-done((bf16[16,2,32,128]{3,2,1,0:T(8,128)(2,1)S(1)}, bf16[16,2,32,128]{3,2,1,0:T(8,128)(2,1)S(1)}, u32[]{:S(2)}, u32[]{:S(2)}) %collective-permute-start.12) | collective-permute-done | bytes 262176 | tf_op jit(solution)/shard_map/ppermute | solution.py:132
  94.6 10.2 %all-to-all-start = ((bf16[32,2,32,128]{3,2,1,0:T(8,128)(2,1)}), bf16[32,2,32,128]{3,2,1,0:T(8,128)(2,1)S(1)}, u32[]{:S(2)}, u32[]{:S(2)}) async-start(bf16[32,2,32,128]{3,2,1,0:T(8,128)(2,1)} %pad_maximum_fusion), calls=%async_computation | async-start | bytes 1048576 | tf_op jit(solution)/shard_map/all_to_all | solution.py:143
  106.5 12.2 %all-to-all-done = bf16[32,2,32,128]{3,2,1,0:T(8,128)(2,1)S(1)} async-done(((bf16[32,2,32,128]{3,2,1,0:T(8,128)(2,1)}), bf16[32,2,32,128]{3,2,1,0:T(8,128)(2,1)S(1)}, u32[]{:S(2)}, u32[]{:S(2)}) %all-to-all-start) | async-done | bytes 524320 | tf_op jit(solution)/shard_map/all_to_all | solution.py:143
  121.4 4.7 %all-to-all-start.1 = ((f32[32,8,128]{2,1,0:T(8,128)}), f32[32,8,128]{2,1,0:T(8,128)S(1)}, u32[]{:S(2)}, u32[]{:S(2)}) async-start(f32[32,8,128]{2,1,0:T(8,128)} %broadcast_in_dim.18), calls=%async_computation.1 | async-start | bytes 262144 | tf_op jit(solution)/shard_map/all_to_all | solution.py:155
  127.1 8.6 %all-to-all-done.1 = f32[32,8,128]{2,1,0:T(8,128)S(1)} async-done(((f32[32,8,128]{2,1,0:T(8,128)}), f32[32,8,128]{2,1,0:T(8,128)S(1)}, u32[]{:S(2)}, u32[]{:S(2)}) %all-to-all-start.1) | async-done | bytes 131104 | tf_op jit(solution)/shard_map/all_to_all | solution.py:155
  (61 shorter events, 16.3 us)
Async XLA Ops:
  0.6 104.1 %copy-start = (bf16[1,2,128,1024]{3,2,1,0:T(8,128)(2,1)S(1)}, bf16[1,2,128,1024]{3,2,1,0:T(8,128)(2,1)}, u32[]{:S(2)}) copy-start(bf16[1,2,128,1024]{3,2,1,0:T(8,128)(2,1)} %param.10) | copy-start | bytes 1572868
  2.8 8.1 %collective-permute-start = (f32[4,32]{1,0:T(4,128)S(1)}, f32[4,32]{1,0:T(4,128)S(1)}, u32[]{:S(2)}, u32[]{:S(2)}) collective-permute-start(f32[4,32]{1,0:T(4,128)S(1)} %get-tuple-element.29), channel_id=1, source_target_pairs={{0,32},{32,0},{64,96},{96,64},{128,160},{160,128},{192,224},{224,1... | collective-permute-start | bytes 1544 | tf_op jit(solution)/shard_map/ppermute | solution.py:106
  6.5 5.2 %collective-permute-start.1 = (bf16[16,32,1024]{2,1,0:T(8,128)(2,1)S(1)}, bf16[16,32,1024]{2,1,0:T(8,128)(2,1)}, u32[]{:S(2)}, u32[]{:S(2)}) collective-permute-start(bf16[16,32,1024]{2,1,0:T(8,128)(2,1)S(1)} %get-tuple-element.12.own), channel_id=1, source_target_pairs={{0,32},{32,0},{64,96},{96,64},{128,160},{160,128},{192,224},{224,1... | collective-permute-start | bytes 3145736 | tf_op jit(solution)/shard_map/ppermute | solution.py:121
  8.9 16.9 %collective-permute-start.9 = (bf16[16,32,1024]{2,1,0:T(8,128)(2,1)S(1)}, bf16[16,32,1024]{2,1,0:T(8,128)(2,1)}, u32[]{:S(2)}, u32[]{:S(2)}) collective-permute-start(bf16[16,32,1024]{2,1,0:T(8,128)(2,1)S(1)} %get-tuple-element.13.own), channel_id=1, source_target_pairs={{0,32},{32,0},{64,96},{96,64},{128,160},{160,128},{192,224},{224,1... | collective-permute-start | bytes 3145736 | tf_op jit(solution)/shard_map/ppermute | solution.py:121
  21.5 26.6 %collective-permute-start.2 = (bf16[16,2,32,128]{3,2,1,0:T(8,128)(2,1)S(1)}, bf16[16,2,32,128]{3,2,1,0:T(8,128)(2,1)S(1)}, u32[]{:S(2)}, u32[]{:S(2)}) collective-permute-start(bf16[16,2,32,128]{3,2,1,0:T(8,128)(2,1)S(1)} %get-tuple-element.10), channel_id=1, source_target_pairs={{0,64},{32,96},{64,128},{96,160},{128,192},{160,224},{192,256},{22... | collective-permute-start | bytes 786440 | tf_op jit(solution)/shard_map/ppermute | solution.py:130
  35.6 16.5 %collective-permute-start.13 = (bf16[16,2,32,128]{3,2,1,0:T(8,128)(2,1)S(1)}, bf16[16,2,32,128]{3,2,1,0:T(8,128)(2,1)S(1)}, u32[]{:S(2)}, u32[]{:S(2)}) collective-permute-start(bf16[16,2,32,128]{3,2,1,0:T(8,128)(2,1)S(1)} %get-tuple-element.19), channel_id=1, source_target_pairs={{0,448},{32,480},{64,0},{96,32},{128,64},{160,96},{192,128},{224,1... | collective-permute-start | bytes 786440 | tf_op jit(solution)/shard_map/ppermute | solution.py:130
  44.2 13.1 %collective-permute-start.6 = (bf16[16,2,32,128]{3,2,1,0:T(8,128)(2,1)S(1)}, bf16[16,2,32,128]{3,2,1,0:T(8,128)(2,1)S(1)}, u32[]{:S(2)}, u32[]{:S(2)}) collective-permute-start(bf16[16,2,32,128]{3,2,1,0:T(8,128)(2,1)S(1)} %get-tuple-element.11), channel_id=1, source_target_pairs={{0,448},{32,480},{64,0},{96,32},{128,64},{160,96},{192,128},{224,1... | collective-permute-start | bytes 786440 | tf_op jit(solution)/shard_map/ppermute | solution.py:130
  48.2 12.3 %collective-permute-start.3 = (bf16[16,2,32,128]{3,2,1,0:T(8,128)(2,1)S(1)}, bf16[16,2,32,128]{3,2,1,0:T(8,128)(2,1)S(1)}, u32[]{:S(2)}, u32[]{:S(2)}) collective-permute-start(bf16[16,2,32,128]{3,2,1,0:T(8,128)(2,1)S(1)} %fusion.15), channel_id=1, source_target_pairs={{0,64},{32,96},{64,128},{96,160},{128,192},{160,224},{192,256},{22... | collective-permute-start | bytes 786440 | tf_op jit(solution)/shard_map/ppermute | solution.py:132
  50.1 17.7 %collective-permute-start.10 = (bf16[16,2,32,128]{3,2,1,0:T(8,128)(2,1)S(1)}, bf16[16,2,32,128]{3,2,1,0:T(8,128)(2,1)S(1)}, u32[]{:S(2)}, u32[]{:S(2)}) collective-permute-start(bf16[16,2,32,128]{3,2,1,0:T(8,128)(2,1)S(1)} %get-tuple-element.18), channel_id=1, source_target_pairs={{0,64},{32,96},{64,128},{96,160},{128,192},{160,224},{192,256},{22... | collective-permute-start | bytes 786440 | tf_op jit(solution)/shard_map/ppermute | solution.py:130
  52.1 15.7 %collective-permute-start.14 = (bf16[16,2,32,128]{3,2,1,0:T(8,128)(2,1)S(1)}, bf16[16,2,32,128]{3,2,1,0:T(8,128)(2,1)S(1)}, u32[]{:S(2)}, u32[]{:S(2)}) collective-permute-start(bf16[16,2,32,128]{3,2,1,0:T(8,128)(2,1)S(1)} %fusion.6), channel_id=1, source_target_pairs={{0,448},{32,480},{64,0},{96,32},{128,64},{160,96},{192,128},{224,1... | collective-permute-start | bytes 786440 | tf_op jit(solution)/shard_map/ppermute | solution.py:132
  60.7 14.4 %collective-permute-start.4 = (bf16[16,2,32,128]{3,2,1,0:T(8,128)(2,1)S(1)}, bf16[16,2,32,128]{3,2,1,0:T(8,128)(2,1)S(1)}, u32[]{:S(2)}, u32[]{:S(2)}) collective-permute-start(bf16[16,2,32,128]{3,2,1,0:T(8,128)(2,1)S(1)} %get-tuple-element.8), channel_id=1, source_target_pairs={{0,64},{32,96},{64,128},{96,160},{128,192},{160,224},{192,256},{22... | collective-permute-start | bytes 786440 | tf_op jit(solution)/shard_map/ppermute | solution.py:132
  62.6 12.4 %collective-permute-start.7 = (bf16[16,2,32,128]{3,2,1,0:T(8,128)(2,1)S(1)}, bf16[16,2,32,128]{3,2,1,0:T(8,128)(2,1)S(1)}, u32[]{:S(2)}, u32[]{:S(2)}) collective-permute-start(bf16[16,2,32,128]{3,2,1,0:T(8,128)(2,1)S(1)} %get-tuple-element.9), channel_id=1, source_target_pairs={{0,448},{32,480},{64,0},{96,32},{128,64},{160,96},{192,128},{224,1... | collective-permute-start | bytes 786440 | tf_op jit(solution)/shard_map/ppermute | solution.py:132
  68.0 14.4 %collective-permute-start.11 = (bf16[16,2,32,128]{3,2,1,0:T(8,128)(2,1)S(1)}, bf16[16,2,32,128]{3,2,1,0:T(8,128)(2,1)S(1)}, u32[]{:S(2)}, u32[]{:S(2)}) collective-permute-start(bf16[16,2,32,128]{3,2,1,0:T(8,128)(2,1)S(1)} %get-tuple-element.16), channel_id=1, source_target_pairs={{0,64},{32,96},{64,128},{96,160},{128,192},{160,224},{192,256},{22... | collective-permute-start | bytes 786440 | tf_op jit(solution)/shard_map/ppermute | solution.py:132
  69.9 12.4 %collective-permute-start.15 = (bf16[16,2,32,128]{3,2,1,0:T(8,128)(2,1)S(1)}, bf16[16,2,32,128]{3,2,1,0:T(8,128)(2,1)S(1)}, u32[]{:S(2)}, u32[]{:S(2)}) collective-permute-start(bf16[16,2,32,128]{3,2,1,0:T(8,128)(2,1)S(1)} %get-tuple-element.17), channel_id=1, source_target_pairs={{0,448},{32,480},{64,0},{96,32},{128,64},{160,96},{192,128},{224,1... | collective-permute-start | bytes 786440 | tf_op jit(solution)/shard_map/ppermute | solution.py:132
  75.3 14.5 %collective-permute-start.5 = (bf16[16,2,32,128]{3,2,1,0:T(8,128)(2,1)S(1)}, bf16[16,2,32,128]{3,2,1,0:T(8,128)(2,1)S(1)}, u32[]{:S(2)}, u32[]{:S(2)}) collective-permute-start(bf16[16,2,32,128]{3,2,1,0:T(8,128)(2,1)S(1)} %get-tuple-element.6), channel_id=1, source_target_pairs={{0,64},{32,96},{64,128},{96,160},{128,192},{160,224},{192,256},{22... | collective-permute-start | bytes 786440 | tf_op jit(solution)/shard_map/ppermute | solution.py:132
  77.2 12.6 %collective-permute-start.8 = (bf16[16,2,32,128]{3,2,1,0:T(8,128)(2,1)S(1)}, bf16[16,2,32,128]{3,2,1,0:T(8,128)(2,1)S(1)}, u32[]{:S(2)}, u32[]{:S(2)}) collective-permute-start(bf16[16,2,32,128]{3,2,1,0:T(8,128)(2,1)S(1)} %get-tuple-element.7), channel_id=1, source_target_pairs={{0,448},{32,480},{64,0},{96,32},{128,64},{160,96},{192,128},{224,1... | collective-permute-start | bytes 786440 | tf_op jit(solution)/shard_map/ppermute | solution.py:132
  82.6 9.5 %collective-permute-start.12 = (bf16[16,2,32,128]{3,2,1,0:T(8,128)(2,1)S(1)}, bf16[16,2,32,128]{3,2,1,0:T(8,128)(2,1)S(1)}, u32[]{:S(2)}, u32[]{:S(2)}) collective-permute-start(bf16[16,2,32,128]{3,2,1,0:T(8,128)(2,1)S(1)} %get-tuple-element.14), channel_id=1, source_target_pairs={{0,64},{32,96},{64,128},{96,160},{128,192},{160,224},{192,256},{22... | collective-permute-start | bytes 786440 | tf_op jit(solution)/shard_map/ppermute | solution.py:132
  84.5 20.3 %copy-start.1 = (bf16[1024,1024]{1,0:T(8,128)(2,1)S(1)}, bf16[1024,1024]{1,0:T(8,128)(2,1)}, u32[]{:S(2)}) copy-start(bf16[1024,1024]{1,0:T(8,128)(2,1)} %constant.108.clone) | copy-start | bytes 6291460
  84.5 9.1 %collective-permute-start.16 = (bf16[16,2,32,128]{3,2,1,0:T(8,128)(2,1)S(1)}, bf16[16,2,32,128]{3,2,1,0:T(8,128)(2,1)S(1)}, u32[]{:S(2)}, u32[]{:S(2)}) collective-permute-start(bf16[16,2,32,128]{3,2,1,0:T(8,128)(2,1)S(1)} %get-tuple-element.15), channel_id=1, source_target_pairs={{0,448},{32,480},{64,0},{96,32},{128,64},{160,96},{192,128},{224,1... | collective-permute-start | bytes 786440 | tf_op jit(solution)/shard_map/ppermute | solution.py:132
  94.6 24.1 %all-to-all-start = ((bf16[32,2,32,128]{3,2,1,0:T(8,128)(2,1)}), bf16[32,2,32,128]{3,2,1,0:T(8,128)(2,1)S(1)}, u32[]{:S(2)}, u32[]{:S(2)}) async-start(bf16[32,2,32,128]{3,2,1,0:T(8,128)(2,1)} %pad_maximum_fusion), calls=%async_computation | async-start | bytes 1048576 | tf_op jit(solution)/shard_map/all_to_all | solution.py:143
  119.3 1.2 copy-start.2
  121.4 14.3 %all-to-all-start.1 = ((f32[32,8,128]{2,1,0:T(8,128)}), f32[32,8,128]{2,1,0:T(8,128)S(1)}, u32[]{:S(2)}, u32[]{:S(2)}) async-start(f32[32,8,128]{2,1,0:T(8,128)} %broadcast_in_dim.18), calls=%async_computation.1 | async-start | bytes 262144 | tf_op jit(solution)/shard_map/all_to_all | solution.py:155

commit v2 on v1

v2 whole, which is shorter than its diff:
```python
import functools
import math

import jax
import jax.numpy as jnp
import numpy as np
from jax import lax
from jax.experimental import pallas as pl
from jax.experimental.pallas import tpu as pltpu
from jax.sharding import PartitionSpec as P

TR = 128
KF = 8
SZ = 1024
TPO = 2
WINDOW = 512
HALF = 16
BATCH = 4
UNROLL = 8
PIECE = 16


def dft_basis(columns):
    column_idx = np.arange(columns, dtype=np.int64)[:, None]
    freq_idx = np.arange(columns // 2, dtype=np.int64)[None, :]
    phases = ((column_idx * freq_idx) % columns).astype(np.float64) * (2.0 * math.pi / columns)
    return np.concatenate([np.cos(phases), np.sin(phases)], axis=1).astype(jnp.bfloat16)


def unit_kernel(hop, half, lanes, chips, here, *refs):
    out, listed = refs[-2:]
    refs = refs[:-1]
    sources = list(zip(refs[0:-1:2], refs[1:-1:2]))
    angles = out.shape[0]
    chip, core = here[0], here[1]
    reach = chips // 2 - hop
    target = lax.rem(chip + jnp.where(core == 0, reach, -reach) + chips, chips)
    owners = 2 * chips
    out[...] = refs[-2][...] if len(refs) % 2 == 0 else jnp.zeros_like(out)
    row = lax.broadcasted_iota(jnp.int32, (PIECE, TR), 1).astype(jnp.float32)
    depth = lax.broadcasted_iota(jnp.int32, (PIECE, TR), 0)
    zero = jnp.zeros((PIECE, TR), jnp.bfloat16)

    first_angle = core * HALF if half is None else (core ^ half) * HALF
    owner = [(2 * target + (core ^ lane)).astype(jnp.float32) for lane in range(lanes)]

    def entry(meta, a, lane):
        k = owner[lane] - meta[0, a]
        k = jnp.where(k < 0.0, k + owners, k)
        return jnp.where(k < 0.0, k + owners, k)

    live = []
    for s, (meta, _) in enumerate(sources):

        def note(i, found):
            a = (first_angle + i) & (2 * HALF - 1)
            for lane in range(lanes):
                listed[s, found] = i * lanes + lane
                found = found + jnp.where(entry(meta, a, lane) < meta[1, a], 1, 0)
            return found

        live.append(lax.fori_loop(0, angles, note, jnp.int32(0), unroll=UNROLL))

    def some(at, carry):
        for m in range(BATCH):
            for s, (meta, views) in enumerate(sources):
                place = at * BATCH + m
                n = listed[s, jnp.clip(place, 0, jnp.maximum(live[s] - 1, 0))]
                i, lane = n >> (lanes - 1), n & (lanes - 1)
                a = (first_angle + i) & (2 * HALF - 1)
                k = entry(meta, a, 0) if lanes == 1 else jnp.where(
                    lane == 0, entry(meta, a, 0), entry(meta, a, 1)
                )
                slope = meta[3, a]
                begin = (TR * k - meta[2, a]) * slope
                block = jnp.clip((begin - 1.0).astype(jnp.int32) >> 7, 0, (SZ - WINDOW) // 128)
                start = jnp.where(place < live[s], begin - (128 * block).astype(jnp.float32), -1e4)
                cycle = jnp.where(meta[0, a] + k >= owners, 1, 0)
                centre = row * slope + start
                below = jnp.floor(centre)
                above = centre - below
                at_below, at_above = (1.0 - above).astype(jnp.bfloat16), above.astype(jnp.bfloat16)
                gap = (below.astype(jnp.int32) - depth).astype(jnp.int16)
                pieces = []
                for p in range(WINDOW // PIECE):
                    hit = jnp.where(gap == jnp.int16(p * PIECE - 1), at_above, zero)
                    pieces.append(jnp.where(gap == jnp.int16(p * PIECE), at_below, hit))
                weights = jnp.concatenate(pieces, axis=0)
                z0 = pl.multiple_of(block * 128, 128)
                tile = jnp.dot(
                    views[a, :, pl.ds(z0, WINDOW)], weights, preferred_element_type=jnp.float32
                )
                old = out[i, lane, cycle].astype(jnp.float32)
                out[i, lane, cycle] = (old + tile).astype(jnp.bfloat16)
        return carry

    most = functools.reduce(jnp.maximum, live)
    lax.fori_loop(0, lax.div(most + BATCH - 1, BATCH), some, 0)


def unit(hop, half, lanes, chips, here, sources, before=None):
    angles = HALF if half is not None else 2 * HALF
    narrow = sources[0][1].shape[1]
    smem = pl.BlockSpec(memory_space=pltpu.SMEM)
    vmem = pl.BlockSpec(memory_space=pltpu.VMEM)
    operands = [here] + [ref for source in sources for ref in source]
    specs = [smem] + [smem, vmem] * len(sources)
    if before is not None:
        operands, specs = operands + [before], specs + [vmem]
    return pl.pallas_call(
        functools.partial(unit_kernel, hop, half, lanes, chips),
        out_shape=jax.ShapeDtypeStruct((angles, lanes, TPO, narrow, TR), jnp.bfloat16),
        in_specs=specs,
        out_specs=vmem,
        scratch_shapes=[pltpu.SMEM((len(sources), angles * lanes + 1), jnp.int32)],
        compiler_params=pltpu.CompilerParams(vmem_limit_bytes=16 * 1024 * 1024),
        cost_estimate=pl.CostEstimate(
            flops=10**9 * len(sources), bytes_accessed=5 * 10**6 * len(sources), transcendentals=0
        ),
    )(*operands)


def add(*terms):
    total = terms[0].astype(jnp.float32)
    for term in terms[1:]:
        total = total + term.astype(jnp.float32)
    return total.astype(jnp.bfloat16)


def body(slab_views, footprint, row_shift, stretch, projections):
    n_grp = lax.axis_size("grp")
    n_ang = lax.axis_size("ang")
    chips = n_grp // 2
    owner = lax.axis_index("grp")
    chip, core = owner // 2, owner % 2
    views = slab_views[0]
    angles = views.shape[0]
    swap = [(i, i ^ 1) for i in range(n_grp)]
    onward = [(i, (i + (2 if i % 2 == 0 else -2)) % n_grp) for i in range(n_grp)]

    sibling_views = lax.ppermute(views, "grp", swap)
    lists = footprint[0]
    count = jnp.sum((lists >= 0).astype(jnp.int32), axis=-1)
    magnify = (TR * count).astype(jnp.float32) * stretch[0] / SZ
    meta = jnp.stack(
        [lists[:, 0].astype(jnp.float32), count.astype(jnp.float32), row_shift[0], 1.0 / magnify]
    )
    sibling_meta = lax.ppermute(meta, "grp", swap)
    here = jnp.stack([chip, core])
    near, far = (meta, views), (sibling_meta, sibling_views)

    early = unit(0, 0, 2, chips, here, [near])
    moving = [lax.ppermute(unit(0, 0, 2, chips, here, [far], early), "grp", onward), None]
    for hop in range(1, 4):
        for half in (1, 0):
            mine = unit(hop, half, 2, chips, here, [near, far])
            if moving[half] is not None:
                mine = add(moving[half], mine)
            moving[half] = lax.ppermute(mine, "grp", onward)
    kept = unit(4, None, 1, chips, here, [near, far])[:, 0]
    from_sibling = lax.ppermute(jnp.stack([moving[0][:, 1], moving[1][:, 1]]), "grp", swap)
    ready = (
        add(moving[0][:, 0], from_sibling[1], kept[:HALF]),
        add(moving[1][:, 0], from_sibling[0], kept[HALF:]),
    )
    summed = jnp.where(core == 0, jnp.concatenate(ready), jnp.concatenate(ready[::-1]))

    got = lax.all_to_all(summed, "ang", split_axis=0, concat_axis=0, tiled=True)
    columns = got.shape[0] * got.shape[2]
    rows = jnp.transpose(got, (1, 3, 0, 2)).reshape(TPO * TR, columns)
    basis = jnp.asarray(dft_basis(columns))
    n_freq = columns // 2
    spec_proj = jnp.dot(projections.reshape(-1, columns), basis, preferred_element_type=jnp.float32)
    spec_grad = jnp.dot(rows, basis, preferred_element_type=jnp.float32)
    product = (
        spec_grad[:, :n_freq] * spec_proj[:, :n_freq]
        + spec_grad[:, n_freq:] * spec_proj[:, n_freq:]
    )
    share = jnp.sum(product.reshape(TPO, TR, n_freq), axis=1).reshape(-1, 128)
    shares = lax.all_to_all(
        jnp.broadcast_to(share[None], (n_ang,) + share.shape), "ang", split_axis=0, concat_axis=0, tiled=True
    )
    filter_grad = (jnp.sum(shares, axis=0) * (1.0 / (columns * angles))).reshape(TPO, 1, n_freq)
    return rows.reshape(1, TPO, TR, columns), filter_grad


def solution(mesh):
    return jax.shard_map(
        body,
        mesh=mesh,
        in_specs=(
            P("grp", None, "ang", None),
            P("grp", None, None),
            P("grp", None),
            P("grp", None),
            P("ang", None, "grp", None),
        ),
        out_specs=(P("ang", None, "grp", None), P(None, "grp", None)),
        check_vma=False,
    )
```

time: 137 us -> 135 us (0.985)
  starting transfers between devices: 75.2 us -> 47.5 us
  Pallas kernels: 19.5 us -> 32.3 us
  waiting for transfers between devices: 27.8 us -> 38.3 us
  other arithmetic: 5.28 us -> 6.98 us
    ppermute x17 -> x10, starting transfers between devices: 60.3 us -> 32.3 us  [the longest x6 22 us: body(): moving[half] = lax.ppermute(mine, 'grp', onward)]
    pallas_call x2 -> x9, Pallas kernels: 19.5 us -> 32.3 us  [unit(): pl.pallas_call(functools.partial(unit_kernel, hop, half, lanes, chips), o...]
    ppermute x17 -> x10, waiting for transfers between devices: 6.99 us -> 12.9 us  [the longest x6 11.6 us: body(): moving[half] = lax.ppermute(mine, 'grp', onward)]
    all_to_all x1, waiting for transfers between devices: 12.2 us -> 16.8 us  [body(): got = lax.all_to_all(summed, 'ang', split_axis=0, concat_axis=0, tiled=True)]
    unnamed x7 -> x19, local copies, waits for them, and re-layouts: 1.51 us -> 3.84 us
    slice x4 -> x0, local copies, waits for them, and re-layouts: 1.84 us -> none  [the longest x1 1.76 us: body(): own = views[g * part:(g + 1) * part]]
  transfers between devices with their start and end apart: 19 -> 12, of which waited for: 5 -> 5; matrix products, arithmetic and copies ran while one was open for 5% -> 5% of each run, Pallas kernels for 14% -> 22%
where the time goes in v2:
time: 135 us; the launch traced here: 134 us
  starting transfers between devices  47.5 us (35%)
  waiting for transfers between devices  38.3 us (28%)
  Pallas kernels  32.3 us (24%)
  other arithmetic  6.98 us (5%)
  local copies, waits for them, and re-layouts  5.17 us (4%)
  matrix products  2.44 us (2%)
    pallas_call x9, Pallas kernels, unit(): pl.pallas_call(functools.partial(unit_kernel, hop, half, lanes, chips), o...  32.3 us
    ppermute x6, starting transfers between devices, body(): moving[half] = lax.ppermute(mine, 'grp', onward)  22 us
    all_to_all x1, waiting for transfers between devices, body(): got = lax.all_to_all(summed, 'ang', split_axis=0, concat_axis=0, tiled=True)  16.8 us
    ppermute x6, waiting for transfers between devices, body(): moving[half] = lax.ppermute(mine, 'grp', onward)  11.6 us
    all_to_all x1, starting transfers between devices, body(): got = lax.all_to_all(summed, 'ang', split_axis=0, concat_axis=0, tiled=True)  10.2 us
    all_to_all x1, waiting for transfers between devices, body(): lax.all_to_all(jnp.broadcast_to(share[None], (n_ang,) + share.shape), 'an...  8.59 us
    all_to_all x1, starting transfers between devices, body(): lax.all_to_all(jnp.broadcast_to(share[None], (n_ang,) + share.shape), 'an...  4.99 us
    ppermute x1, starting transfers between devices, body(): lax.ppermute(unit(0, 0, 2, chips, here, [far], early), 'grp', onward)  4.01 us
  transfers between devices with their start and end apart: 12, of which 5 were waited for; matrix products, arithmetic and copies ran while one was open for 5% of the time, Pallas kernels for 22%

profile of v2, /device:TPU:8, one launch (start us, length us, event | category | flops | bytes accessed | tf_op | source)
XLA Modules:
  0.0 133.8 jit_solution(1154549908466797145)
XLA Ops:
  0.6 2.1 %collective-permute-start.1 = (bf16[32,32,1024]{2,1,0:T(8,128)(2,1)}, bf16[32,32,1024]{2,1,0:T(8,128)(2,1)}, u32[]{:S(2)}, u32[]{:S(2)}) collective-permute-start(bf16[32,32,1024]{2,1,0:T(8,128)(2,1)} %bitcast.70), channel_id=1, source_target_pairs={{0,32},{32,0},{64,96},{96,64},{128,160},{160,128},{192,224},{224,1... | collective-permute-start | bytes 6291464 | tf_op jit(solution)/shard_map/ppermute | solution.py:141
  5.4 2.4 %collective-permute-start = (f32[4,32]{1,0:T(4,128)S(1)}, f32[4,32]{1,0:T(4,128)S(1)}, u32[]{:S(2)}, u32[]{:S(2)}) collective-permute-start(f32[4,32]{1,0:T(4,128)S(1)} %pad_maximum_fusion.1.refs_0_), channel_id=1, source_target_pairs={{0,32},{32,0},{64,96},{96,64},{128,160},{160,128},{192,224},{224,1... | collective-permute-start | bytes 1544 | tf_op jit(solution)/shard_map/ppermute | solution.py:148
  11.5 2.8 %shard_map.78 = bf16[16,2,2,32,128]{4,3,2,1,0:T(8,128)(2,1)S(1)} custom-call(s32[2]{0:T(128)S(1)} %pad_add_fusion.here, f32[4,32]{1,0:T(4,128)S(1)} %collective-permute-done.refs_0_.refs_2_, bf16[32,32,1024]{2,1,0:T(8,128)(2,1)} %collective-permute-done.1.refs_1_.refs_3_, bf16[16,2,2,32,128]{4,3,2,1,0:T(8,128)(2,1)S(1)} %shard_map.77.refs_2_), custom_call_target="tpu_custom_call" | custom-call | flops 1000000000 | bytes 5000000 | tf_op jit(solution)/shard_map/pallas_call | solution.py:110
  14.3 4.0 %collective-permute-start.2 = (bf16[16,2,2,32,128]{4,3,2,0,1:T(8,128)(2,1)S(1)}, bf16[16,2,2,32,128]{4,3,2,0,1:T(8,128)(2,1)S(1)}, u32[]{:S(2)}, u32[]{:S(2)}) collective-permute-start(bf16[16,2,2,32,128]{4,3,2,0,1:T(8,128)(2,1)S(1)} %copy.27), channel_id=1, source_target_pairs={{0,64},{32,480},{64,128},{96,32},{128,192},{160,96},{192,256},{224... | collective-permute-start | bytes 1572872 | tf_op jit(solution)/shard_map/ppermute | solution.py:153
  18.3 4.2 %shard_map.82 = bf16[16,2,2,32,128]{4,3,2,1,0:T(8,128)(2,1)S(1)} custom-call(s32[2]{0:T(128)S(1)} %pad_add_fusion.here, f32[4,32]{1,0:T(4,128)S(1)} %pad_maximum_fusion.1.refs_0_, bf16[32,32,1024]{2,1,0:T(8,128)(2,1)S(1)} %bitcast.72, f32[4,32]{1,0:T(4,128)S(1)} %collective-permute-done.refs_0_.refs_2_, ...), custom_call_target="tpu_custom_call" | custom-call | flops 2000000000 | bytes 10000000 | tf_op jit(solution)/shard_map/pallas_call | solution.py:110
  22.6 4.4 %collective-permute-start.6 = (bf16[16,2,2,32,128]{4,3,2,0,1:T(8,128)(2,1)S(1)}, bf16[16,2,2,32,128]{4,3,2,0,1:T(8,128)(2,1)S(1)}, u32[]{:S(2)}, u32[]{:S(2)}) collective-permute-start(bf16[16,2,2,32,128]{4,3,2,0,1:T(8,128)(2,1)S(1)} %copy.31), channel_id=1, source_target_pairs={{0,64},{32,480},{64,128},{96,32},{128,192},{160,96},{192,256},{224... | collective-permute-start | bytes 1572872 | tf_op jit(solution)/shard_map/ppermute | solution.py:159
  27.0 4.2 %shard_map.79 = bf16[16,2,2,32,128]{4,3,2,1,0:T(8,128)(2,1)S(1)} custom-call(s32[2]{0:T(128)S(1)} %pad_add_fusion.here, f32[4,32]{1,0:T(4,128)S(1)} %pad_maximum_fusion.1.refs_0_, bf16[32,32,1024]{2,1,0:T(8,128)(2,1)S(1)} %bitcast.73, f32[4,32]{1,0:T(4,128)S(1)} %collective-permute-done.refs_0_.refs_2_, ...), custom_call_target="tpu_custom_call" | custom-call | flops 2000000000 | bytes 10000000 | tf_op jit(solution)/shard_map/pallas_call | solution.py:110
  32.6 2.5 %collective-permute-start.3 = (bf16[16,2,2,32,128]{4,3,2,0,1:T(8,128)(2,1)S(1)}, bf16[16,2,2,32,128]{4,3,2,0,1:T(8,128)(2,1)S(1)}, u32[]{:S(2)}, u32[]{:S(2)}) collective-permute-start(bf16[16,2,2,32,128]{4,3,2,0,1:T(8,128)(2,1)S(1)} %add_convert_fusion.4), channel_id=1, source_target_pairs={{0,64},{32,480},{64,128},{96,32},{128,192},{160,96},{192,256},{224... | collective-permute-start | bytes 1572872 | tf_op jit(solution)/shard_map/ppermute | solution.py:159
  35.1 4.2 %shard_map.80 = bf16[16,2,2,32,128]{4,3,2,1,0:T(8,128)(2,1)S(1)} custom-call(s32[2]{0:T(128)S(1)} %pad_add_fusion.here, f32[4,32]{1,0:T(4,128)S(1)} %pad_maximum_fusion.1.refs_0_, bf16[32,32,1024]{2,1,0:T(8,128)(2,1)S(1)} %bitcast.74, f32[4,32]{1,0:T(4,128)S(1)} %collective-permute-done.refs_0_.refs_2_, ...), custom_call_target="tpu_custom_call" | custom-call | flops 2000000000 | bytes 10000000 | tf_op jit(solution)/shard_map/pallas_call | solution.py:110
  39.3 4.2 %shard_map.83 = bf16[16,2,2,32,128]{4,3,2,1,0:T(8,128)(2,1)S(1)} custom-call(s32[2]{0:T(128)S(1)} %pad_add_fusion.here, f32[4,32]{1,0:T(4,128)S(1)} %pad_maximum_fusion.1.refs_0_, bf16[32,32,1024]{2,1,0:T(8,128)(2,1)S(1)} %bitcast.75, f32[4,32]{1,0:T(4,128)S(1)} %collective-permute-done.refs_0_.refs_2_, ...), custom_call_target="tpu_custom_call" | custom-call | flops 2000000000 | bytes 10000000 | tf_op jit(solution)/shard_map/pallas_call | solution.py:110
  43.7 4.4 %collective-permute-start.7 = (bf16[16,2,2,32,128]{4,3,2,0,1:T(8,128)(2,1)S(1)}, bf16[16,2,2,32,128]{4,3,2,0,1:T(8,128)(2,1)S(1)}, u32[]{:S(2)}, u32[]{:S(2)}) collective-permute-start(bf16[16,2,2,32,128]{4,3,2,0,1:T(8,128)(2,1)S(1)} %add_convert_fusion.1), channel_id=1, source_target_pairs={{0,64},{32,480},{64,128},{96,32},{128,192},{160,96},{192,256},{224... | collective-permute-start | bytes 1572872 | tf_op jit(solution)/shard_map/ppermute | solution.py:159
  48.3 4.6 %collective-permute-start.4 = (bf16[16,2,2,32,128]{4,3,2,0,1:T(8,128)(2,1)S(1)}, bf16[16,2,2,32,128]{4,3,2,0,1:T(8,128)(2,1)S(1)}, u32[]{:S(2)}, u32[]{:S(2)}) collective-permute-start(bf16[16,2,2,32,128]{4,3,2,0,1:T(8,128)(2,1)S(1)} %add_convert_fusion.3), channel_id=1, source_target_pairs={{0,64},{32,480},{64,128},{96,32},{128,192},{160,96},{192,256},{224... | collective-permute-start | bytes 1572872 | tf_op jit(solution)/shard_map/ppermute | solution.py:159
  52.9 3.8 %shard_map.81 = bf16[16,2,2,32,128]{4,3,2,1,0:T(8,128)(2,1)S(1)} custom-call(s32[2]{0:T(128)S(1)} %pad_add_fusion.here, f32[4,32]{1,0:T(4,128)S(1)} %pad_maximum_fusion.1.refs_0_, bf16[32,32,1024]{2,1,0:T(8,128)(2,1)S(1)} %bitcast.76, f32[4,32]{1,0:T(4,128)S(1)} %collective-permute-done.refs_0_.refs_2_, ...), custom_call_target="tpu_custom_call" | custom-call | flops 2000000000 | bytes 10000000 | tf_op jit(solution)/shard_map/pallas_call | solution.py:110
  56.6 3.8 %shard_map.84 = bf16[16,2,2,32,128]{4,3,2,1,0:T(8,128)(2,1)S(1)} custom-call(s32[2]{0:T(128)S(1)} %pad_add_fusion.here, f32[4,32]{1,0:T(4,128)S(1)} %pad_maximum_fusion.1.refs_0_, bf16[32,32,1024]{2,1,0:T(8,128)(2,1)S(1)} %bitcast.77, f32[4,32]{1,0:T(4,128)S(1)} %collective-permute-done.refs_0_.refs_2_, ...), custom_call_target="tpu_custom_call" | custom-call | flops 2000000000 | bytes 10000000 | tf_op jit(solution)/shard_map/pallas_call | solution.py:110
  60.6 2.8 %collective-permute-start.8 = (bf16[16,2,2,32,128]{4,3,2,0,1:T(8,128)(2,1)S(1)}, bf16[16,2,2,32,128]{4,3,2,0,1:T(8,128)(2,1)S(1)}, u32[]{:S(2)}, u32[]{:S(2)}) collective-permute-start(bf16[16,2,2,32,128]{4,3,2,0,1:T(8,128)(2,1)S(1)} %add_convert_fusion), channel_id=1, source_target_pairs={{0,64},{32,480},{64,128},{96,32},{128,192},{160,96},{192,256},{224... | collective-permute-start | bytes 1572872 | tf_op jit(solution)/shard_map/ppermute | solution.py:159
  63.6 3.3 %collective-permute-start.5 = (bf16[16,2,2,32,128]{4,3,2,0,1:T(8,128)(2,1)S(1)}, bf16[16,2,2,32,128]{4,3,2,0,1:T(8,128)(2,1)S(1)}, u32[]{:S(2)}, u32[]{:S(2)}) collective-permute-start(bf16[16,2,2,32,128]{4,3,2,0,1:T(8,128)(2,1)S(1)} %add_convert_fusion.2), channel_id=1, source_target_pairs={{0,64},{32,480},{64,128},{96,32},{128,192},{160,96},{192,256},{224... | collective-permute-start | bytes 1572872 | tf_op jit(solution)/shard_map/ppermute | solution.py:159
  66.9 6.0 %collective-permute-done.8 = bf16[16,2,2,32,128]{4,3,2,0,1:T(8,128)(2,1)S(1)} collective-permute-done((bf16[16,2,2,32,128]{4,3,2,0,1:T(8,128)(2,1)S(1)}, bf16[16,2,2,32,128]{4,3,2,0,1:T(8,128)(2,1)S(1)}, u32[]{:S(2)}, u32[]{:S(2)}) %collective-permute-start.8) | collective-permute-done | bytes 524320 | tf_op jit(solution)/shard_map/ppermute | solution.py:159
  72.9 5.6 %collective-permute-done.5 = bf16[16,2,2,32,128]{4,3,2,0,1:T(8,128)(2,1)S(1)} collective-permute-done((bf16[16,2,2,32,128]{4,3,2,0,1:T(8,128)(2,1)S(1)}, bf16[16,2,2,32,128]{4,3,2,0,1:T(8,128)(2,1)S(1)}, u32[]{:S(2)}, u32[]{:S(2)}) %collective-permute-start.5) | collective-permute-done | bytes 524320 | tf_op jit(solution)/shard_map/ppermute | solution.py:159
  79.3 1.9 %collective-permute-start.9 = (bf16[2,16,2,32,128]{4,3,2,1,0:T(8,128)(2,1)S(1)}, bf16[2,16,2,32,128]{4,3,2,1,0:T(8,128)(2,1)}, u32[]{:S(2)}, u32[]{:S(2)}) collective-permute-start(bf16[2,16,2,32,128]{4,3,2,1,0:T(8,128)(2,1)S(1)} %pad_maximum_fusion), channel_id=1, source_target_pairs={{0,32},{32,0},{64,96},{96,64},{128,160},{160,128},{192,224},{224,1... | collective-permute-start | bytes 1572872 | tf_op jit(solution)/shard_map/ppermute | solution.py:161
  81.3 3.4 %shard_map.85 = bf16[32,1,2,32,128]{4,3,2,1,0:T(8,128)(2,1)S(1)} custom-call(s32[2]{0:T(128)S(1)} %pad_add_fusion.here, f32[4,32]{1,0:T(4,128)S(1)} %pad_maximum_fusion.1.refs_0_, bf16[32,32,1024]{2,1,0:T(8,128)(2,1)S(1)} %bitcast.78, f32[4,32]{1,0:T(4,128)S(1)} %collective-permute-done.refs_0_.refs_2_, ...), custom_call_target="tpu_custom_call" | custom-call | flops 2000000000 | bytes 10000000 | tf_op jit(solution)/shard_map/pallas_call | solution.py:110
  87.1 10.2 %all-to-all-start = ((bf16[32,2,32,128]{3,2,1,0:T(8,128)(2,1)}), bf16[32,2,32,128]{3,2,1,0:T(8,128)(2,1)S(1)}, u32[]{:S(2)}, u32[]{:S(2)}) async-start(bf16[32,2,32,128]{3,2,1,0:T(8,128)(2,1)} %maximum_select_fusion), calls=%async_computation | async-start | bytes 1048576 | tf_op jit(solution)/shard_map/all_to_all | solution.py:168
  99.0 16.8 %all-to-all-done = bf16[32,2,32,128]{3,2,1,0:T(8,128)(2,1)S(1)} async-done(((bf16[32,2,32,128]{3,2,1,0:T(8,128)(2,1)}), bf16[32,2,32,128]{3,2,1,0:T(8,128)(2,1)S(1)}, u32[]{:S(2)}, u32[]{:S(2)}) %all-to-all-start) | async-done | bytes 524320 | tf_op jit(solution)/shard_map/all_to_all | solution.py:168
  118.5 5.0 %all-to-all-start.1 = ((f32[32,8,128]{2,1,0:T(8,128)}), f32[32,8,128]{2,1,0:T(8,128)S(1)}, u32[]{:S(2)}, u32[]{:S(2)}) async-start(f32[32,8,128]{2,1,0:T(8,128)} %broadcast_in_dim.8), calls=%async_computation.1 | async-start | bytes 262144 | tf_op jit(solution)/shard_map/all_to_all | solution.py:180
  124.5 8.6 %all-to-all-done.1 = f32[32,8,128]{2,1,0:T(8,128)S(1)} async-done(((f32[32,8,128]{2,1,0:T(8,128)}), f32[32,8,128]{2,1,0:T(8,128)S(1)}, u32[]{:S(2)}, u32[]{:S(2)}) %all-to-all-start.1) | async-done | bytes 131104 | tf_op jit(solution)/shard_map/all_to_all | solution.py:180
  (55 shorter events, 17.8 us)
Async XLA Ops:
  0.6 96.6 %copy-start = (bf16[1,2,128,1024]{3,2,1,0:T(8,128)(2,1)S(1)}, bf16[1,2,128,1024]{3,2,1,0:T(8,128)(2,1)}, u32[]{:S(2)}) copy-start(bf16[1,2,128,1024]{3,2,1,0:T(8,128)(2,1)} %param.10) | copy-start | bytes 1572868
  0.6 10.8 %collective-permute-start.1 = (bf16[32,32,1024]{2,1,0:T(8,128)(2,1)}, bf16[32,32,1024]{2,1,0:T(8,128)(2,1)}, u32[]{:S(2)}, u32[]{:S(2)}) collective-permute-start(bf16[32,32,1024]{2,1,0:T(8,128)(2,1)} %bitcast.70), channel_id=1, source_target_pairs={{0,32},{32,0},{64,96},{96,64},{128,160},{160,128},{192,224},{224,1... | collective-permute-start | bytes 6291464 | tf_op jit(solution)/shard_map/ppermute | solution.py:141
  5.4 6.0 %collective-permute-start = (f32[4,32]{1,0:T(4,128)S(1)}, f32[4,32]{1,0:T(4,128)S(1)}, u32[]{:S(2)}, u32[]{:S(2)}) collective-permute-start(f32[4,32]{1,0:T(4,128)S(1)} %pad_maximum_fusion.1.refs_0_), channel_id=1, source_target_pairs={{0,32},{32,0},{64,96},{96,64},{128,160},{160,128},{192,224},{224,1... | collective-permute-start | bytes 1544 | tf_op jit(solution)/shard_map/ppermute | solution.py:148
  7.9 1.6 %copy-start.1 = (bf16[1,32,32,1024]{3,2,1,0:T(8,128)(2,1)S(1)}, bf16[1,32,32,1024]{3,2,1,0:T(8,128)(2,1)}, u32[]{:S(2)}) copy-start(bf16[1,32,32,1024]{3,2,1,0:T(8,128)(2,1)} %param.6) | copy-start | bytes 6291460
  11.4 6.9 %copy-start.2 = (bf16[1,32,32,1024]{3,2,1,0:T(8,128)(2,1)S(1)}, bf16[1,32,32,1024]{3,2,1,0:T(8,128)(2,1)}, u32[]{:S(2)}) copy-start(bf16[1,32,32,1024]{3,2,1,0:T(8,128)(2,1)} %param.6) | copy-start | bytes 6291460
  14.3 18.1 %collective-permute-start.2 = (bf16[16,2,2,32,128]{4,3,2,0,1:T(8,128)(2,1)S(1)}, bf16[16,2,2,32,128]{4,3,2,0,1:T(8,128)(2,1)S(1)}, u32[]{:S(2)}, u32[]{:S(2)}) collective-permute-start(bf16[16,2,2,32,128]{4,3,2,0,1:T(8,128)(2,1)S(1)} %copy.27), channel_id=1, source_target_pairs={{0,64},{32,480},{64,128},{96,32},{128,192},{160,96},{192,256},{224... | collective-permute-start | bytes 1572872 | tf_op jit(solution)/shard_map/ppermute | solution.py:153
  22.6 20.9 %collective-permute-start.6 = (bf16[16,2,2,32,128]{4,3,2,0,1:T(8,128)(2,1)S(1)}, bf16[16,2,2,32,128]{4,3,2,0,1:T(8,128)(2,1)S(1)}, u32[]{:S(2)}, u32[]{:S(2)}) collective-permute-start(bf16[16,2,2,32,128]{4,3,2,0,1:T(8,128)(2,1)S(1)} %copy.31), channel_id=1, source_target_pairs={{0,64},{32,480},{64,128},{96,32},{128,192},{160,96},{192,256},{224... | collective-permute-start | bytes 1572872 | tf_op jit(solution)/shard_map/ppermute | solution.py:159
  32.6 15.5 %collective-permute-start.3 = (bf16[16,2,2,32,128]{4,3,2,0,1:T(8,128)(2,1)S(1)}, bf16[16,2,2,32,128]{4,3,2,0,1:T(8,128)(2,1)S(1)}, u32[]{:S(2)}, u32[]{:S(2)}) collective-permute-start(bf16[16,2,2,32,128]{4,3,2,0,1:T(8,128)(2,1)S(1)} %add_convert_fusion.4), channel_id=1, source_target_pairs={{0,64},{32,480},{64,128},{96,32},{128,192},{160,96},{192,256},{224... | collective-permute-start | bytes 1572872 | tf_op jit(solution)/shard_map/ppermute | solution.py:159
  43.7 16.7 %collective-permute-start.7 = (bf16[16,2,2,32,128]{4,3,2,0,1:T(8,128)(2,1)S(1)}, bf16[16,2,2,32,128]{4,3,2,0,1:T(8,128)(2,1)S(1)}, u32[]{:S(2)}, u32[]{:S(2)}) collective-permute-start(bf16[16,2,2,32,128]{4,3,2,0,1:T(8,128)(2,1)S(1)} %add_convert_fusion.1), channel_id=1, source_target_pairs={{0,64},{32,480},{64,128},{96,32},{128,192},{160,96},{192,256},{224... | collective-permute-start | bytes 1572872 | tf_op jit(solution)/shard_map/ppermute | solution.py:159
  48.3 15.1 %collective-permute-start.4 = (bf16[16,2,2,32,128]{4,3,2,0,1:T(8,128)(2,1)S(1)}, bf16[16,2,2,32,128]{4,3,2,0,1:T(8,128)(2,1)S(1)}, u32[]{:S(2)}, u32[]{:S(2)}) collective-permute-start(bf16[16,2,2,32,128]{4,3,2,0,1:T(8,128)(2,1)S(1)} %add_convert_fusion.3), channel_id=1, source_target_pairs={{0,64},{32,480},{64,128},{96,32},{128,192},{160,96},{192,256},{224... | collective-permute-start | bytes 1572872 | tf_op jit(solution)/shard_map/ppermute | solution.py:159
  60.6 12.3 %collective-permute-start.8 = (bf16[16,2,2,32,128]{4,3,2,0,1:T(8,128)(2,1)S(1)}, bf16[16,2,2,32,128]{4,3,2,0,1:T(8,128)(2,1)S(1)}, u32[]{:S(2)}, u32[]{:S(2)}) collective-permute-start(bf16[16,2,2,32,128]{4,3,2,0,1:T(8,128)(2,1)S(1)} %add_convert_fusion), channel_id=1, source_target_pairs={{0,64},{32,480},{64,128},{96,32},{128,192},{160,96},{192,256},{224... | collective-permute-start | bytes 1572872 | tf_op jit(solution)/shard_map/ppermute | solution.py:159
  63.6 14.9 %collective-permute-start.5 = (bf16[16,2,2,32,128]{4,3,2,0,1:T(8,128)(2,1)S(1)}, bf16[16,2,2,32,128]{4,3,2,0,1:T(8,128)(2,1)S(1)}, u32[]{:S(2)}, u32[]{:S(2)}) collective-permute-start(bf16[16,2,2,32,128]{4,3,2,0,1:T(8,128)(2,1)S(1)} %add_convert_fusion.2), channel_id=1, source_target_pairs={{0,64},{32,480},{64,128},{96,32},{128,192},{160,96},{192,256},{224... | collective-permute-start | bytes 1572872 | tf_op jit(solution)/shard_map/ppermute | solution.py:159
  72.9 5.7 %copy-start.5 = (bf16[16,2,2,32,128]{4,3,2,0,1:T(8,128)(2,1)}, bf16[16,2,2,32,128]{4,3,2,0,1:T(8,128)(2,1)S(1)}, u32[]{:S(2)}) copy-start(bf16[16,2,2,32,128]{4,3,2,0,1:T(8,128)(2,1)S(1)} %collective-permute-done.8) | copy-start | bytes 1572868
  78.5 0.8 copy-start.7
  79.3 5.4 %collective-permute-start.9 = (bf16[2,16,2,32,128]{4,3,2,1,0:T(8,128)(2,1)S(1)}, bf16[2,16,2,32,128]{4,3,2,1,0:T(8,128)(2,1)}, u32[]{:S(2)}, u32[]{:S(2)}) collective-permute-start(bf16[2,16,2,32,128]{4,3,2,1,0:T(8,128)(2,1)S(1)} %pad_maximum_fusion), channel_id=1, source_target_pairs={{0,32},{32,0},{64,96},{96,64},{128,160},{160,128},{192,224},{224,1... | collective-permute-start | bytes 1572872 | tf_op jit(solution)/shard_map/ppermute | solution.py:161
  81.2 3.5 %copy-start.6 = (bf16[16,2,2,32,128]{4,3,2,0,1:T(8,128)(2,1)S(1)}, bf16[16,2,2,32,128]{4,3,2,0,1:T(8,128)(2,1)}, u32[]{:S(2)}) copy-start(bf16[16,2,2,32,128]{4,3,2,0,1:T(8,128)(2,1)} %copy-done.5) | copy-start | bytes 1572868
  81.2 3.5 %copy-start.8 = (bf16[16,2,2,32,128]{4,3,2,0,1:T(8,128)(2,1)S(1)}, bf16[16,2,2,32,128]{4,3,2,0,1:T(8,128)(2,1)}, u32[]{:S(2)}) copy-start(bf16[16,2,2,32,128]{4,3,2,0,1:T(8,128)(2,1)} %copy-done.7) | copy-start | bytes 1572868
  84.7 12.5 %copy-start.3 = (bf16[1024,1024]{1,0:T(8,128)(2,1)S(1)}, bf16[1024,1024]{1,0:T(8,128)(2,1)}, u32[]{:S(2)}) copy-start(bf16[1024,1024]{1,0:T(8,128)(2,1)} %constant.45.clone) | copy-start | bytes 6291460
  87.1 28.7 %all-to-all-start = ((bf16[32,2,32,128]{3,2,1,0:T(8,128)(2,1)}), bf16[32,2,32,128]{3,2,1,0:T(8,128)(2,1)S(1)}, u32[]{:S(2)}, u32[]{:S(2)}) async-start(bf16[32,2,32,128]{3,2,1,0:T(8,128)(2,1)} %maximum_select_fusion), calls=%async_computation | async-start | bytes 1048576 | tf_op jit(solution)/shard_map/all_to_all | solution.py:168
  116.3 1.2 copy-start.4
  118.5 14.7 %all-to-all-start.1 = ((f32[32,8,128]{2,1,0:T(8,128)}), f32[32,8,128]{2,1,0:T(8,128)S(1)}, u32[]{:S(2)}, u32[]{:S(2)}) async-start(f32[32,8,128]{2,1,0:T(8,128)} %broadcast_in_dim.8), calls=%async_computation.1 | async-start | bytes 262144 | tf_op jit(solution)/shard_map/all_to_all | solution.py:180

commit v3 on v2

v3 whole, which is shorter than its diff:
```python
import functools
import math

import jax
import jax.numpy as jnp
import numpy as np
from jax import lax
from jax.experimental import pallas as pl
from jax.experimental.pallas import tpu as pltpu
from jax.sharding import PartitionSpec as P

TR = 128
KF = 8
SZ = 1024
TPO = 2
WINDOW = 512
HALF = 16
BATCH = 8
UNROLL = 16
PIECE = 16


def dft_basis(columns):
    column_idx = np.arange(columns, dtype=np.int64)[:, None]
    freq_idx = np.arange(columns // 2, dtype=np.int64)[None, :]
    phases = ((column_idx * freq_idx) % columns).astype(np.float64) * (2.0 * math.pi / columns)
    return np.concatenate([np.cos(phases), np.sin(phases)], axis=1).astype(jnp.bfloat16)


def unit_kernel(hop, lanes, chips, near, near_views, far, far_views, *refs):
    outs, (total, listed) = refs[:-2], refs[-2:]
    angles = total.shape[0]
    chip, core = near[4, 0].astype(jnp.int32), near[4, 1].astype(jnp.int32)
    reach = chips // 2 - hop
    target = lax.rem(chip + jnp.where(core == 0, reach, -reach) + chips, chips)
    owners = 2 * chips
    sources = ((near, near_views), (far, far_views))
    row = lax.broadcasted_iota(jnp.int32, (PIECE, TR), 1).astype(jnp.float32)
    depth = lax.broadcasted_iota(jnp.int32, (PIECE, TR), 0)
    zero = jnp.zeros((PIECE, TR), jnp.bfloat16)
    owner = [(2 * target + (core ^ lane)).astype(jnp.float32) for lane in range(lanes)]
    first_angle = core * HALF
    total[...] = jnp.zeros_like(total)

    def entry(meta, a, lane):
        k = owner[lane] - meta[0, a]
        k = jnp.where(k < 0.0, k + owners, k)
        return jnp.where(k < 0.0, k + owners, k)

    live = []
    for s, (meta, _) in enumerate(sources):

        def note(i, found):
            a = (first_angle + i) & (2 * HALF - 1)
            for lane in range(lanes):
                listed[s, found] = i * lanes + lane
                found = found + jnp.where(entry(meta, a, lane) < meta[1, a], 1, 0)
            return found

        live.append(lax.fori_loop(0, angles, note, jnp.int32(0), unroll=UNROLL))

    def some(at, carry):
        for m in range(BATCH):
            for s, (meta, views) in enumerate(sources):
                place = at * BATCH + m
                n = listed[s, jnp.clip(place, 0, jnp.maximum(live[s] - 1, 0))]
                i, lane = n >> (lanes - 1), n & (lanes - 1)
                a = (first_angle + i) & (2 * HALF - 1)
                k = entry(meta, a, 0) if lanes == 1 else jnp.where(
                    lane == 0, entry(meta, a, 0), entry(meta, a, 1)
                )
                slope = meta[3, a]
                begin = (TR * k - meta[2, a]) * slope
                block = jnp.clip((begin - 1.0).astype(jnp.int32) >> 7, 0, (SZ - WINDOW) // 128)
                start = jnp.where(place < live[s], begin - (128 * block).astype(jnp.float32), -1e4)
                cycle = jnp.where(meta[0, a] + k >= owners, 1, 0)
                centre = row * slope + start
                below = jnp.floor(centre)
                above = centre - below
                at_below = (1.0 - above).astype(jnp.bfloat16)
                at_above = above.astype(jnp.bfloat16)
                gap = (below.astype(jnp.int32) - depth).astype(jnp.int16)
                pieces = []
                for p in range(WINDOW // PIECE):
                    hit = jnp.where(gap == jnp.int16(p * PIECE - 1), at_above, zero)
                    pieces.append(jnp.where(gap == jnp.int16(p * PIECE), at_below, hit))
                weights = jnp.concatenate(pieces, axis=0)
                z0 = pl.multiple_of(block * 128, 128)
                total[i, lane, cycle] += jnp.dot(
                    views[a, :, pl.ds(z0, WINDOW)], weights, preferred_element_type=jnp.float32
                )
        return carry

    most = functools.reduce(jnp.maximum, live)
    lax.fori_loop(0, lax.div(most + BATCH - 1, BATCH), some, 0)
    for half, out in enumerate(outs):
        out[...] = total[half * HALF : (half + 1) * HALF].astype(jnp.bfloat16)


def units(hop, halves, lanes, chips, near, near_views, far, far_views):
    narrow = near_views.shape[1]
    smem = pl.BlockSpec(memory_space=pltpu.SMEM)
    vmem = pl.BlockSpec(memory_space=pltpu.VMEM)
    shape = (HALF, lanes, TPO, narrow, TR)
    return pl.pallas_call(
        functools.partial(unit_kernel, hop, lanes, chips),
        out_shape=[jax.ShapeDtypeStruct(shape, jnp.bfloat16)] * halves,
        in_specs=[smem, vmem, smem, vmem],
        out_specs=[vmem] * halves,
        scratch_shapes=[
            pltpu.VMEM((halves * HALF,) + shape[1:], jnp.float32),
            pltpu.SMEM((2, halves * HALF * lanes + 1), jnp.int32),
        ],
        compiler_params=pltpu.CompilerParams(vmem_limit_bytes=16 * 1024 * 1024),
        cost_estimate=pl.CostEstimate(
            flops=25 * 10**8 * halves, bytes_accessed=10**6, transcendentals=0
        ),
    )(near, near_views, far, far_views)


def add(*terms):
    total = terms[0].astype(jnp.float32)
    for term in terms[1:]:
        total = total + term.astype(jnp.float32)
    return total.astype(jnp.bfloat16)


def body(slab_views, footprint, row_shift, stretch, projections):
    n_grp = lax.axis_size("grp")
    n_ang = lax.axis_size("ang")
    chips = n_grp // 2
    owner = lax.axis_index("grp")
    chip, core = owner // 2, owner % 2
    views = slab_views[0]
    angles = views.shape[0]
    swap = [(i, i ^ 1) for i in range(n_grp)]
    onward = [(i, (i + (2 if i % 2 == 0 else -2)) % n_grp) for i in range(n_grp)]

    sibling_views = lax.ppermute(views, "grp", swap)
    lists = footprint[0]
    count = sum((lists[:, k] >= 0).astype(jnp.float32) for k in range(KF))
    magnify = TR * count * stretch[0] / SZ
    place = jnp.where(jnp.arange(angles) == 0, chip, core).astype(jnp.float32)
    meta = jnp.stack([lists[:, 0].astype(jnp.float32), count, row_shift[0], 1.0 / magnify, place])
    known = (chips, meta, views, lax.ppermute(meta, "grp", swap), sibling_views)

    moving = [lax.ppermute(units(0, 1, 2, *known)[0], "grp", onward), None]
    for hop in range(1, 4):
        mine = units(hop, 2, 2, *known)
        for half in (1, 0):
            sending = mine[half] if moving[half] is None else add(moving[half], mine[half])
            moving[half] = lax.ppermute(sending, "grp", onward)
    kept = [own[:, 0] for own in units(4, 2, 1, *known)]
    from_sibling = lax.ppermute(jnp.stack([moving[0][:, 1], moving[1][:, 1]]), "grp", swap)
    ready = (
        add(moving[0][:, 0], from_sibling[1], kept[0]),
        add(moving[1][:, 0], from_sibling[0], kept[1]),
    )
    summed = jnp.where(core == 0, jnp.concatenate(ready), jnp.concatenate(ready[::-1]))

    n_freq = n_ang * views.shape[1] // 2
    basis = jnp.asarray(dft_basis(2 * n_freq))
    spec_proj = jnp.dot(
        projections.reshape(-1, 2 * n_freq), basis, preferred_element_type=jnp.float32
    )
    summed, spec_proj = lax.optimization_barrier((summed, spec_proj))
    got = lax.all_to_all(summed, "ang", split_axis=0, concat_axis=0, tiled=True)
    rows = jnp.transpose(got, (1, 3, 0, 2)).reshape(TPO * TR, 2 * n_freq)
    spec_grad = jnp.dot(rows, basis, preferred_element_type=jnp.float32)
    product = (
        spec_grad[:, :n_freq] * spec_proj[:, :n_freq]
        + spec_grad[:, n_freq:] * spec_proj[:, n_freq:]
    )
    share = jnp.sum(product.reshape(TPO, TR, n_freq), axis=1).reshape(-1, 128)
    rows, share = lax.optimization_barrier((rows.reshape(1, TPO, TR, 2 * n_freq), share))
    shares = lax.all_to_all(
        jnp.broadcast_to(share[None], (n_ang,) + share.shape), "ang", split_axis=0, concat_axis=0, tiled=True
    )
    filter_grad = (jnp.sum(shares, axis=0) * (1.0 / (2 * n_freq * angles))).reshape(TPO, 1, n_freq)
    return rows, filter_grad


def solution(mesh):
    return jax.shard_map(
        body,
        mesh=mesh,
        in_specs=(
            P("grp", None, "ang", None),
            P("grp", None, None),
            P("grp", None),
            P("grp", None),
            P("ang", None, "grp", None),
        ),
        out_specs=(P("ang", None, "grp", None), P(None, "grp", None)),
        check_vma=False,
    )
```

time: 135 us -> 127 us (0.941)
  blocking collectives: 0 us -> 28.4 us
  starting transfers between devices: 47.5 us -> 30.2 us
  Pallas kernels: 32.3 us -> 19.1 us
  waiting for transfers between devices: 38.3 us -> 32.3 us
  local copies, waits for them, and re-layouts: 5.17 us -> 6.88 us
  other arithmetic: 6.98 us -> 5.42 us
    all_to_all x0 -> x1, blocking collectives: none -> 28.4 us  [body(): got = lax.all_to_all(summed, 'ang', split_axis=0, concat_axis=0, tiled=True)]
    all_to_all x1 -> x0, waiting for transfers between devices: 16.8 us -> none  [body(): got = lax.all_to_all(summed, 'ang', split_axis=0, concat_axis=0, tiled=True)]
    pallas_call x9 -> x5, Pallas kernels: 32.3 us -> 19.1 us  [units(): pl.pallas_call(functools.partial(unit_kernel, hop, lanes, chips), out_sha...]
    ppermute x8, waiting for transfers between devices: 12.8 us -> 23.6 us  [the longest x6 18 us: body(): moving[half] = lax.ppermute(sending, 'grp', onward)]
    all_to_all x1 -> x0, starting transfers between devices: 10.2 us -> none  [body(): got = lax.all_to_all(summed, 'ang', split_axis=0, concat_axis=0, tiled=True)]
    ppermute x8, starting transfers between devices: 28.4 us -> 21.4 us  [the longest x6 14 us: body(): moving[half] = lax.ppermute(sending, 'grp', onward)]
    unnamed x19 -> x25, local copies, waits for them, and re-layouts: 3.84 us -> 4.49 us
  transfers between devices with their start and end apart: 12 -> 11, of which waited for: 5 -> 9; matrix products, arithmetic and copies ran while one was open for 5% -> 5% of each run, Pallas kernels for 22% -> 13%
where the time goes in v3:
time: 127 us; the launch traced here: 126 us
  waiting for transfers between devices  32.3 us (25%)
  starting transfers between devices  30.2 us (24%)
  blocking collectives  28.4 us (22%)
  Pallas kernels  19.1 us (15%)
  local copies, waits for them, and re-layouts  6.88 us (5%)
  other arithmetic  5.42 us (4%)
  matrix products  2.71 us (2%)
    all_to_all x1, blocking collectives, body(): got = lax.all_to_all(summed, 'ang', split_axis=0, concat_axis=0, tiled=True)  28.4 us
    pallas_call x5, Pallas kernels, units(): pl.pallas_call(functools.partial(unit_kernel, hop, lanes, chips), out_sha...  19.1 us
    ppermute x6, waiting for transfers between devices, body(): moving[half] = lax.ppermute(sending, 'grp', onward)  18 us
    ppermute x6, starting transfers between devices, body(): moving[half] = lax.ppermute(sending, 'grp', onward)  14 us
    all_to_all x1, waiting for transfers between devices, body(): lax.all_to_all(jnp.broadcast_to(share[None], (n_ang,) + share.shape), 'an...  8.66 us
    ppermute x1, starting transfers between devices, body(): moving = [lax.ppermute(units(0, 1, 2, *known)[0], 'grp', onward), None]  5.02 us
    ppermute x1, waiting for transfers between devices, body(): moving = [lax.ppermute(units(0, 1, 2, *known)[0], 'grp', onward), None]  4.84 us
    all_to_all x1, starting transfers between devices, body(): lax.all_to_all(jnp.broadcast_to(share[None], (n_ang,) + share.shape), 'an...  4.84 us
  transfers between devices with their start and end apart: 11, of which 9 were waited for; matrix products, arithmetic and copies ran while one was open for 5% of the time, Pallas kernels for 13%

profile of v3, /device:TPU:8, one launch (start us, length us, event | category | flops | bytes accessed | tf_op | source)
XLA Modules:
  0.0 126.1 jit_solution(329266719899911644)
XLA Ops:
  0.6 2.1 %collective-permute-start.1 = (bf16[32,32,1024]{2,1,0:T(8,128)(2,1)}, bf16[32,32,1024]{2,1,0:T(8,128)(2,1)S(1)}, u32[]{:S(2)}, u32[]{:S(2)}) collective-permute-start(bf16[32,32,1024]{2,1,0:T(8,128)(2,1)} %bitcast.58), channel_id=1, source_target_pairs={{0,32},{32,0},{64,96},{96,64},{128,160},{160,128},{192,224},{224,1... | collective-permute-start | bytes 6291464 | tf_op jit(solution)/shard_map/ppermute | solution.py:139
  5.1 2.4 %collective-permute-start = (f32[5,32]{1,0:T(8,128)S(1)}, f32[5,32]{1,0:T(8,128)S(1)}, u32[]{:S(2)}, u32[]{:S(2)}) collective-permute-start(f32[5,32]{1,0:T(8,128)S(1)} %stack.4.near), channel_id=1, source_target_pairs={{0,32},{32,0},{64,96},{96,64},{128,160},{160,128},{192,224},{224,1... | collective-permute-start | bytes 1928 | tf_op jit(solution)/shard_map/ppermute | solution.py:145
  9.9 2.6 %shard_map.77 = bf16[16,2,2,32,128]{4,3,2,1,0:T(8,128)(2,1)S(1)} custom-call(f32[5,32]{1,0:T(8,128)S(1)} %stack.4.near, bf16[32,32,1024]{2,1,0:T(8,128)(2,1)S(1)} %bitcast.59, f32[5,32]{1,0:T(8,128)S(1)} %collective-permute-done.far, bf16[32,32,1024]{2,1,0:T(8,128)(2,1)S(1)} %collective-permute-done.1.far_views), custom_call_target="tpu_custom_call" | custom-call | flops 2500000000 | bytes 1000000 | tf_op jit(solution)/shard_map/pallas_call | solution.py:105
  12.5 5.0 %collective-permute-start.2 = (bf16[16,2,2,32,128]{4,3,2,0,1:T(8,128)(2,1)S(1)}, bf16[16,2,2,32,128]{4,3,2,0,1:T(8,128)(2,1)S(1)}, u32[]{:S(2)}, u32[]{:S(2)}) collective-permute-start(bf16[16,2,2,32,128]{4,3,2,0,1:T(8,128)(2,1)S(1)} %copy.58), channel_id=1, source_target_pairs={{0,64},{32,480},{64,128},{96,32},{128,192},{160,96},{192,256},{224... | collective-permute-start | bytes 1572872 | tf_op jit(solution)/shard_map/ppermute | solution.py:147
  17.6 4.6 %shard_map.78 = (bf16[16,2,2,32,128]{4,3,2,1,0:T(8,128)(2,1)S(1)}, bf16[16,2,2,32,128]{4,3,2,1,0:T(8,128)(2,1)S(1)}) custom-call(f32[5,32]{1,0:T(8,128)S(1)} %stack.4.near, bf16[32,32,1024]{2,1,0:T(8,128)(2,1)S(1)} %bitcast.60, f32[5,32]{1,0:T(8,128)S(1)} %collective-permute-done.far, bf16[32,32,1024]{2,1,0:T(8,128)(2,1)S(1)} %collective-permute-done.1.far_views), custom_call_target="tpu_custom_call" | custom-call | flops 5000000000 | bytes 1000000 | tf_op jit(solution)/shard_map/pallas_call | solution.py:105
  22.2 4.3 %collective-permute-start.6 = (bf16[16,2,2,32,128]{4,3,2,0,1:T(8,128)(2,1)S(1)}, bf16[16,2,2,32,128]{4,3,2,0,1:T(8,128)(2,1)S(1)}, u32[]{:S(2)}, u32[]{:S(2)}) collective-permute-start(bf16[16,2,2,32,128]{4,3,2,0,1:T(8,128)(2,1)S(1)} %copy.62), channel_id=1, source_target_pairs={{0,64},{32,480},{64,128},{96,32},{128,192},{160,96},{192,256},{224... | collective-permute-start | bytes 1572872 | tf_op jit(solution)/shard_map/ppermute | solution.py:152
  26.5 4.8 %collective-permute-done.2 = bf16[16,2,2,32,128]{4,3,2,0,1:T(8,128)(2,1)S(1)} collective-permute-done((bf16[16,2,2,32,128]{4,3,2,0,1:T(8,128)(2,1)S(1)}, bf16[16,2,2,32,128]{4,3,2,0,1:T(8,128)(2,1)S(1)}, u32[]{:S(2)}, u32[]{:S(2)}) %collective-permute-start.2) | collective-permute-done | bytes 524320 | tf_op jit(solution)/shard_map/ppermute | solution.py:147
  31.6 1.9 %collective-permute-start.3 = (bf16[16,2,2,32,128]{4,3,2,0,1:T(8,128)(2,1)S(1)}, bf16[16,2,2,32,128]{4,3,2,0,1:T(8,128)(2,1)S(1)}, u32[]{:S(2)}, u32[]{:S(2)}) collective-permute-start(bf16[16,2,2,32,128]{4,3,2,0,1:T(8,128)(2,1)S(1)} %add_convert_fusion.4), channel_id=1, source_target_pairs={{0,64},{32,480},{64,128},{96,32},{128,192},{160,96},{192,256},{224... | collective-permute-start | bytes 1572872 | tf_op jit(solution)/shard_map/ppermute | solution.py:152
  33.5 4.6 %shard_map.79 = (bf16[16,2,2,32,128]{4,3,2,1,0:T(8,128)(2,1)S(1)}, bf16[16,2,2,32,128]{4,3,2,1,0:T(8,128)(2,1)S(1)}) custom-call(f32[5,32]{1,0:T(8,128)S(1)} %stack.4.near, bf16[32,32,1024]{2,1,0:T(8,128)(2,1)S(1)} %bitcast.61, f32[5,32]{1,0:T(8,128)S(1)} %collective-permute-done.far, bf16[32,32,1024]{2,1,0:T(8,128)(2,1)S(1)} %collective-permute-done.1.far_views), custom_call_target="tpu_custom_call" | custom-call | flops 5000000000 | bytes 1000000 | tf_op jit(solution)/shard_map/pallas_call | solution.py:105
  38.9 1.9 %collective-permute-start.7 = (bf16[16,2,2,32,128]{4,3,2,0,1:T(8,128)(2,1)S(1)}, bf16[16,2,2,32,128]{4,3,2,0,1:T(8,128)(2,1)S(1)}, u32[]{:S(2)}, u32[]{:S(2)}) collective-permute-start(bf16[16,2,2,32,128]{4,3,2,0,1:T(8,128)(2,1)S(1)} %add_convert_fusion.1), channel_id=1, source_target_pairs={{0,64},{32,480},{64,128},{96,32},{128,192},{160,96},{192,256},{224... | collective-permute-start | bytes 1572872 | tf_op jit(solution)/shard_map/ppermute | solution.py:152
  40.8 3.5 %collective-permute-done.3 = bf16[16,2,2,32,128]{4,3,2,0,1:T(8,128)(2,1)S(1)} collective-permute-done((bf16[16,2,2,32,128]{4,3,2,0,1:T(8,128)(2,1)S(1)}, bf16[16,2,2,32,128]{4,3,2,0,1:T(8,128)(2,1)S(1)}, u32[]{:S(2)}, u32[]{:S(2)}) %collective-permute-start.3) | collective-permute-done | bytes 524320 | tf_op jit(solution)/shard_map/ppermute | solution.py:152
  44.5 1.9 %collective-permute-start.4 = (bf16[16,2,2,32,128]{4,3,2,0,1:T(8,128)(2,1)S(1)}, bf16[16,2,2,32,128]{4,3,2,0,1:T(8,128)(2,1)S(1)}, u32[]{:S(2)}, u32[]{:S(2)}) collective-permute-start(bf16[16,2,2,32,128]{4,3,2,0,1:T(8,128)(2,1)S(1)} %add_convert_fusion.3), channel_id=1, source_target_pairs={{0,64},{32,480},{64,128},{96,32},{128,192},{160,96},{192,256},{224... | collective-permute-start | bytes 1572872 | tf_op jit(solution)/shard_map/ppermute | solution.py:152
  46.5 4.6 %shard_map.80 = (bf16[16,2,2,32,128]{4,3,2,1,0:T(8,128)(2,1)S(1)}, bf16[16,2,2,32,128]{4,3,2,1,0:T(8,128)(2,1)S(1)}) custom-call(f32[5,32]{1,0:T(8,128)S(1)} %stack.4.near, bf16[32,32,1024]{2,1,0:T(8,128)(2,1)S(1)} %bitcast.62, f32[5,32]{1,0:T(8,128)S(1)} %collective-permute-done.far, bf16[32,32,1024]{2,1,0:T(8,128)(2,1)S(1)} %collective-permute-done.1.far_views), custom_call_target="tpu_custom_call" | custom-call | flops 5000000000 | bytes 1000000 | tf_op jit(solution)/shard_map/pallas_call | solution.py:105
  51.4 2.1 %collective-permute-start.8 = (bf16[16,2,2,32,128]{4,3,2,0,1:T(8,128)(2,1)S(1)}, bf16[16,2,2,32,128]{4,3,2,0,1:T(8,128)(2,1)S(1)}, u32[]{:S(2)}, u32[]{:S(2)}) collective-permute-start(bf16[16,2,2,32,128]{4,3,2,0,1:T(8,128)(2,1)S(1)} %add_convert_fusion), channel_id=1, source_target_pairs={{0,64},{32,480},{64,128},{96,32},{128,192},{160,96},{192,256},{224... | collective-permute-start | bytes 1572872 | tf_op jit(solution)/shard_map/ppermute | solution.py:152
  53.5 3.4 %collective-permute-done.4 = bf16[16,2,2,32,128]{4,3,2,0,1:T(8,128)(2,1)S(1)} collective-permute-done((bf16[16,2,2,32,128]{4,3,2,0,1:T(8,128)(2,1)S(1)}, bf16[16,2,2,32,128]{4,3,2,0,1:T(8,128)(2,1)S(1)}, u32[]{:S(2)}, u32[]{:S(2)}) %collective-permute-start.4) | collective-permute-done | bytes 524320 | tf_op jit(solution)/shard_map/ppermute | solution.py:152
  57.0 1.9 %collective-permute-start.5 = (bf16[16,2,2,32,128]{4,3,2,0,1:T(8,128)(2,1)S(1)}, bf16[16,2,2,32,128]{4,3,2,0,1:T(8,128)(2,1)S(1)}, u32[]{:S(2)}, u32[]{:S(2)}) collective-permute-start(bf16[16,2,2,32,128]{4,3,2,0,1:T(8,128)(2,1)S(1)} %add_convert_fusion.2), channel_id=1, source_target_pairs={{0,64},{32,480},{64,128},{96,32},{128,192},{160,96},{192,256},{224... | collective-permute-start | bytes 1572872 | tf_op jit(solution)/shard_map/ppermute | solution.py:152
  58.9 4.9 %collective-permute-done.8 = bf16[16,2,2,32,128]{4,3,2,0,1:T(8,128)(2,1)S(1)} collective-permute-done((bf16[16,2,2,32,128]{4,3,2,0,1:T(8,128)(2,1)S(1)}, bf16[16,2,2,32,128]{4,3,2,0,1:T(8,128)(2,1)S(1)}, u32[]{:S(2)}, u32[]{:S(2)}) %collective-permute-start.8) | collective-permute-done | bytes 524320 | tf_op jit(solution)/shard_map/ppermute | solution.py:152
  63.8 5.6 %collective-permute-done.5 = bf16[16,2,2,32,128]{4,3,2,0,1:T(8,128)(2,1)S(1)} collective-permute-done((bf16[16,2,2,32,128]{4,3,2,0,1:T(8,128)(2,1)S(1)}, bf16[16,2,2,32,128]{4,3,2,0,1:T(8,128)(2,1)S(1)}, u32[]{:S(2)}, u32[]{:S(2)}) %collective-permute-start.5) | collective-permute-done | bytes 524320 | tf_op jit(solution)/shard_map/ppermute | solution.py:152
  69.5 1.9 %collective-permute-start.9 = (bf16[2,16,2,32,128]{4,3,2,1,0:T(8,128)(2,1)S(1)}, bf16[2,16,2,32,128]{4,3,2,1,0:T(8,128)(2,1)}, u32[]{:S(2)}, u32[]{:S(2)}) collective-permute-start(bf16[2,16,2,32,128]{4,3,2,1,0:T(8,128)(2,1)S(1)} %pad_maximum_fusion), channel_id=1, source_target_pairs={{0,32},{32,0},{64,96},{96,64},{128,160},{160,128},{192,224},{224,1... | collective-permute-start | bytes 1572872 | tf_op jit(solution)/shard_map/ppermute | solution.py:154
  71.5 1.8 %convolution_bitcast_fusion = f32[256,1024]{0,1:T(8,128)} fusion(bf16[1024,1024]{1,0:T(8,128)(2,1)S(1)} %copy-done.5, bf16[256,1024]{1,0:T(8,128)(2,1)S(1)} %bitcast.57), kind=kOutput, calls=%fused_computation | convolution fusion | flops 536870912 | bytes 3670016 | tf_op jit(solution)/shard_map/dot_general | solution.py:163
  74.9 2.7 %shard_map.81 = (bf16[16,1,2,32,128]{4,3,2,1,0:T(8,128)(2,1)S(1)}, bf16[16,1,2,32,128]{4,3,2,1,0:T(8,128)(2,1)S(1)}) custom-call(f32[5,32]{1,0:T(8,128)S(1)} %stack.4.near, bf16[32,32,1024]{2,1,0:T(8,128)(2,1)S(1)} %bitcast.63, f32[5,32]{1,0:T(8,128)S(1)} %collective-permute-done.far, bf16[32,32,1024]{2,1,0:T(8,128)(2,1)S(1)} %copy-done.4), custom_call_target="tpu_custom_call" | custom-call | flops 5000000000 | bytes 1000000 | tf_op jit(solution)/shard_map/pallas_call | solution.py:105
  79.0 28.4 %all_to_all.10 = bf16[32,2,32,128]{3,2,1,0:T(8,128)(2,1)S(1)} all-to-all(bf16[32,2,32,128]{3,2,1,0:T(8,128)(2,1)S(1)} %maximum_select_fusion), channel_id=1, replica_groups=mesh['grp'=16,'ang'=32] {'ang'}, dimensions={0} | all-to-all | bytes 1048576 | tf_op jit(solution)/shard_map/all_to_all | solution.py:167
  111.0 4.8 %all-to-all-start.1 = ((f32[32,8,128]{2,1,0:T(8,128)}), f32[32,8,128]{2,1,0:T(8,128)S(1)}, u32[]{:S(2)}, u32[]{:S(2)}) async-start(f32[32,8,128]{2,1,0:T(8,128)} %broadcast_in_dim.16), calls=%async_computation.1 | async-start | bytes 262144 | tf_op jit(solution)/shard_map/all_to_all | solution.py:176
  116.8 8.7 %all-to-all-done.1 = f32[32,8,128]{2,1,0:T(8,128)S(1)} async-done(((f32[32,8,128]{2,1,0:T(8,128)}), f32[32,8,128]{2,1,0:T(8,128)S(1)}, u32[]{:S(2)}, u32[]{:S(2)}) %all-to-all-start.1) | async-done | bytes 131104 | tf_op jit(solution)/shard_map/all_to_all | solution.py:176
  (57 shorter events, 14.7 us)
Async XLA Ops:
  0.6 70.8 %copy-start = (bf16[1,2,128,1024]{3,2,1,0:T(8,128)(2,1)S(1)}, bf16[1,2,128,1024]{3,2,1,0:T(8,128)(2,1)}, u32[]{:S(2)}) copy-start(bf16[1,2,128,1024]{3,2,1,0:T(8,128)(2,1)} %param.10) | copy-start | bytes 1572868
  0.6 7.7 %collective-permute-start.1 = (bf16[32,32,1024]{2,1,0:T(8,128)(2,1)}, bf16[32,32,1024]{2,1,0:T(8,128)(2,1)S(1)}, u32[]{:S(2)}, u32[]{:S(2)}) collective-permute-start(bf16[32,32,1024]{2,1,0:T(8,128)(2,1)} %bitcast.58), channel_id=1, source_target_pairs={{0,32},{32,0},{64,96},{96,64},{128,160},{160,128},{192,224},{224,1... | collective-permute-start | bytes 6291464 | tf_op jit(solution)/shard_map/ppermute | solution.py:139
  5.1 3.2 %collective-permute-start = (f32[5,32]{1,0:T(8,128)S(1)}, f32[5,32]{1,0:T(8,128)S(1)}, u32[]{:S(2)}, u32[]{:S(2)}) collective-permute-start(f32[5,32]{1,0:T(8,128)S(1)} %stack.4.near), channel_id=1, source_target_pairs={{0,32},{32,0},{64,96},{96,64},{128,160},{160,128},{192,224},{224,1... | collective-permute-start | bytes 1928 | tf_op jit(solution)/shard_map/ppermute | solution.py:145
  8.3 1.6 %copy-start.1 = (bf16[1,32,32,1024]{3,2,1,0:T(8,128)(2,1)S(1)}, bf16[1,32,32,1024]{3,2,1,0:T(8,128)(2,1)}, u32[]{:S(2)}) copy-start(bf16[1,32,32,1024]{3,2,1,0:T(8,128)(2,1)} %param.6) | copy-start | bytes 6291460
  9.9 36.6 %copy-start.3 = (bf16[32,32,1024]{2,1,0:T(8,128)(2,1)}, bf16[32,32,1024]{2,1,0:T(8,128)(2,1)S(1)}, u32[]{:S(2)}) copy-start(bf16[32,32,1024]{2,1,0:T(8,128)(2,1)S(1)} %collective-permute-done.1.far_views) | copy-start | bytes 6291460
  12.5 18.8 %collective-permute-start.2 = (bf16[16,2,2,32,128]{4,3,2,0,1:T(8,128)(2,1)S(1)}, bf16[16,2,2,32,128]{4,3,2,0,1:T(8,128)(2,1)S(1)}, u32[]{:S(2)}, u32[]{:S(2)}) collective-permute-start(bf16[16,2,2,32,128]{4,3,2,0,1:T(8,128)(2,1)S(1)} %copy.58), channel_id=1, source_target_pairs={{0,64},{32,480},{64,128},{96,32},{128,192},{160,96},{192,256},{224... | collective-permute-start | bytes 1572872 | tf_op jit(solution)/shard_map/ppermute | solution.py:147
  22.2 16.5 %collective-permute-start.6 = (bf16[16,2,2,32,128]{4,3,2,0,1:T(8,128)(2,1)S(1)}, bf16[16,2,2,32,128]{4,3,2,0,1:T(8,128)(2,1)S(1)}, u32[]{:S(2)}, u32[]{:S(2)}) collective-permute-start(bf16[16,2,2,32,128]{4,3,2,0,1:T(8,128)(2,1)S(1)} %copy.62), channel_id=1, source_target_pairs={{0,64},{32,480},{64,128},{96,32},{128,192},{160,96},{192,256},{224... | collective-permute-start | bytes 1572872 | tf_op jit(solution)/shard_map/ppermute | solution.py:152
  31.6 12.8 %collective-permute-start.3 = (bf16[16,2,2,32,128]{4,3,2,0,1:T(8,128)(2,1)S(1)}, bf16[16,2,2,32,128]{4,3,2,0,1:T(8,128)(2,1)S(1)}, u32[]{:S(2)}, u32[]{:S(2)}) collective-permute-start(bf16[16,2,2,32,128]{4,3,2,0,1:T(8,128)(2,1)S(1)} %add_convert_fusion.4), channel_id=1, source_target_pairs={{0,64},{32,480},{64,128},{96,32},{128,192},{160,96},{192,256},{224... | collective-permute-start | bytes 1572872 | tf_op jit(solution)/shard_map/ppermute | solution.py:152
  38.9 12.3 %collective-permute-start.7 = (bf16[16,2,2,32,128]{4,3,2,0,1:T(8,128)(2,1)S(1)}, bf16[16,2,2,32,128]{4,3,2,0,1:T(8,128)(2,1)S(1)}, u32[]{:S(2)}, u32[]{:S(2)}) collective-permute-start(bf16[16,2,2,32,128]{4,3,2,0,1:T(8,128)(2,1)S(1)} %add_convert_fusion.1), channel_id=1, source_target_pairs={{0,64},{32,480},{64,128},{96,32},{128,192},{160,96},{192,256},{224... | collective-permute-start | bytes 1572872 | tf_op jit(solution)/shard_map/ppermute | solution.py:152
  44.5 12.3 %collective-permute-start.4 = (bf16[16,2,2,32,128]{4,3,2,0,1:T(8,128)(2,1)S(1)}, bf16[16,2,2,32,128]{4,3,2,0,1:T(8,128)(2,1)S(1)}, u32[]{:S(2)}, u32[]{:S(2)}) collective-permute-start(bf16[16,2,2,32,128]{4,3,2,0,1:T(8,128)(2,1)S(1)} %add_convert_fusion.3), channel_id=1, source_target_pairs={{0,64},{32,480},{64,128},{96,32},{128,192},{160,96},{192,256},{224... | collective-permute-start | bytes 1572872 | tf_op jit(solution)/shard_map/ppermute | solution.py:152
  51.4 20.1 %copy-start.5 = (bf16[1024,1024]{1,0:T(8,128)(2,1)S(1)}, bf16[1024,1024]{1,0:T(8,128)(2,1)}, u32[]{:S(2)}) copy-start(bf16[1024,1024]{1,0:T(8,128)(2,1)} %constant.45.clone) | copy-start | bytes 6291460
  51.4 12.4 %collective-permute-start.8 = (bf16[16,2,2,32,128]{4,3,2,0,1:T(8,128)(2,1)S(1)}, bf16[16,2,2,32,128]{4,3,2,0,1:T(8,128)(2,1)S(1)}, u32[]{:S(2)}, u32[]{:S(2)}) collective-permute-start(bf16[16,2,2,32,128]{4,3,2,0,1:T(8,128)(2,1)S(1)} %add_convert_fusion), channel_id=1, source_target_pairs={{0,64},{32,480},{64,128},{96,32},{128,192},{160,96},{192,256},{224... | collective-permute-start | bytes 1572872 | tf_op jit(solution)/shard_map/ppermute | solution.py:152
  57.0 12.4 %collective-permute-start.5 = (bf16[16,2,2,32,128]{4,3,2,0,1:T(8,128)(2,1)S(1)}, bf16[16,2,2,32,128]{4,3,2,0,1:T(8,128)(2,1)S(1)}, u32[]{:S(2)}, u32[]{:S(2)}) collective-permute-start(bf16[16,2,2,32,128]{4,3,2,0,1:T(8,128)(2,1)S(1)} %add_convert_fusion.2), channel_id=1, source_target_pairs={{0,64},{32,480},{64,128},{96,32},{128,192},{160,96},{192,256},{224... | collective-permute-start | bytes 1572872 | tf_op jit(solution)/shard_map/ppermute | solution.py:152
  63.8 7.6 %copy-start.8 = (bf16[16,2,2,32,128]{4,3,2,0,1:T(8,128)(2,1)}, bf16[16,2,2,32,128]{4,3,2,0,1:T(8,128)(2,1)S(1)}, u32[]{:S(2)}) copy-start(bf16[16,2,2,32,128]{4,3,2,0,1:T(8,128)(2,1)S(1)} %collective-permute-done.8) | copy-start | bytes 1572868
  69.4 2.0 %copy-start.10 = (bf16[16,2,2,32,128]{4,3,2,0,1:T(8,128)(2,1)}, bf16[16,2,2,32,128]{4,3,2,0,1:T(8,128)(2,1)S(1)}, u32[]{:S(2)}) copy-start(bf16[16,2,2,32,128]{4,3,2,0,1:T(8,128)(2,1)S(1)} %collective-permute-done.5) | copy-start | bytes 1572868
  69.5 8.0 %collective-permute-start.9 = (bf16[2,16,2,32,128]{4,3,2,1,0:T(8,128)(2,1)S(1)}, bf16[2,16,2,32,128]{4,3,2,1,0:T(8,128)(2,1)}, u32[]{:S(2)}, u32[]{:S(2)}) collective-permute-start(bf16[2,16,2,32,128]{4,3,2,1,0:T(8,128)(2,1)S(1)} %pad_maximum_fusion), channel_id=1, source_target_pairs={{0,32},{32,0},{64,96},{96,64},{128,160},{160,128},{192,224},{224,1... | collective-permute-start | bytes 1572872 | tf_op jit(solution)/shard_map/ppermute | solution.py:154
  71.5 1.8 %copy-start.2 = (bf16[1,32,32,1024]{3,2,1,0:T(8,128)(2,1)S(1)}, bf16[1,32,32,1024]{3,2,1,0:T(8,128)(2,1)}, u32[]{:S(2)}) copy-start(bf16[1,32,32,1024]{3,2,1,0:T(8,128)(2,1)} %param.6) | copy-start | bytes 6291460
  73.3 1.6 %copy-start.4 = (bf16[32,32,1024]{2,1,0:T(8,128)(2,1)S(1)}, bf16[32,32,1024]{2,1,0:T(8,128)(2,1)}, u32[]{:S(2)}) copy-start(bf16[32,32,1024]{2,1,0:T(8,128)(2,1)} %copy-done.3) | copy-start | bytes 6291460
  74.9 2.7 %copy-start.9 = (bf16[16,2,2,32,128]{4,3,2,0,1:T(8,128)(2,1)S(1)}, bf16[16,2,2,32,128]{4,3,2,0,1:T(8,128)(2,1)}, u32[]{:S(2)}) copy-start(bf16[16,2,2,32,128]{4,3,2,0,1:T(8,128)(2,1)} %copy-done.8) | copy-start | bytes 1572868
  74.9 2.7 %copy-start.11 = (bf16[16,2,2,32,128]{4,3,2,0,1:T(8,128)(2,1)S(1)}, bf16[16,2,2,32,128]{4,3,2,0,1:T(8,128)(2,1)}, u32[]{:S(2)}) copy-start(bf16[16,2,2,32,128]{4,3,2,0,1:T(8,128)(2,1)} %copy-done.10) | copy-start | bytes 1572868
  78.8 29.1 %copy-start.6 = (bf16[1024,1024]{1,0:T(8,128)(2,1)S(1)}, bf16[1024,1024]{1,0:T(8,128)(2,1)}, u32[]{:S(2)}) copy-start(bf16[1024,1024]{1,0:T(8,128)(2,1)} %constant.45.clone) | copy-start | bytes 6291460
  107.9 1.2 copy-start.7
  111.0 14.5 %all-to-all-start.1 = ((f32[32,8,128]{2,1,0:T(8,128)}), f32[32,8,128]{2,1,0:T(8,128)S(1)}, u32[]{:S(2)}, u32[]{:S(2)}) async-start(f32[32,8,128]{2,1,0:T(8,128)} %broadcast_in_dim.16), calls=%async_computation.1 | async-start | bytes 262144 | tf_op jit(solution)/shard_map/all_to_all | solution.py:176

commit v4 on v3

--- a/solution.py
+++ b/solution.py
@@ -29,7 +29,7 @@
 
 def unit_kernel(hop, lanes, chips, near, near_views, far, far_views, *refs):
     outs, (total, listed) = refs[:-2], refs[-2:]
-    angles = total.shape[0]
+    angles = total.shape[1]
     chip, core = near[4, 0].astype(jnp.int32), near[4, 1].astype(jnp.int32)
     reach = chips // 2 - hop
     target = lax.rem(chip + jnp.where(core == 0, reach, -reach) + chips, chips)
@@ -86,7 +86,7 @@
                     pieces.append(jnp.where(gap == jnp.int16(p * PIECE), at_below, hit))
                 weights = jnp.concatenate(pieces, axis=0)
                 z0 = pl.multiple_of(block * 128, 128)
-                total[i, lane, cycle] += jnp.dot(
+                total[lane, i, cycle] += jnp.dot(
                     views[a, :, pl.ds(z0, WINDOW)], weights, preferred_element_type=jnp.float32
                 )
         return carry
@@ -94,21 +94,21 @@
     most = functools.reduce(jnp.maximum, live)
     lax.fori_loop(0, lax.div(most + BATCH - 1, BATCH), some, 0)
     for half, out in enumerate(outs):
-        out[...] = total[half * HALF : (half + 1) * HALF].astype(jnp.bfloat16)
+        out[...] = total[:, half * HALF : (half + 1) * HALF].astype(jnp.bfloat16)
 
 
 def units(hop, halves, lanes, chips, near, near_views, far, far_views):
     narrow = near_views.shape[1]
     smem = pl.BlockSpec(memory_space=pltpu.SMEM)
     vmem = pl.BlockSpec(memory_space=pltpu.VMEM)
-    shape = (HALF, lanes, TPO, narrow, TR)
+    shape = (lanes, HALF, TPO, narrow, TR)
     return pl.pallas_call(
         functools.partial(unit_kernel, hop, lanes, chips),
         out_shape=[jax.ShapeDtypeStruct(shape, jnp.bfloat16)] * halves,
         in_specs=[smem, vmem, smem, vmem],
         out_specs=[vmem] * halves,
         scratch_shapes=[
-            pltpu.VMEM((halves * HALF,) + shape[1:], jnp.float32),
+            pltpu.VMEM((lanes, halves * HALF) + shape[2:], jnp.float32),
             pltpu.SMEM((2, halves * HALF * lanes + 1), jnp.int32),
         ],
         compiler_params=pltpu.CompilerParams(vmem_limit_bytes=16 * 1024 * 1024),
@@ -123,6 +123,36 @@
     for term in terms[1:]:
         total = total + term.astype(jnp.float32)
     return total.astype(jnp.bfloat16)
+
+
+def finish_kernel(got, basis, spec_proj, rows, copies):
+    n_freq = basis.shape[1] // 2
+    blocks = n_freq // 128
+    for p in range(TPO):
+        turned = got[:, p].reshape(-1, TR).T
+        rows[0, p] = turned
+        spec_grad = jnp.dot(turned, basis[...], preferred_element_type=jnp.float32)
+        both = spec_grad * spec_proj[p * TR : (p + 1) * TR]
+        share = jnp.sum(both[:, :n_freq] + both[:, n_freq:], axis=0, keepdims=True)
+        for n in range(blocks):
+            block = jnp.broadcast_to(share[:, n * 128 : (n + 1) * 128], (copies.shape[0], 1, 128))
+            copies[:, p * blocks + n : p * blocks + n + 1] = block
+
+
+def finish(got, basis, spec_proj, n_ang):
+    columns = basis.shape[0]
+    vmem = pl.BlockSpec(memory_space=pltpu.VMEM)
+    return pl.pallas_call(
+        finish_kernel,
+        out_shape=[
+            jax.ShapeDtypeStruct((1, TPO, TR, columns), jnp.bfloat16),
+            jax.ShapeDtypeStruct((n_ang, TPO * columns // 256, 128), jnp.float32),
+        ],
+        in_specs=[vmem] * 3,
+        out_specs=[vmem] * 2,
+        compiler_params=pltpu.CompilerParams(vmem_limit_bytes=24 * 1024 * 1024),
+        cost_estimate=pl.CostEstimate(flops=10**9, bytes_accessed=10**6, transcendentals=0),
+    )(got, basis, spec_proj)
 
 
 def body(slab_views, footprint, row_shift, stretch, projections):
@@ -144,38 +174,40 @@
     meta = jnp.stack([lists[:, 0].astype(jnp.float32), count, row_shift[0], 1.0 / magnify, place])
     known = (chips, meta, views, lax.ppermute(meta, "grp", swap), sibling_views)
 
-    moving = [lax.ppermute(units(0, 1, 2, *known)[0], "grp", onward), None]
-    for hop in range(1, 4):
-        mine = units(hop, 2, 2, *known)
-        for half in (1, 0):
-            sending = mine[half] if moving[half] is None else add(moving[half], mine[half])
-            moving[half] = lax.ppermute(sending, "grp", onward)
-    kept = [own[:, 0] for own in units(4, 2, 1, *known)]
-    from_sibling = lax.ppermute(jnp.stack([moving[0][:, 1], moving[1][:, 1]]), "grp", swap)
-    ready = (
-        add(moving[0][:, 0], from_sibling[1], kept[0]),
-        add(moving[1][:, 0], from_sibling[0], kept[1]),
-    )
-    summed = jnp.where(core == 0, jnp.concatenate(ready), jnp.concatenate(ready[::-1]))
+    across = [(i, j ^ 1) for i, j in onward]
 
     n_freq = n_ang * views.shape[1] // 2
     basis = jnp.asarray(dft_basis(2 * n_freq))
     spec_proj = jnp.dot(
         projections.reshape(-1, 2 * n_freq), basis, preferred_element_type=jnp.float32
     )
-    summed, spec_proj = lax.optimization_barrier((summed, spec_proj))
+
+    first = lax.ppermute(units(0, 1, 2, *known)[0], "grp", onward)
+    mine = units(1, 2, 2, *known)
+    second = lax.ppermute(mine[1], "grp", onward)
+    later = units(2, 2, 2, *known)
+    sending, later, meta = lax.optimization_barrier((add(first, mine[0]), later, meta))
+    first = lax.ppermute(sending, "grp", onward)
+    known = known[:1] + (meta,) + known[2:]
+    last = units(3, 2, 2, *known)
+    sending, last = lax.optimization_barrier((add(second, later[1]), last))
+    second = lax.ppermute(sending, "grp", onward)
+    kept = units(4, 2, 1, *known)
+    sending, kept = lax.optimization_barrier((add(first, later[0]), kept))
+    first = lax.ppermute(sending, "grp", onward)
+    sending, spec_proj = lax.optimization_barrier((add(second, last[1]), spec_proj))
+    second = [lax.ppermute(sending[lane], "grp", (onward, across)[lane]) for lane in range(2)]
+    sending = add(first, last[0])
+    first = [lax.ppermute(sending[lane], "grp", (onward, across)[lane]) for lane in range(2)]
+    ready = (
+        add(first[0], second[1], kept[0][0]),
+        add(second[0], first[1], kept[1][0]),
+    )
+    summed = jnp.where(core == 0, jnp.concatenate(ready), jnp.concatenate(ready[::-1]))
+
     got = lax.all_to_all(summed, "ang", split_axis=0, concat_axis=0, tiled=True)
-    rows = jnp.transpose(got, (1, 3, 0, 2)).reshape(TPO * TR, 2 * n_freq)
-    spec_grad = jnp.dot(rows, basis, preferred_element_type=jnp.float32)
-    product = (
-        spec_grad[:, :n_freq] * spec_proj[:, :n_freq]
-        + spec_grad[:, n_freq:] * spec_proj[:, n_freq:]
-    )
-    share = jnp.sum(product.reshape(TPO, TR, n_freq), axis=1).reshape(-1, 128)
-    rows, share = lax.optimization_barrier((rows.reshape(1, TPO, TR, 2 * n_freq), share))
-    shares = lax.all_to_all(
-        jnp.broadcast_to(share[None], (n_ang,) + share.shape), "ang", split_axis=0, concat_axis=0, tiled=True
-    )
+    rows, copies = finish(got, basis, spec_proj, n_ang)
+    shares = lax.all_to_all(copies, "ang", split_axis=0, concat_axis=0, tiled=True)
     filter_grad = (jnp.sum(shares, axis=0) * (1.0 / (2 * n_freq * angles))).reshape(TPO, 1, n_freq)
     return rows, filter_grad
 

time: 127 us -> 122 us (0.961)
  waiting for transfers between devices: 32.3 us -> 8.29 us
  blocking collectives: 28.4 us -> 40.5 us
  starting transfers between devices: 30.2 us -> 36.2 us
  Pallas kernels: 19.1 us -> 22 us
  local copies, waits for them, and re-layouts: 6.88 us -> 5.45 us
    ppermute x8 -> x9, waiting for transfers between devices: 22.8 us -> 7.49 us  [the longest x4 5.88 us: body(): lax.ppermute(sending[lane], 'grp', (onward, across)[lane])]
    all_to_all x0 -> x1, blocking collectives: none -> 14.3 us  [body(): lax.all_to_all(copies, 'ang', split_axis=0, concat_axis=0, tiled=True)]
    ppermute x8 -> x9, starting transfers between devices: 21 us -> 31.7 us  [the longest x4 13 us: body(): lax.ppermute(sending[lane], 'grp', (onward, across)[lane])]
    all_to_all x1 -> x0, waiting for transfers between devices: 8.66 us -> none  [body(): lax.all_to_all(jnp.broadcast_to(share[None], (n_ang,) + share.shape), 'an...]
    all_to_all x1 -> x0, starting transfers between devices: 4.84 us -> none  [body(): lax.all_to_all(jnp.broadcast_to(share[None], (n_ang,) + share.shape), 'an...]
    all_to_all x1, blocking collectives: 28.4 us -> 26.2 us  [body(): got = lax.all_to_all(summed, 'ang', split_axis=0, concat_axis=0, tiled=True)]
    squeeze x0 -> x2, local copies, waits for them, and re-layouts: none -> 1.57 us  [body(): sending[lane]]
    pallas_call x5, Pallas kernels: 19.1 us -> 20.6 us  [units(): pl.pallas_call(functools.partial(unit_kernel, hop, lanes, chips), out_sha...]
  transfers between devices with their start and end apart: 11 -> 11, of which waited for: 9 -> 5; matrix products, arithmetic and copies ran while one was open for 5% -> 6% of each run, Pallas kernels for 13% -> 14%
where the time goes in v4:
time: 122 us; the launch traced here: 121 us
  blocking collectives  40.5 us (33%)
  starting transfers between devices  36.2 us (30%)
  Pallas kernels  22 us (18%)
  waiting for transfers between devices  8.29 us (7%)
  other arithmetic  5.7 us (5%)
  local copies, waits for them, and re-layouts  5.45 us (4%)
  matrix products  1.71 us (1%)
    all_to_all x1, blocking collectives, body(): got = lax.all_to_all(summed, 'ang', split_axis=0, concat_axis=0, tiled=True)  26.2 us
    pallas_call x5, Pallas kernels, units(): pl.pallas_call(functools.partial(unit_kernel, hop, lanes, chips), out_sha...  20.6 us
    all_to_all x1, blocking collectives, body(): lax.all_to_all(copies, 'ang', split_axis=0, concat_axis=0, tiled=True)  14.3 us
    ppermute x4, starting transfers between devices, body(): lax.ppermute(sending[lane], 'grp', (onward, across)[lane])  13 us
    ppermute x2, starting transfers between devices, body(): first = lax.ppermute(sending, 'grp', onward)  7.44 us
    ppermute x4, waiting for transfers between devices, body(): lax.ppermute(sending[lane], 'grp', (onward, across)[lane])  5.88 us
    ppermute x1, starting transfers between devices, body(): second = lax.ppermute(sending, 'grp', onward)  4.89 us
    ppermute x1, starting transfers between devices, body(): second = lax.ppermute(mine[1], 'grp', onward)  3.54 us
  transfers between devices with their start and end apart: 11, of which 5 were waited for; matrix products, arithmetic and copies ran while one was open for 6% of the time, Pallas kernels for 14%

profile of v4, /device:TPU:8, one launch (start us, length us, event | category | flops | bytes accessed | tf_op | source)
XLA Modules:
  0.0 120.8 jit_solution(13788945000555847747)
XLA Ops:
  0.6 2.1 %collective-permute-start.1 = (bf16[32,32,1024]{2,1,0:T(8,128)(2,1)}, bf16[32,32,1024]{2,1,0:T(8,128)(2,1)S(1)}, u32[]{:S(2)}, u32[]{:S(2)}) collective-permute-start(bf16[32,32,1024]{2,1,0:T(8,128)(2,1)} %bitcast.28), channel_id=1, source_target_pairs={{0,32},{32,0},{64,96},{96,64},{128,160},{160,128},{192,224},{224,1... | collective-permute-start | bytes 6291464 | tf_op jit(solution)/shard_map/ppermute | solution.py:169
  5.1 2.4 %collective-permute-start = (f32[5,32]{1,0:T(8,128)S(1)}, f32[5,32]{1,0:T(8,128)S(1)}, u32[]{:S(2)}, u32[]{:S(2)}) collective-permute-start(f32[5,32]{1,0:T(8,128)S(1)} %stack.2.near), channel_id=1, source_target_pairs={{0,32},{32,0},{64,96},{96,64},{128,160},{160,128},{192,224},{224,1... | collective-permute-start | bytes 1928 | tf_op jit(solution)/shard_map/ppermute | solution.py:175
  8.3 1.6 %copy-done.3 = bf16[1,32,32,1024]{3,2,1,0:T(8,128)(2,1)S(1)} copy-done((bf16[1,32,32,1024]{3,2,1,0:T(8,128)(2,1)S(1)}, bf16[1,32,32,1024]{3,2,1,0:T(8,128)(2,1)}, u32[]{:S(2)}) %copy-start.3) | copy-done | bytes 2097176
  9.9 4.0 %shard_map.77 = bf16[2,16,2,32,128]{4,3,2,1,0:T(8,128)(2,1)S(1)} custom-call(f32[5,32]{1,0:T(8,128)S(1)} %stack.2.near, bf16[32,32,1024]{2,1,0:T(8,128)(2,1)S(1)} %bitcast.29, f32[5,32]{1,0:T(8,128)S(1)} %collective-permute-done.far, bf16[32,32,1024]{2,1,0:T(8,128)(2,1)S(1)} %collective-permute-done.1.far_views), custom_call_target="tpu_custom_call" | custom-call | flops 2500000000 | bytes 1000000 | tf_op jit(solution)/shard_map/pallas_call | solution.py:105
  14.0 2.8 %collective-permute-start.2 = (bf16[2,16,2,32,128]{4,3,2,1,0:T(8,128)(2,1)S(1)}, bf16[2,16,2,32,128]{4,3,2,1,0:T(8,128)(2,1)S(1)}, u32[]{:S(2)}, u32[]{:S(2)}) collective-permute-start(bf16[2,16,2,32,128]{4,3,2,1,0:T(8,128)(2,1)S(1)} %shard_map.77), channel_id=1, source_target_pairs={{0,64},{32,480},{64,128},{96,32},{128,192},{160,96},{192,256},{224... | collective-permute-start | bytes 1572872 | tf_op jit(solution)/shard_map/ppermute | solution.py:185
  16.8 5.4 %shard_map.78 = (bf16[2,16,2,32,128]{4,3,2,1,0:T(8,128)(2,1)S(1)}, bf16[2,16,2,32,128]{4,3,2,1,0:T(8,128)(2,1)S(1)}) custom-call(f32[5,32]{1,0:T(8,128)S(1)} %stack.2.near, bf16[32,32,1024]{2,1,0:T(8,128)(2,1)S(1)} %bitcast.30, f32[5,32]{1,0:T(8,128)S(1)} %collective-permute-done.far, bf16[32,32,1024]{2,1,0:T(8,128)(2,1)S(1)} %collective-permute-done.1.far_views), custom_call_target="tpu_custom_call" | custom-call | flops 5000000000 | bytes 1000000 | tf_op jit(solution)/shard_map/pallas_call | solution.py:105
  22.2 3.5 %collective-permute-start.5 = (bf16[2,16,2,32,128]{4,3,2,1,0:T(8,128)(2,1)S(1)}, bf16[2,16,2,32,128]{4,3,2,1,0:T(8,128)(2,1)S(1)}, u32[]{:S(2)}, u32[]{:S(2)}) collective-permute-start(bf16[2,16,2,32,128]{4,3,2,1,0:T(8,128)(2,1)S(1)} %get-tuple-element.33), channel_id=1, source_target_pairs={{0,64},{32,480},{64,128},{96,32},{128,192},{160,96},{192,256},{224... | collective-permute-start | bytes 1572872 | tf_op jit(solution)/shard_map/ppermute | solution.py:187
  25.7 4.6 %shard_map.79 = (bf16[2,16,2,32,128]{4,3,2,1,0:T(8,128)(2,1)S(1)}, bf16[2,16,2,32,128]{4,3,2,1,0:T(8,128)(2,1)S(1)}) custom-call(f32[5,32]{1,0:T(8,128)S(1)} %stack.2.near, bf16[32,32,1024]{2,1,0:T(8,128)(2,1)S(1)} %bitcast.31, f32[5,32]{1,0:T(8,128)S(1)} %collective-permute-done.far, bf16[32,32,1024]{2,1,0:T(8,128)(2,1)S(1)} %collective-permute-done.1.far_views), custom_call_target="tpu_custom_call" | custom-call | flops 5000000000 | bytes 1000000 | tf_op jit(solution)/shard_map/pallas_call | solution.py:105
  30.8 4.1 %collective-permute-start.3 = (bf16[2,16,2,32,128]{4,3,2,1,0:T(8,128)(2,1)S(1)}, bf16[2,16,2,32,128]{4,3,2,1,0:T(8,128)(2,1)S(1)}, u32[]{:S(2)}, u32[]{:S(2)}) collective-permute-start(bf16[2,16,2,32,128]{4,3,2,1,0:T(8,128)(2,1)S(1)} %add_convert_fusion.4), channel_id=1, source_target_pairs={{0,64},{32,480},{64,128},{96,32},{128,192},{160,96},{192,256},{224... | collective-permute-start | bytes 1572872 | tf_op jit(solution)/shard_map/ppermute | solution.py:190
  34.8 3.9 %shard_map.81 = (bf16[2,16,2,32,128]{4,3,2,1,0:T(8,128)(2,1)S(1)}, bf16[2,16,2,32,128]{4,3,2,1,0:T(8,128)(2,1)S(1)}) custom-call(f32[5,32]{1,0:T(8,128)S(1)} %stack.2.near, bf16[32,32,1024]{2,1,0:T(8,128)(2,1)S(1)} %bitcast.32, f32[5,32]{1,0:T(8,128)S(1)} %collective-permute-done.far, bf16[32,32,1024]{2,1,0:T(8,128)(2,1)S(1)} %collective-permute-done.1.far_views), custom_call_target="tpu_custom_call" | custom-call | flops 5000000000 | bytes 1000000 | tf_op jit(solution)/shard_map/pallas_call | solution.py:105
  39.0 4.9 %collective-permute-start.7 = (bf16[2,16,2,32,128]{4,3,2,1,0:T(8,128)(2,1)S(1)}, bf16[2,16,2,32,128]{4,3,2,1,0:T(8,128)(2,1)S(1)}, u32[]{:S(2)}, u32[]{:S(2)}) collective-permute-start(bf16[2,16,2,32,128]{4,3,2,1,0:T(8,128)(2,1)S(1)} %add_convert_fusion.2), channel_id=1, source_target_pairs={{0,64},{32,480},{64,128},{96,32},{128,192},{160,96},{192,256},{224... | collective-permute-start | bytes 1572872 | tf_op jit(solution)/shard_map/ppermute | solution.py:194
  43.9 1.6 %copy-done.5 = bf16[32,32,1024]{2,1,0:T(8,128)(2,1)S(1)} copy-done((bf16[32,32,1024]{2,1,0:T(8,128)(2,1)S(1)}, bf16[32,32,1024]{2,1,0:T(8,128)(2,1)}, u32[]{:S(2)}) %copy-start.5) | copy-done | bytes 2097176
  45.5 2.7 %shard_map.80 = (bf16[1,16,2,32,128]{4,3,2,1,0:T(8,128)(2,1)S(1)}, bf16[1,16,2,32,128]{4,3,2,1,0:T(8,128)(2,1)S(1)}) custom-call(f32[5,32]{1,0:T(8,128)S(1)} %stack.2.near, bf16[32,32,1024]{2,1,0:T(8,128)(2,1)S(1)} %bitcast.33, f32[5,32]{1,0:T(8,128)S(1)} %collective-permute-done.far, bf16[32,32,1024]{2,1,0:T(8,128)(2,1)S(1)} %copy-done.5), custom_call_target="tpu_custom_call" | custom-call | flops 5000000000 | bytes 1000000 | tf_op jit(solution)/shard_map/pallas_call | solution.py:105
  48.3 3.4 %collective-permute-start.4 = (bf16[2,16,2,32,128]{4,3,2,1,0:T(8,128)(2,1)S(1)}, bf16[2,16,2,32,128]{4,3,2,1,0:T(8,128)(2,1)S(1)}, u32[]{:S(2)}, u32[]{:S(2)}) collective-permute-start(bf16[2,16,2,32,128]{4,3,2,1,0:T(8,128)(2,1)S(1)} %add_convert_fusion.3), channel_id=1, source_target_pairs={{0,64},{32,480},{64,128},{96,32},{128,192},{160,96},{192,256},{224... | collective-permute-start | bytes 1572872 | tf_op jit(solution)/shard_map/ppermute | solution.py:197
  51.7 1.7 %convolution_bitcast_fusion.spec_proj = f32[256,1024]{1,0:T(8,128)} fusion(bf16[256,1024]{1,0:T(8,128)(2,1)S(1)} %bitcast.27, bf16[1024,1024]{1,0:T(8,128)(2,1)S(1)} %copy-done.1), kind=kOutput, calls=%fused_computation | convolution fusion | flops 536870912 | bytes 3670016 | tf_op jit(solution)/shard_map/dot_general | solution.py:181
  54.4 4.8 %collective-permute-start.9 = (bf16[16,2,32,128]{3,2,1,0:T(8,128)(2,1)}, bf16[16,2,32,128]{3,2,1,0:T(8,128)(2,1)}, u32[]{:S(2)}, u32[]{:S(2)}) collective-permute-start(bf16[16,2,32,128]{3,2,1,0:T(8,128)(2,1)} %get-tuple-element.51), channel_id=1, source_target_pairs={{0,64},{32,480},{64,128},{96,32},{128,192},{160,96},{192,256},{224... | collective-permute-start | bytes 786440 | tf_op jit(solution)/shard_map/ppermute | solution.py:199
  59.3 1.4 %collective-permute-done.4 = bf16[2,16,2,32,128]{4,3,2,1,0:T(8,128)(2,1)S(1)} collective-permute-done((bf16[2,16,2,32,128]{4,3,2,1,0:T(8,128)(2,1)S(1)}, bf16[2,16,2,32,128]{4,3,2,1,0:T(8,128)(2,1)S(1)}, u32[]{:S(2)}, u32[]{:S(2)}) %collective-permute-start.4) | collective-permute-done | bytes 524320 | tf_op jit(solution)/shard_map/ppermute | solution.py:197
  61.6 1.9 %collective-permute-start.10 = (bf16[16,2,32,128]{3,2,1,0:T(8,128)(2,1)}, bf16[16,2,32,128]{3,2,1,0:T(8,128)(2,1)}, u32[]{:S(2)}, u32[]{:S(2)}) collective-permute-start(bf16[16,2,32,128]{3,2,1,0:T(8,128)(2,1)} %get-tuple-element.49), channel_id=1, source_target_pairs={{0,96},{32,448},{64,160},{96,0},{128,224},{160,64},{192,288},{224,... | collective-permute-start | bytes 786440 | tf_op jit(solution)/shard_map/ppermute | solution.py:201
  63.6 3.6 %collective-permute-start.8 = (bf16[16,2,32,128]{3,2,1,0:T(8,128)(2,1)S(1)}, bf16[16,2,32,128]{3,2,1,0:T(8,128)(2,1)}, u32[]{:S(2)}, u32[]{:S(2)}) collective-permute-start(bf16[16,2,32,128]{3,2,1,0:T(8,128)(2,1)S(1)} %get-tuple-element.50), channel_id=1, source_target_pairs={{0,96},{32,448},{64,160},{96,0},{128,224},{160,64},{192,288},{224,... | collective-permute-start | bytes 786440 | tf_op jit(solution)/shard_map/ppermute | solution.py:199
  67.2 2.6 %collective-permute-start.6 = (bf16[16,2,32,128]{3,2,1,0:T(8,128)(2,1)}, bf16[16,2,32,128]{3,2,1,0:T(8,128)(2,1)}, u32[]{:S(2)}, u32[]{:S(2)}) collective-permute-start(bf16[16,2,32,128]{3,2,1,0:T(8,128)(2,1)} %get-tuple-element.48), channel_id=1, source_target_pairs={{0,64},{32,480},{64,128},{96,32},{128,192},{160,96},{192,256},{224... | collective-permute-start | bytes 786440 | tf_op jit(solution)/shard_map/ppermute | solution.py:201
  72.4 4.6 %collective-permute-done.6 = bf16[16,2,32,128]{3,2,1,0:T(8,128)(2,1)} collective-permute-done((bf16[16,2,32,128]{3,2,1,0:T(8,128)(2,1)}, bf16[16,2,32,128]{3,2,1,0:T(8,128)(2,1)}, u32[]{:S(2)}, u32[]{:S(2)}) %collective-permute-start.6) | collective-permute-done | bytes 262176 | tf_op jit(solution)/shard_map/ppermute | solution.py:201
  78.2 26.2 %all_to_all.10.got = bf16[32,2,32,128]{3,2,1,0:T(8,128)(2,1)S(1)} all-to-all(bf16[32,2,32,128]{3,2,1,0:T(8,128)(2,1)S(1)} %maximum_select_fusion), channel_id=1, replica_groups=mesh['grp'=16,'ang'=32] {'ang'}, dimensions={0} | all-to-all | bytes 1048576 | tf_op jit(solution)/shard_map/all_to_all | solution.py:208
  104.5 1.4 %shard_map.82 = (bf16[1,2,128,1024]{3,2,1,0:T(8,128)(2,1)}, f32[32,8,128]{2,1,0:T(8,128)S(1)}) custom-call(bf16[32,2,32,128]{3,2,1,0:T(8,128)(2,1)S(1)} %all_to_all.10.got, bf16[1024,1024]{1,0:T(8,128)(2,1)S(1)} %copy-done.1, f32[256,1024]{1,0:T(8,128)S(1)} %copy-done.2), custom_call_target="tpu_custom_call" | custom-call | flops 1000000000 | bytes 1000000 | tf_op jit(solution)/shard_map/pallas_call | solution.py:145
  105.9 14.3 %all_to_all.11 = f32[32,8,128]{2,1,0:T(8,128)S(1)} all-to-all(f32[32,8,128]{2,1,0:T(8,128)S(1)} %get-tuple-element.45), channel_id=1, replica_groups=mesh['grp'=16,'ang'=32] {'ang'}, dimensions={0} | all-to-all | bytes 262144 | tf_op jit(solution)/shard_map/all_to_all | solution.py:210
  (35 shorter events, 10.3 us)
Async XLA Ops:
  0.6 51.1 %copy-start = (bf16[1,2,128,1024]{3,2,1,0:T(8,128)(2,1)S(1)}, bf16[1,2,128,1024]{3,2,1,0:T(8,128)(2,1)}, u32[]{:S(2)}) copy-start(bf16[1,2,128,1024]{3,2,1,0:T(8,128)(2,1)} %param.10) | copy-start | bytes 1572868
  0.6 7.7 %collective-permute-start.1 = (bf16[32,32,1024]{2,1,0:T(8,128)(2,1)}, bf16[32,32,1024]{2,1,0:T(8,128)(2,1)S(1)}, u32[]{:S(2)}, u32[]{:S(2)}) collective-permute-start(bf16[32,32,1024]{2,1,0:T(8,128)(2,1)} %bitcast.28), channel_id=1, source_target_pairs={{0,32},{32,0},{64,96},{96,64},{128,160},{160,128},{192,224},{224,1... | collective-permute-start | bytes 6291464 | tf_op jit(solution)/shard_map/ppermute | solution.py:169
  5.1 3.2 %collective-permute-start = (f32[5,32]{1,0:T(8,128)S(1)}, f32[5,32]{1,0:T(8,128)S(1)}, u32[]{:S(2)}, u32[]{:S(2)}) collective-permute-start(f32[5,32]{1,0:T(8,128)S(1)} %stack.2.near), channel_id=1, source_target_pairs={{0,32},{32,0},{64,96},{96,64},{128,160},{160,128},{192,224},{224,1... | collective-permute-start | bytes 1928 | tf_op jit(solution)/shard_map/ppermute | solution.py:175
  8.3 1.6 %copy-start.3 = (bf16[1,32,32,1024]{3,2,1,0:T(8,128)(2,1)S(1)}, bf16[1,32,32,1024]{3,2,1,0:T(8,128)(2,1)}, u32[]{:S(2)}) copy-start(bf16[1,32,32,1024]{3,2,1,0:T(8,128)(2,1)} %param.6) | copy-start | bytes 6291460
  9.9 24.9 %copy-start.4 = (bf16[32,32,1024]{2,1,0:T(8,128)(2,1)}, bf16[32,32,1024]{2,1,0:T(8,128)(2,1)S(1)}, u32[]{:S(2)}) copy-start(bf16[32,32,1024]{2,1,0:T(8,128)(2,1)S(1)} %collective-permute-done.1.far_views) | copy-start | bytes 6291460
  14.0 16.6 %collective-permute-start.2 = (bf16[2,16,2,32,128]{4,3,2,1,0:T(8,128)(2,1)S(1)}, bf16[2,16,2,32,128]{4,3,2,1,0:T(8,128)(2,1)S(1)}, u32[]{:S(2)}, u32[]{:S(2)}) collective-permute-start(bf16[2,16,2,32,128]{4,3,2,1,0:T(8,128)(2,1)S(1)} %shard_map.77), channel_id=1, source_target_pairs={{0,64},{32,480},{64,128},{96,32},{128,192},{160,96},{192,256},{224... | collective-permute-start | bytes 1572872 | tf_op jit(solution)/shard_map/ppermute | solution.py:185
  22.2 16.6 %collective-permute-start.5 = (bf16[2,16,2,32,128]{4,3,2,1,0:T(8,128)(2,1)S(1)}, bf16[2,16,2,32,128]{4,3,2,1,0:T(8,128)(2,1)S(1)}, u32[]{:S(2)}, u32[]{:S(2)}) collective-permute-start(bf16[2,16,2,32,128]{4,3,2,1,0:T(8,128)(2,1)S(1)} %get-tuple-element.33), channel_id=1, source_target_pairs={{0,64},{32,480},{64,128},{96,32},{128,192},{160,96},{192,256},{224... | collective-permute-start | bytes 1572872 | tf_op jit(solution)/shard_map/ppermute | solution.py:187
  30.8 17.3 %collective-permute-start.3 = (bf16[2,16,2,32,128]{4,3,2,1,0:T(8,128)(2,1)S(1)}, bf16[2,16,2,32,128]{4,3,2,1,0:T(8,128)(2,1)S(1)}, u32[]{:S(2)}, u32[]{:S(2)}) collective-permute-start(bf16[2,16,2,32,128]{4,3,2,1,0:T(8,128)(2,1)S(1)} %add_convert_fusion.4), channel_id=1, source_target_pairs={{0,64},{32,480},{64,128},{96,32},{128,192},{160,96},{192,256},{224... | collective-permute-start | bytes 1572872 | tf_op jit(solution)/shard_map/ppermute | solution.py:190
  39.0 12.8 %copy-start.1 = (bf16[1024,1024]{1,0:T(8,128)(2,1)S(1)}, bf16[1024,1024]{1,0:T(8,128)(2,1)}, u32[]{:S(2)}) copy-start(bf16[1024,1024]{1,0:T(8,128)(2,1)} %constant.45.clone.basis) | copy-start | bytes 6291460
  39.0 14.5 %collective-permute-start.7 = (bf16[2,16,2,32,128]{4,3,2,1,0:T(8,128)(2,1)S(1)}, bf16[2,16,2,32,128]{4,3,2,1,0:T(8,128)(2,1)S(1)}, u32[]{:S(2)}, u32[]{:S(2)}) collective-permute-start(bf16[2,16,2,32,128]{4,3,2,1,0:T(8,128)(2,1)S(1)} %add_convert_fusion.2), channel_id=1, source_target_pairs={{0,64},{32,480},{64,128},{96,32},{128,192},{160,96},{192,256},{224... | collective-permute-start | bytes 1572872 | tf_op jit(solution)/shard_map/ppermute | solution.py:194
  43.9 1.6 %copy-start.5 = (bf16[32,32,1024]{2,1,0:T(8,128)(2,1)S(1)}, bf16[32,32,1024]{2,1,0:T(8,128)(2,1)}, u32[]{:S(2)}) copy-start(bf16[32,32,1024]{2,1,0:T(8,128)(2,1)} %copy-done.4) | copy-start | bytes 6291460
  48.3 12.3 %collective-permute-start.4 = (bf16[2,16,2,32,128]{4,3,2,1,0:T(8,128)(2,1)S(1)}, bf16[2,16,2,32,128]{4,3,2,1,0:T(8,128)(2,1)S(1)}, u32[]{:S(2)}, u32[]{:S(2)}) collective-permute-start(bf16[2,16,2,32,128]{4,3,2,1,0:T(8,128)(2,1)S(1)} %add_convert_fusion.3), channel_id=1, source_target_pairs={{0,64},{32,480},{64,128},{96,32},{128,192},{160,96},{192,256},{224... | collective-permute-start | bytes 1572872 | tf_op jit(solution)/shard_map/ppermute | solution.py:197
  54.4 15.5 %collective-permute-start.9 = (bf16[16,2,32,128]{3,2,1,0:T(8,128)(2,1)}, bf16[16,2,32,128]{3,2,1,0:T(8,128)(2,1)}, u32[]{:S(2)}, u32[]{:S(2)}) collective-permute-start(bf16[16,2,32,128]{3,2,1,0:T(8,128)(2,1)} %get-tuple-element.51), channel_id=1, source_target_pairs={{0,64},{32,480},{64,128},{96,32},{128,192},{160,96},{192,256},{224... | collective-permute-start | bytes 786440 | tf_op jit(solution)/shard_map/ppermute | solution.py:199
  61.6 8.2 %collective-permute-start.10 = (bf16[16,2,32,128]{3,2,1,0:T(8,128)(2,1)}, bf16[16,2,32,128]{3,2,1,0:T(8,128)(2,1)}, u32[]{:S(2)}, u32[]{:S(2)}) collective-permute-start(bf16[16,2,32,128]{3,2,1,0:T(8,128)(2,1)} %get-tuple-element.49), channel_id=1, source_target_pairs={{0,96},{32,448},{64,160},{96,0},{128,224},{160,64},{192,288},{224,... | collective-permute-start | bytes 786440 | tf_op jit(solution)/shard_map/ppermute | solution.py:201
  63.6 8.9 %collective-permute-start.8 = (bf16[16,2,32,128]{3,2,1,0:T(8,128)(2,1)S(1)}, bf16[16,2,32,128]{3,2,1,0:T(8,128)(2,1)}, u32[]{:S(2)}, u32[]{:S(2)}) collective-permute-start(bf16[16,2,32,128]{3,2,1,0:T(8,128)(2,1)S(1)} %get-tuple-element.50), channel_id=1, source_target_pairs={{0,96},{32,448},{64,160},{96,0},{128,224},{160,64},{192,288},{224,... | collective-permute-start | bytes 786440 | tf_op jit(solution)/shard_map/ppermute | solution.py:199
  67.2 9.8 %collective-permute-start.6 = (bf16[16,2,32,128]{3,2,1,0:T(8,128)(2,1)}, bf16[16,2,32,128]{3,2,1,0:T(8,128)(2,1)}, u32[]{:S(2)}, u32[]{:S(2)}) collective-permute-start(bf16[16,2,32,128]{3,2,1,0:T(8,128)(2,1)} %get-tuple-element.48), channel_id=1, source_target_pairs={{0,64},{32,480},{64,128},{96,32},{128,192},{160,96},{192,256},{224... | collective-permute-start | bytes 786440 | tf_op jit(solution)/shard_map/ppermute | solution.py:201
  69.9 34.6 %copy-start.2 = (f32[256,1024]{1,0:T(8,128)S(1)}, f32[256,1024]{1,0:T(8,128)}, u32[]{:S(2)}) copy-start(f32[256,1024]{1,0:T(8,128)} %convolution_bitcast_fusion.spec_proj) | copy-start | bytes 3145732

commit v5 on v4

--- a/solution.py
+++ b/solution.py
@@ -25,6 +25,26 @@
     freq_idx = np.arange(columns // 2, dtype=np.int64)[None, :]
     phases = ((column_idx * freq_idx) % columns).astype(np.float64) * (2.0 * math.pi / columns)
     return np.concatenate([np.cos(phases), np.sin(phases)], axis=1).astype(jnp.bfloat16)
+
+
+def describe_kernel(lists, row_shift, stretch, place, meta):
+    count = jnp.sum((lists[...] >= 0).astype(jnp.float32), axis=0, keepdims=True)
+    lane = lax.broadcasted_iota(jnp.int32, count.shape, 1)
+    meta[0:1] = lists[0:1].astype(jnp.float32)
+    meta[1:2] = count
+    meta[2:3] = row_shift[...]
+    meta[3:4] = 1.0 / (TR * count * stretch[...] / SZ)
+    meta[4:5] = jnp.where(lane == 0, place[0], place[1]).astype(jnp.float32)
+
+
+def describe(lists, row_shift, stretch, place):
+    vmem = pl.BlockSpec(memory_space=pltpu.VMEM)
+    return pl.pallas_call(
+        describe_kernel,
+        out_shape=jax.ShapeDtypeStruct((5, lists.shape[1]), jnp.float32),
+        in_specs=[vmem, vmem, vmem, pl.BlockSpec(memory_space=pltpu.SMEM)],
+        out_specs=vmem,
+    )(lists, row_shift, stretch, place)
 
 
 def unit_kernel(hop, lanes, chips, near, near_views, far, far_views, *refs):
@@ -167,14 +187,8 @@
     onward = [(i, (i + (2 if i % 2 == 0 else -2)) % n_grp) for i in range(n_grp)]
 
     sibling_views = lax.ppermute(views, "grp", swap)
-    lists = footprint[0]
-    count = sum((lists[:, k] >= 0).astype(jnp.float32) for k in range(KF))
-    magnify = TR * count * stretch[0] / SZ
-    place = jnp.where(jnp.arange(angles) == 0, chip, core).astype(jnp.float32)
-    meta = jnp.stack([lists[:, 0].astype(jnp.float32), count, row_shift[0], 1.0 / magnify, place])
+    meta = describe(footprint[0].T, row_shift, stretch, jnp.stack([chip, core]))
     known = (chips, meta, views, lax.ppermute(meta, "grp", swap), sibling_views)
-
-    across = [(i, j ^ 1) for i, j in onward]
 
     n_freq = n_ang * views.shape[1] // 2
     basis = jnp.asarray(dft_basis(2 * n_freq))
@@ -185,23 +199,21 @@
     first = lax.ppermute(units(0, 1, 2, *known)[0], "grp", onward)
     mine = units(1, 2, 2, *known)
     second = lax.ppermute(mine[1], "grp", onward)
-    later = units(2, 2, 2, *known)
-    sending, later, meta = lax.optimization_barrier((add(first, mine[0]), later, meta))
+    kept = units(4, 2, 1, *known)
+    sending, kept, meta = lax.optimization_barrier((add(first, mine[0]), kept, meta))
+    known = known[:1] + (meta,) + known[2:]
     first = lax.ppermute(sending, "grp", onward)
-    known = known[:1] + (meta,) + known[2:]
-    last = units(3, 2, 2, *known)
-    sending, last = lax.optimization_barrier((add(second, later[1]), last))
-    second = lax.ppermute(sending, "grp", onward)
-    kept = units(4, 2, 1, *known)
-    sending, kept = lax.optimization_barrier((add(first, later[0]), kept))
-    first = lax.ppermute(sending, "grp", onward)
-    sending, spec_proj = lax.optimization_barrier((add(second, last[1]), spec_proj))
-    second = [lax.ppermute(sending[lane], "grp", (onward, across)[lane]) for lane in range(2)]
-    sending = add(first, last[0])
-    first = [lax.ppermute(sending[lane], "grp", (onward, across)[lane]) for lane in range(2)]
+    mine = units(2, 2, 2, *known)
+    second = lax.ppermute(add(second, mine[1]), "grp", onward)
+    first = lax.ppermute(add(first, mine[0]), "grp", onward)
+    mine = units(3, 2, 2, *known)
+    second = lax.ppermute(add(second, mine[1]), "grp", onward)
+    first = lax.ppermute(add(first, mine[0]), "grp", onward)
+    leaving, spec_proj = lax.optimization_barrier((jnp.stack([second[1], first[1]]), spec_proj))
+    from_sibling = lax.ppermute(leaving, "grp", swap)
     ready = (
-        add(first[0], second[1], kept[0][0]),
-        add(second[0], first[1], kept[1][0]),
+        add(first[0], from_sibling[0], kept[0][0]),
+        add(second[0], from_sibling[1], kept[1][0]),
     )
     summed = jnp.where(core == 0, jnp.concatenate(ready), jnp.concatenate(ready[::-1]))
 

time: 122 us -> 123 us (level)
  waiting for transfers between devices: 8.29 us -> 14.5 us
  starting transfers between devices: 36.2 us -> 32.9 us
  local copies, waits for them, and re-layouts: 5.45 us -> 2.42 us
  blocking collectives: 40.5 us -> 42.2 us
    ppermute x2 -> x1, starting transfers between devices: 7.44 us -> 1.92 us  [body(): first = lax.ppermute(sending, 'grp', onward)]
    ppermute x5, waiting for transfers between devices: 5.88 us -> 10.6 us  [the longest x2 6.81 us: body(): first = lax.ppermute(add(first, mine[0]), 'grp', onward)]
    ppermute x1, waiting for transfers between devices: 0.24 us -> 2.93 us  [body(): first = lax.ppermute(units(0, 1, 2, *known)[0], 'grp', onward)]
    all_to_all x1, blocking collectives: 26.2 us -> 27.9 us  [body(): got = lax.all_to_all(summed, 'ang', split_axis=0, concat_axis=0, tiled=True)]
    squeeze x2 -> x0, local copies, waits for them, and re-layouts: 1.57 us -> none  [body(): sending[lane]]
    another operation x0 -> x2, other arithmetic: none -> 1.5 us  [the longest x1 0.91 us: body(): jnp.stack([second[1], first[1]])]
    pallas_call x0 -> x1, Pallas kernels: none -> 1.41 us  [describe(): pl.pallas_call(describe_kernel, out_shape=jax.ShapeDtypeStruct((5, lists....]
    ppermute x2 -> x1, waiting for transfers between devices: 1.36 us -> 0.01 us  [body(): first = lax.ppermute(sending, 'grp', onward)]
  transfers between devices with their start and end apart: 11 -> 10, of which waited for: 5 -> 6; matrix products, arithmetic and copies ran while one was open for 6% -> 3% of each run, Pallas kernels for 14% -> 15%
where the time goes in v5:
time: 123 us; the launch traced here: 122 us
  blocking collectives  42.2 us (34%)
  starting transfers between devices  32.9 us (27%)
  Pallas kernels  22.7 us (18%)
  waiting for transfers between devices  14.5 us (12%)
  other arithmetic  4.58 us (4%)
  local copies, waits for them, and re-layouts  2.42 us (2%)
  matrix products  1.71 us (1%)
    all_to_all x1, blocking collectives, body(): got = lax.all_to_all(summed, 'ang', split_axis=0, concat_axis=0, tiled=True)  27.9 us
    pallas_call x5, Pallas kernels, units(): pl.pallas_call(functools.partial(unit_kernel, hop, lanes, chips), out_sha...  19.9 us
    all_to_all x1, blocking collectives, body(): lax.all_to_all(copies, 'ang', split_axis=0, concat_axis=0, tiled=True)  14.3 us
    ppermute x2, starting transfers between devices, body(): second = lax.ppermute(add(second, mine[1]), 'grp', onward)  9.89 us
    ppermute x2, starting transfers between devices, body(): first = lax.ppermute(add(first, mine[0]), 'grp', onward)  6.87 us
    ppermute x2, waiting for transfers between devices, body(): first = lax.ppermute(add(first, mine[0]), 'grp', onward)  6.81 us
    ppermute x1, starting transfers between devices, body(): second = lax.ppermute(mine[1], 'grp', onward)  4.28 us
    ppermute x1, starting transfers between devices, body(): first = lax.ppermute(units(0, 1, 2, *known)[0], 'grp', onward)  3.55 us
  transfers between devices with their start and end apart: 10, of which 6 were waited for; matrix products, arithmetic and copies ran while one was open for 3% of the time, Pallas kernels for 15%

profile of v5, /device:TPU:8, one launch (start us, length us, event | category | flops | bytes accessed | tf_op | source)
XLA Modules:
  0.0 121.9 jit_solution(9281695638126738365)
XLA Ops:
  0.6 2.1 %collective-permute-start.1 = (bf16[32,32,1024]{2,1,0:T(8,128)(2,1)}, bf16[32,32,1024]{2,1,0:T(8,128)(2,1)S(1)}, u32[]{:S(2)}, u32[]{:S(2)}) collective-permute-start(bf16[32,32,1024]{2,1,0:T(8,128)(2,1)} %bitcast.17), channel_id=1, source_target_pairs={{0,32},{32,0},{64,96},{96,64},{128,160},{160,128},{192,224},{224,1... | collective-permute-start | bytes 6291464 | tf_op jit(solution)/shard_map/ppermute | solution.py:189
  4.7 2.4 %collective-permute-start = (f32[5,32]{1,0:T(8,128)}, f32[5,32]{1,0:T(8,128)S(1)}, u32[]{:S(2)}, u32[]{:S(2)}) collective-permute-start(f32[5,32]{1,0:T(8,128)} %shard_map.77.near), channel_id=1, source_target_pairs={{0,32},{32,0},{64,96},{96,64},{128,160},{160,128},{192,224},{224,1... | collective-permute-start | bytes 1928 | tf_op jit(solution)/shard_map/ppermute | solution.py:191
  8.8 1.6 %copy-done.5 = bf16[1,32,32,1024]{3,2,1,0:T(8,128)(2,1)S(1)} copy-done((bf16[1,32,32,1024]{3,2,1,0:T(8,128)(2,1)S(1)}, bf16[1,32,32,1024]{3,2,1,0:T(8,128)(2,1)}, u32[]{:S(2)}) %copy-start.5) | copy-done | bytes 2097176
  10.4 3.3 %shard_map.78 = bf16[2,16,2,32,128]{4,3,2,1,0:T(8,128)(2,1)S(1)} custom-call(f32[5,32]{1,0:T(8,128)S(1)} %copy-done.3, bf16[32,32,1024]{2,1,0:T(8,128)(2,1)S(1)} %bitcast.18, f32[5,32]{1,0:T(8,128)S(1)} %collective-permute-done.far, bf16[32,32,1024]{2,1,0:T(8,128)(2,1)S(1)} %collective-permute-done.1.far_views), custom_call_target="tpu_custom_call" | custom-call | flops 2500000000 | bytes 1000000 | tf_op jit(solution)/shard_map/pallas_call | solution.py:125
  13.7 3.6 %collective-permute-start.2 = (bf16[2,16,2,32,128]{4,3,2,1,0:T(8,128)(2,1)S(1)}, bf16[2,16,2,32,128]{4,3,2,1,0:T(8,128)(2,1)S(1)}, u32[]{:S(2)}, u32[]{:S(2)}) collective-permute-start(bf16[2,16,2,32,128]{4,3,2,1,0:T(8,128)(2,1)S(1)} %shard_map.78), channel_id=1, source_target_pairs={{0,64},{32,480},{64,128},{96,32},{128,192},{160,96},{192,256},{224... | collective-permute-start | bytes 1572872 | tf_op jit(solution)/shard_map/ppermute | solution.py:199
  17.3 4.6 %shard_map.79 = (bf16[2,16,2,32,128]{4,3,2,1,0:T(8,128)(2,1)S(1)}, bf16[2,16,2,32,128]{4,3,2,1,0:T(8,128)(2,1)S(1)}) custom-call(f32[5,32]{1,0:T(8,128)S(1)} %copy-done.4, bf16[32,32,1024]{2,1,0:T(8,128)(2,1)S(1)} %bitcast.19, f32[5,32]{1,0:T(8,128)S(1)} %collective-permute-done.far, bf16[32,32,1024]{2,1,0:T(8,128)(2,1)S(1)} %collective-permute-done.1.far_views), custom_call_target="tpu_custom_call" | custom-call | flops 5000000000 | bytes 1000000 | tf_op jit(solution)/shard_map/pallas_call | solution.py:125
  22.0 4.3 %collective-permute-start.6 = (bf16[2,16,2,32,128]{4,3,2,1,0:T(8,128)(2,1)S(1)}, bf16[2,16,2,32,128]{4,3,2,1,0:T(8,128)(2,1)S(1)}, u32[]{:S(2)}, u32[]{:S(2)}) collective-permute-start(bf16[2,16,2,32,128]{4,3,2,1,0:T(8,128)(2,1)S(1)} %get-tuple-element.25), channel_id=1, source_target_pairs={{0,64},{32,480},{64,128},{96,32},{128,192},{160,96},{192,256},{224... | collective-permute-start | bytes 1572872 | tf_op jit(solution)/shard_map/ppermute | solution.py:201
  26.2 2.7 %shard_map.80 = (bf16[1,16,2,32,128]{4,3,2,1,0:T(8,128)(2,1)S(1)}, bf16[1,16,2,32,128]{4,3,2,1,0:T(8,128)(2,1)S(1)}) custom-call(f32[5,32]{1,0:T(8,128)S(1)} %copy-done.4, bf16[32,32,1024]{2,1,0:T(8,128)(2,1)S(1)} %bitcast.20, f32[5,32]{1,0:T(8,128)S(1)} %collective-permute-done.far, bf16[32,32,1024]{2,1,0:T(8,128)(2,1)S(1)} %collective-permute-done.1.far_views), custom_call_target="tpu_custom_call" | custom-call | flops 5000000000 | bytes 1000000 | tf_op jit(solution)/shard_map/pallas_call | solution.py:125
  28.9 2.9 %collective-permute-done.2 = bf16[2,16,2,32,128]{4,3,2,1,0:T(8,128)(2,1)S(1)} collective-permute-done((bf16[2,16,2,32,128]{4,3,2,1,0:T(8,128)(2,1)S(1)}, bf16[2,16,2,32,128]{4,3,2,1,0:T(8,128)(2,1)S(1)}, u32[]{:S(2)}, u32[]{:S(2)}) %collective-permute-start.2) | collective-permute-done | bytes 524320 | tf_op jit(solution)/shard_map/ppermute | solution.py:199
  32.0 1.9 %collective-permute-start.3 = (bf16[2,16,2,32,128]{4,3,2,1,0:T(8,128)(2,1)S(1)}, bf16[2,16,2,32,128]{4,3,2,1,0:T(8,128)(2,1)S(1)}, u32[]{:S(2)}, u32[]{:S(2)}) collective-permute-start(bf16[2,16,2,32,128]{4,3,2,1,0:T(8,128)(2,1)S(1)} %add_convert_fusion.4), channel_id=1, source_target_pairs={{0,64},{32,480},{64,128},{96,32},{128,192},{160,96},{192,256},{224... | collective-permute-start | bytes 1572872 | tf_op jit(solution)/shard_map/ppermute | solution.py:205
  34.0 4.6 %shard_map.81 = (bf16[2,16,2,32,128]{4,3,2,1,0:T(8,128)(2,1)S(1)}, bf16[2,16,2,32,128]{4,3,2,1,0:T(8,128)(2,1)S(1)}) custom-call(f32[5,32]{1,0:T(8,128)S(1)} %copy-done.4, bf16[32,32,1024]{2,1,0:T(8,128)(2,1)S(1)} %bitcast.21, f32[5,32]{1,0:T(8,128)S(1)} %collective-permute-done.far, bf16[32,32,1024]{2,1,0:T(8,128)(2,1)S(1)} %collective-permute-done.1.far_views), custom_call_target="tpu_custom_call" | custom-call | flops 5000000000 | bytes 1000000 | tf_op jit(solution)/shard_map/pallas_call | solution.py:125
  38.8 6.4 %collective-permute-start.7 = (bf16[2,16,2,32,128]{4,3,2,1,0:T(8,128)(2,1)S(1)}, bf16[2,16,2,32,128]{4,3,2,1,0:T(8,128)(2,1)S(1)}, u32[]{:S(2)}, u32[]{:S(2)}) collective-permute-start(bf16[2,16,2,32,128]{4,3,2,1,0:T(8,128)(2,1)S(1)} %add_convert_fusion.1), channel_id=1, source_target_pairs={{0,64},{32,480},{64,128},{96,32},{128,192},{160,96},{192,256},{224... | collective-permute-start | bytes 1572872 | tf_op jit(solution)/shard_map/ppermute | solution.py:207
  45.4 2.7 %collective-permute-start.4 = (bf16[2,16,2,32,128]{4,3,2,1,0:T(8,128)(2,1)S(1)}, bf16[2,16,2,32,128]{4,3,2,1,0:T(8,128)(2,1)S(1)}, u32[]{:S(2)}, u32[]{:S(2)}) collective-permute-start(bf16[2,16,2,32,128]{4,3,2,1,0:T(8,128)(2,1)S(1)} %add_convert_fusion.3), channel_id=1, source_target_pairs={{0,64},{32,480},{64,128},{96,32},{128,192},{160,96},{192,256},{224... | collective-permute-start | bytes 1572872 | tf_op jit(solution)/shard_map/ppermute | solution.py:208
  48.1 4.6 %shard_map.82 = (bf16[2,16,2,32,128]{4,3,2,1,0:T(8,128)(2,1)S(1)}, bf16[2,16,2,32,128]{4,3,2,1,0:T(8,128)(2,1)S(1)}) custom-call(f32[5,32]{1,0:T(8,128)S(1)} %copy-done.4, bf16[32,32,1024]{2,1,0:T(8,128)(2,1)S(1)} %bitcast.22, f32[5,32]{1,0:T(8,128)S(1)} %collective-permute-done.far, bf16[32,32,1024]{2,1,0:T(8,128)(2,1)S(1)} %collective-permute-done.1.far_views), custom_call_target="tpu_custom_call" | custom-call | flops 5000000000 | bytes 1000000 | tf_op jit(solution)/shard_map/pallas_call | solution.py:125
  52.9 3.5 %collective-permute-start.8 = (bf16[2,16,2,32,128]{4,3,2,1,0:T(8,128)(2,1)S(1)}, bf16[2,16,2,32,128]{4,3,2,1,0:T(8,128)(2,1)S(1)}, u32[]{:S(2)}, u32[]{:S(2)}) collective-permute-start(bf16[2,16,2,32,128]{4,3,2,1,0:T(8,128)(2,1)S(1)} %add_convert_fusion), channel_id=1, source_target_pairs={{0,64},{32,480},{64,128},{96,32},{128,192},{160,96},{192,256},{224... | collective-permute-start | bytes 1572872 | tf_op jit(solution)/shard_map/ppermute | solution.py:210
  57.9 4.2 %collective-permute-start.5 = (bf16[2,16,2,32,128]{4,3,2,1,0:T(8,128)(2,1)S(1)}, bf16[2,16,2,32,128]{4,3,2,1,0:T(8,128)(2,1)S(1)}, u32[]{:S(2)}, u32[]{:S(2)}) collective-permute-start(bf16[2,16,2,32,128]{4,3,2,1,0:T(8,128)(2,1)S(1)} %add_convert_fusion.2), channel_id=1, source_target_pairs={{0,64},{32,480},{64,128},{96,32},{128,192},{160,96},{192,256},{224... | collective-permute-start | bytes 1572872 | tf_op jit(solution)/shard_map/ppermute | solution.py:211
  62.1 1.7 %convolution_bitcast_fusion.spec_proj = f32[256,1024]{1,0:T(8,128)} fusion(bf16[256,1024]{1,0:T(8,128)(2,1)S(1)} %bitcast.16, bf16[1024,1024]{1,0:T(8,128)(2,1)S(1)} %copy-done.1), kind=kOutput, calls=%fused_computation | convolution fusion | flops 536870912 | bytes 3670016 | tf_op jit(solution)/shard_map/dot_general | solution.py:195
  63.8 1.5 %collective-permute-done.8 = bf16[2,16,2,32,128]{4,3,2,1,0:T(8,128)(2,1)S(1)} collective-permute-done((bf16[2,16,2,32,128]{4,3,2,1,0:T(8,128)(2,1)S(1)}, bf16[2,16,2,32,128]{4,3,2,1,0:T(8,128)(2,1)S(1)}, u32[]{:S(2)}, u32[]{:S(2)}) %collective-permute-start.8) | collective-permute-done | bytes 524320 | tf_op jit(solution)/shard_map/ppermute | solution.py:210
  65.4 5.6 %collective-permute-done.5 = bf16[2,16,2,32,128]{4,3,2,1,0:T(8,128)(2,1)S(1)} collective-permute-done((bf16[2,16,2,32,128]{4,3,2,1,0:T(8,128)(2,1)S(1)}, bf16[2,16,2,32,128]{4,3,2,1,0:T(8,128)(2,1)S(1)}, u32[]{:S(2)}, u32[]{:S(2)}) %collective-permute-start.5) | collective-permute-done | bytes 524320 | tf_op jit(solution)/shard_map/ppermute | solution.py:211
  72.0 1.9 %collective-permute-start.9 = (bf16[2,16,2,32,128]{4,3,2,1,0:T(8,128)(2,1)}, bf16[2,16,2,32,128]{4,3,2,1,0:T(8,128)(2,1)}, u32[]{:S(2)}, u32[]{:S(2)}) collective-permute-start(bf16[2,16,2,32,128]{4,3,2,1,0:T(8,128)(2,1)} %pad_maximum_fusion), channel_id=1, source_target_pairs={{0,32},{32,0},{64,96},{96,64},{128,160},{160,128},{192,224},{224,1... | collective-permute-start | bytes 1572872 | tf_op jit(solution)/shard_map/ppermute | solution.py:213
  73.9 2.2 %collective-permute-done.9 = bf16[2,16,2,32,128]{4,3,2,1,0:T(8,128)(2,1)} collective-permute-done((bf16[2,16,2,32,128]{4,3,2,1,0:T(8,128)(2,1)}, bf16[2,16,2,32,128]{4,3,2,1,0:T(8,128)(2,1)}, u32[]{:S(2)}, u32[]{:S(2)}) %collective-permute-start.9) | collective-permute-done | bytes 524320 | tf_op jit(solution)/shard_map/ppermute | solution.py:213
  77.7 27.9 %all_to_all.10.got = bf16[32,2,32,128]{3,2,1,0:T(8,128)(2,1)S(1)} all-to-all(bf16[32,2,32,128]{3,2,1,0:T(8,128)(2,1)S(1)} %maximum_select_fusion), channel_id=1, replica_groups=mesh['grp'=16,'ang'=32] {'ang'}, dimensions={0} | all-to-all | bytes 1048576 | tf_op jit(solution)/shard_map/all_to_all | solution.py:220
  105.6 1.4 %shard_map.83 = (bf16[1,2,128,1024]{3,2,1,0:T(8,128)(2,1)}, f32[32,8,128]{2,1,0:T(8,128)S(1)}) custom-call(bf16[32,2,32,128]{3,2,1,0:T(8,128)(2,1)S(1)} %all_to_all.10.got, bf16[1024,1024]{1,0:T(8,128)(2,1)S(1)} %copy-done.1, f32[256,1024]{1,0:T(8,128)S(1)} %copy-done.2), custom_call_target="tpu_custom_call" | custom-call | flops 1000000000 | bytes 1000000 | tf_op jit(solution)/shard_map/pallas_call | solution.py:165
  107.0 14.3 %all_to_all.11 = f32[32,8,128]{2,1,0:T(8,128)S(1)} all-to-all(f32[32,8,128]{2,1,0:T(8,128)S(1)} %get-tuple-element.33), channel_id=1, replica_groups=mesh['grp'=16,'ang'=32] {'ang'}, dimensions={0} | all-to-all | bytes 262144 | tf_op jit(solution)/shard_map/all_to_all | solution.py:222
  (37 shorter events, 9.1 us)
Async XLA Ops:
  0.6 61.4 %copy-start = (bf16[1,2,128,1024]{3,2,1,0:T(8,128)(2,1)S(1)}, bf16[1,2,128,1024]{3,2,1,0:T(8,128)(2,1)}, u32[]{:S(2)}) copy-start(bf16[1,2,128,1024]{3,2,1,0:T(8,128)(2,1)} %param.10) | copy-start | bytes 1572868
  0.6 7.5 %collective-permute-start.1 = (bf16[32,32,1024]{2,1,0:T(8,128)(2,1)}, bf16[32,32,1024]{2,1,0:T(8,128)(2,1)S(1)}, u32[]{:S(2)}, u32[]{:S(2)}) collective-permute-start(bf16[32,32,1024]{2,1,0:T(8,128)(2,1)} %bitcast.17), channel_id=1, source_target_pairs={{0,32},{32,0},{64,96},{96,64},{128,160},{160,128},{192,224},{224,1... | collective-permute-start | bytes 6291464 | tf_op jit(solution)/shard_map/ppermute | solution.py:189
  4.7 3.4 %collective-permute-start = (f32[5,32]{1,0:T(8,128)}, f32[5,32]{1,0:T(8,128)S(1)}, u32[]{:S(2)}, u32[]{:S(2)}) collective-permute-start(f32[5,32]{1,0:T(8,128)} %shard_map.77.near), channel_id=1, source_target_pairs={{0,32},{32,0},{64,96},{96,64},{128,160},{160,128},{192,224},{224,1... | collective-permute-start | bytes 1928 | tf_op jit(solution)/shard_map/ppermute | solution.py:191
  8.1 0.7 copy-start.3
  8.8 1.6 %copy-start.5 = (bf16[1,32,32,1024]{3,2,1,0:T(8,128)(2,1)S(1)}, bf16[1,32,32,1024]{3,2,1,0:T(8,128)(2,1)}, u32[]{:S(2)}) copy-start(bf16[1,32,32,1024]{3,2,1,0:T(8,128)(2,1)} %param.6) | copy-start | bytes 6291460
  10.4 6.9 %copy-start.4 = (f32[5,32]{1,0:T(8,128)S(1)}, f32[5,32]{1,0:T(8,128)}, u32[]{:S(2)}) copy-start(f32[5,32]{1,0:T(8,128)} %shard_map.77.near) | copy-start | bytes 1924
  10.4 6.9 %copy-start.6 = (bf16[1,32,32,1024]{3,2,1,0:T(8,128)(2,1)S(1)}, bf16[1,32,32,1024]{3,2,1,0:T(8,128)(2,1)}, u32[]{:S(2)}) copy-start(bf16[1,32,32,1024]{3,2,1,0:T(8,128)(2,1)} %param.6) | copy-start | bytes 6291460
  13.7 18.1 %collective-permute-start.2 = (bf16[2,16,2,32,128]{4,3,2,1,0:T(8,128)(2,1)S(1)}, bf16[2,16,2,32,128]{4,3,2,1,0:T(8,128)(2,1)S(1)}, u32[]{:S(2)}, u32[]{:S(2)}) collective-permute-start(bf16[2,16,2,32,128]{4,3,2,1,0:T(8,128)(2,1)S(1)} %shard_map.78), channel_id=1, source_target_pairs={{0,64},{32,480},{64,128},{96,32},{128,192},{160,96},{192,256},{224... | collective-permute-start | bytes 1572872 | tf_op jit(solution)/shard_map/ppermute | solution.py:199
  22.0 16.6 %collective-permute-start.6 = (bf16[2,16,2,32,128]{4,3,2,1,0:T(8,128)(2,1)S(1)}, bf16[2,16,2,32,128]{4,3,2,1,0:T(8,128)(2,1)S(1)}, u32[]{:S(2)}, u32[]{:S(2)}) collective-permute-start(bf16[2,16,2,32,128]{4,3,2,1,0:T(8,128)(2,1)S(1)} %get-tuple-element.25), channel_id=1, source_target_pairs={{0,64},{32,480},{64,128},{96,32},{128,192},{160,96},{192,256},{224... | collective-permute-start | bytes 1572872 | tf_op jit(solution)/shard_map/ppermute | solution.py:201
  32.0 13.2 %collective-permute-start.3 = (bf16[2,16,2,32,128]{4,3,2,1,0:T(8,128)(2,1)S(1)}, bf16[2,16,2,32,128]{4,3,2,1,0:T(8,128)(2,1)S(1)}, u32[]{:S(2)}, u32[]{:S(2)}) collective-permute-start(bf16[2,16,2,32,128]{4,3,2,1,0:T(8,128)(2,1)S(1)} %add_convert_fusion.4), channel_id=1, source_target_pairs={{0,64},{32,480},{64,128},{96,32},{128,192},{160,96},{192,256},{224... | collective-permute-start | bytes 1572872 | tf_op jit(solution)/shard_map/ppermute | solution.py:205
  38.8 13.9 %collective-permute-start.7 = (bf16[2,16,2,32,128]{4,3,2,1,0:T(8,128)(2,1)S(1)}, bf16[2,16,2,32,128]{4,3,2,1,0:T(8,128)(2,1)S(1)}, u32[]{:S(2)}, u32[]{:S(2)}) collective-permute-start(bf16[2,16,2,32,128]{4,3,2,1,0:T(8,128)(2,1)S(1)} %add_convert_fusion.1), channel_id=1, source_target_pairs={{0,64},{32,480},{64,128},{96,32},{128,192},{160,96},{192,256},{224... | collective-permute-start | bytes 1572872 | tf_op jit(solution)/shard_map/ppermute | solution.py:207
  45.4 12.3 %collective-permute-start.4 = (bf16[2,16,2,32,128]{4,3,2,1,0:T(8,128)(2,1)S(1)}, bf16[2,16,2,32,128]{4,3,2,1,0:T(8,128)(2,1)S(1)}, u32[]{:S(2)}, u32[]{:S(2)}) collective-permute-start(bf16[2,16,2,32,128]{4,3,2,1,0:T(8,128)(2,1)S(1)} %add_convert_fusion.3), channel_id=1, source_target_pairs={{0,64},{32,480},{64,128},{96,32},{128,192},{160,96},{192,256},{224... | collective-permute-start | bytes 1572872 | tf_op jit(solution)/shard_map/ppermute | solution.py:208
  52.7 9.4 %copy-start.1 = (bf16[1024,1024]{1,0:T(8,128)(2,1)S(1)}, bf16[1024,1024]{1,0:T(8,128)(2,1)}, u32[]{:S(2)}) copy-start(bf16[1024,1024]{1,0:T(8,128)(2,1)} %constant.37.clone.basis) | copy-start | bytes 6291460
  52.9 12.4 %collective-permute-start.8 = (bf16[2,16,2,32,128]{4,3,2,1,0:T(8,128)(2,1)S(1)}, bf16[2,16,2,32,128]{4,3,2,1,0:T(8,128)(2,1)S(1)}, u32[]{:S(2)}, u32[]{:S(2)}) collective-permute-start(bf16[2,16,2,32,128]{4,3,2,1,0:T(8,128)(2,1)S(1)} %add_convert_fusion), channel_id=1, source_target_pairs={{0,64},{32,480},{64,128},{96,32},{128,192},{160,96},{192,256},{224... | collective-permute-start | bytes 1572872 | tf_op jit(solution)/shard_map/ppermute | solution.py:210
  57.9 13.1 %collective-permute-start.5 = (bf16[2,16,2,32,128]{4,3,2,1,0:T(8,128)(2,1)S(1)}, bf16[2,16,2,32,128]{4,3,2,1,0:T(8,128)(2,1)S(1)}, u32[]{:S(2)}, u32[]{:S(2)}) collective-permute-start(bf16[2,16,2,32,128]{4,3,2,1,0:T(8,128)(2,1)S(1)} %add_convert_fusion.2), channel_id=1, source_target_pairs={{0,64},{32,480},{64,128},{96,32},{128,192},{160,96},{192,256},{224... | collective-permute-start | bytes 1572872 | tf_op jit(solution)/shard_map/ppermute | solution.py:211
  65.3 6.6 %copy-start.7 = (bf16[2,16,2,32,128]{4,3,2,1,0:T(8,128)(2,1)}, bf16[2,16,2,32,128]{4,3,2,1,0:T(8,128)(2,1)S(1)}, u32[]{:S(2)}) copy-start(bf16[2,16,2,32,128]{4,3,2,1,0:T(8,128)(2,1)S(1)} %collective-permute-done.8) | copy-start | bytes 1572868
  71.0 1.0 copy-start.8
  72.0 4.1 %collective-permute-start.9 = (bf16[2,16,2,32,128]{4,3,2,1,0:T(8,128)(2,1)}, bf16[2,16,2,32,128]{4,3,2,1,0:T(8,128)(2,1)}, u32[]{:S(2)}, u32[]{:S(2)}) collective-permute-start(bf16[2,16,2,32,128]{4,3,2,1,0:T(8,128)(2,1)} %pad_maximum_fusion), channel_id=1, source_target_pairs={{0,32},{32,0},{64,96},{96,64},{128,160},{160,128},{192,224},{224,1... | collective-permute-start | bytes 1572872 | tf_op jit(solution)/shard_map/ppermute | solution.py:213
  73.9 31.7 %copy-start.2 = (f32[256,1024]{1,0:T(8,128)S(1)}, f32[256,1024]{1,0:T(8,128)}, u32[]{:S(2)}) copy-start(f32[256,1024]{1,0:T(8,128)} %convolution_bitcast_fusion.spec_proj) | copy-start | bytes 3145732

commit v6 on v5

--- a/solution.py
+++ b/solution.py
@@ -27,40 +27,44 @@
     return np.concatenate([np.cos(phases), np.sin(phases)], axis=1).astype(jnp.bfloat16)
 
 
-def describe_kernel(lists, row_shift, stretch, place, meta):
+def describe_kernel(lists, row_shift, stretch, meta):
     count = jnp.sum((lists[...] >= 0).astype(jnp.float32), axis=0, keepdims=True)
-    lane = lax.broadcasted_iota(jnp.int32, count.shape, 1)
     meta[0:1] = lists[0:1].astype(jnp.float32)
     meta[1:2] = count
     meta[2:3] = row_shift[...]
     meta[3:4] = 1.0 / (TR * count * stretch[...] / SZ)
-    meta[4:5] = jnp.where(lane == 0, place[0], place[1]).astype(jnp.float32)
-
-
-def describe(lists, row_shift, stretch, place):
+
+
+def describe(lists, row_shift, stretch):
     vmem = pl.BlockSpec(memory_space=pltpu.VMEM)
     return pl.pallas_call(
         describe_kernel,
-        out_shape=jax.ShapeDtypeStruct((5, lists.shape[1]), jnp.float32),
-        in_specs=[vmem, vmem, vmem, pl.BlockSpec(memory_space=pltpu.SMEM)],
+        out_shape=jax.ShapeDtypeStruct((4, lists.shape[1]), jnp.float32),
+        in_specs=[vmem] * 3,
         out_specs=vmem,
-    )(lists, row_shift, stretch, place)
-
-
-def unit_kernel(hop, lanes, chips, near, near_views, far, far_views, *refs):
-    outs, (total, listed) = refs[:-2], refs[-2:]
+        compiler_params=pltpu.CompilerParams(vmem_limit_bytes=1024 * 1024),
+    )(lists, row_shift, stretch)
+
+
+def unit_kernel(hop, lanes, chips, slabs, resumed, fetched, place, *refs):
+    sources = [refs[2 * s : 2 * s + 2] for s in range(slabs)]
+    if fetched:
+        refs, (brought, arrived) = refs[:-2], refs[-2:]
+    outs, (total, listed) = refs[2 * slabs + resumed : -2], refs[-2:]
     angles = total.shape[1]
-    chip, core = near[4, 0].astype(jnp.int32), near[4, 1].astype(jnp.int32)
+    chip, core = place[0], place[1]
     reach = chips // 2 - hop
     target = lax.rem(chip + jnp.where(core == 0, reach, -reach) + chips, chips)
     owners = 2 * chips
-    sources = ((near, near_views), (far, far_views))
     row = lax.broadcasted_iota(jnp.int32, (PIECE, TR), 1).astype(jnp.float32)
     depth = lax.broadcasted_iota(jnp.int32, (PIECE, TR), 0)
     zero = jnp.zeros((PIECE, TR), jnp.bfloat16)
     owner = [(2 * target + (core ^ lane)).astype(jnp.float32) for lane in range(lanes)]
     first_angle = core * HALF
-    total[...] = jnp.zeros_like(total)
+    if fetched:
+        fetch = pltpu.make_async_copy(sources[0][1].at[pl.ds(first_angle, HALF)], brought, arrived)
+        fetch.start()
+    total[...] = refs[2 * slabs][...] if resumed else jnp.zeros_like(total)
 
     def entry(meta, a, lane):
         k = owner[lane] - meta[0, a]
@@ -78,6 +82,9 @@
             return found
 
         live.append(lax.fori_loop(0, angles, note, jnp.int32(0), unroll=UNROLL))
+
+    if fetched:
+        fetch.wait()
 
     def some(at, carry):
         for m in range(BATCH):
@@ -106,36 +113,65 @@
                     pieces.append(jnp.where(gap == jnp.int16(p * PIECE), at_below, hit))
                 weights = jnp.concatenate(pieces, axis=0)
                 z0 = pl.multiple_of(block * 128, 128)
-                total[lane, i, cycle] += jnp.dot(
-                    views[a, :, pl.ds(z0, WINDOW)], weights, preferred_element_type=jnp.float32
-                )
+                depths = pl.ds(z0, WINDOW)
+                view = brought[i, :, depths] if fetched else views[a, :, depths]
+                total[lane, i, cycle] += jnp.dot(view, weights, preferred_element_type=jnp.float32)
         return carry
 
     most = functools.reduce(jnp.maximum, live)
     lax.fori_loop(0, lax.div(most + BATCH - 1, BATCH), some, 0)
     for half, out in enumerate(outs):
-        out[...] = total[:, half * HALF : (half + 1) * HALF].astype(jnp.bfloat16)
-
-
-def units(hop, halves, lanes, chips, near, near_views, far, far_views):
-    narrow = near_views.shape[1]
+        out[...] = total[:, half * HALF : (half + 1) * HALF].astype(out.dtype)
+
+
+def units(hop, halves, lanes, chips, place, sources, before=None, fetched=False):
+    narrow = sources[0][1].shape[1]
     smem = pl.BlockSpec(memory_space=pltpu.SMEM)
     vmem = pl.BlockSpec(memory_space=pltpu.VMEM)
     shape = (lanes, HALF, TPO, narrow, TR)
-    return pl.pallas_call(
-        functools.partial(unit_kernel, hop, lanes, chips),
-        out_shape=[jax.ShapeDtypeStruct(shape, jnp.bfloat16)] * halves,
-        in_specs=[smem, vmem, smem, vmem],
+    operands = [place] + [ref for source in sources for ref in source]
+    specs = [smem] + [smem, pl.BlockSpec(memory_space=pl.ANY) if fetched else vmem] * len(sources)
+    scratch = [
+        pltpu.VMEM((lanes, halves * HALF) + shape[2:], jnp.float32),
+        pltpu.SMEM((len(sources), halves * HALF * lanes + 1), jnp.int32),
+    ]
+    if fetched:
+        scratch += [pltpu.VMEM((HALF,) + sources[0][1].shape[1:], jnp.bfloat16), pltpu.SemaphoreType.DMA]
+    dtype = jnp.float32 if fetched else jnp.bfloat16
+    if before is not None:
+        operands, specs = operands + [before], specs + [vmem]
+    return pl.pallas_call(
+        functools.partial(
+            unit_kernel, hop, lanes, chips, len(sources), before is not None, fetched
+        ),
+        out_shape=[jax.ShapeDtypeStruct(shape, dtype)] * halves,
+        in_specs=specs,
         out_specs=[vmem] * halves,
-        scratch_shapes=[
-            pltpu.VMEM((lanes, halves * HALF) + shape[2:], jnp.float32),
-            pltpu.SMEM((2, halves * HALF * lanes + 1), jnp.int32),
-        ],
-        compiler_params=pltpu.CompilerParams(vmem_limit_bytes=16 * 1024 * 1024),
+        scratch_shapes=scratch,
+        compiler_params=pltpu.CompilerParams(vmem_limit_bytes=12 * 1024 * 1024),
         cost_estimate=pl.CostEstimate(
-            flops=25 * 10**8 * halves, bytes_accessed=10**6, transcendentals=0
+            flops=12 * 10**8 * halves * len(sources), bytes_accessed=10**6, transcendentals=0
         ),
-    )(near, near_views, far, far_views)
+    )(*operands)
+
+
+def close_kernel(place, here, there, mine, other_here, other_there, other_mine, out):
+    core = place[1]
+    for half, terms in enumerate(((here, there, mine), (other_here, other_there, other_mine))):
+        total = sum(term[...].astype(jnp.float32) for term in terms)
+        out[pl.ds((core ^ half) * HALF, HALF)] = total.astype(jnp.bfloat16)
+
+
+def close(place, *terms):
+    smem = pl.BlockSpec(memory_space=pltpu.SMEM)
+    vmem = pl.BlockSpec(memory_space=pltpu.VMEM)
+    return pl.pallas_call(
+        close_kernel,
+        out_shape=jax.ShapeDtypeStruct((2 * HALF,) + terms[0].shape[1:], jnp.bfloat16),
+        in_specs=[smem] + [vmem] * len(terms),
+        out_specs=vmem,
+        compiler_params=pltpu.CompilerParams(vmem_limit_bytes=6 * 1024 * 1024),
+    )(place, *terms)
 
 
 def add(*terms):
@@ -170,7 +206,7 @@
         ],
         in_specs=[vmem] * 3,
         out_specs=[vmem] * 2,
-        compiler_params=pltpu.CompilerParams(vmem_limit_bytes=24 * 1024 * 1024),
+        compiler_params=pltpu.CompilerParams(vmem_limit_bytes=12 * 1024 * 1024),
         cost_estimate=pl.CostEstimate(flops=10**9, bytes_accessed=10**6, transcendentals=0),
     )(got, basis, spec_proj)
 
@@ -187,8 +223,10 @@
     onward = [(i, (i + (2 if i % 2 == 0 else -2)) % n_grp) for i in range(n_grp)]
 
     sibling_views = lax.ppermute(views, "grp", swap)
-    meta = describe(footprint[0].T, row_shift, stretch, jnp.stack([chip, core]))
-    known = (chips, meta, views, lax.ppermute(meta, "grp", swap), sibling_views)
+    place = jnp.stack([chip, core])
+    meta = describe(footprint[0].T, row_shift, stretch)
+    near, far = (meta, views), (lax.ppermute(meta, "grp", swap), sibling_views)
+    known = (2, chips, place, [near, far])
 
     n_freq = n_ang * views.shape[1] // 2
     basis = jnp.asarray(dft_basis(2 * n_freq))
@@ -196,26 +234,24 @@
         projections.reshape(-1, 2 * n_freq), basis, preferred_element_type=jnp.float32
     )
 
-    first = lax.ppermute(units(0, 1, 2, *known)[0], "grp", onward)
-    mine = units(1, 2, 2, *known)
+    early = units(0, 1, 2, chips, place, [near], fetched=True)[0]
+    first = lax.ppermute(units(0, 1, 2, chips, place, [far], early)[0], "grp", onward)
+    mine = units(1, 2, *known)
     second = lax.ppermute(mine[1], "grp", onward)
-    kept = units(4, 2, 1, *known)
-    sending, kept, meta = lax.optimization_barrier((add(first, mine[0]), kept, meta))
-    known = known[:1] + (meta,) + known[2:]
+    kept = units(4, 2, 1, *known[1:])
+    sending, kept, place = lax.optimization_barrier((add(first, mine[0]), kept, place))
+    known = (2, chips, place, [near, far])
     first = lax.ppermute(sending, "grp", onward)
-    mine = units(2, 2, 2, *known)
+    mine = units(2, 2, *known)
     second = lax.ppermute(add(second, mine[1]), "grp", onward)
     first = lax.ppermute(add(first, mine[0]), "grp", onward)
-    mine = units(3, 2, 2, *known)
+    mine = units(3, 2, *known)
     second = lax.ppermute(add(second, mine[1]), "grp", onward)
     first = lax.ppermute(add(first, mine[0]), "grp", onward)
-    leaving, spec_proj = lax.optimization_barrier((jnp.stack([second[1], first[1]]), spec_proj))
-    from_sibling = lax.ppermute(leaving, "grp", swap)
-    ready = (
-        add(first[0], from_sibling[0], kept[0][0]),
-        add(second[0], from_sibling[1], kept[1][0]),
-    )
-    summed = jnp.where(core == 0, jnp.concatenate(ready), jnp.concatenate(ready[::-1]))
+    to_first = lax.ppermute(second[1], "grp", swap)
+    leaving, spec_proj = lax.optimization_barrier((first[1], spec_proj))
+    to_second = lax.ppermute(leaving, "grp", swap)
+    summed = close(place, first[0], to_first, kept[0][0], second[0], to_second, kept[1][0])
 
     got = lax.all_to_all(summed, "ang", split_axis=0, concat_axis=0, tiled=True)
     rows, copies = finish(got, basis, spec_proj, n_ang)

time: 123 us -> 118 us (0.959)
  waiting for transfers between devices: 14.5 us -> 11.4 us
  other arithmetic: 4.58 us -> 1.63 us
  local copies, waits for them, and re-layouts: 2.42 us -> 3.67 us
    ppermute x3 -> x4, starting transfers between devices: 7.86 us -> 10.1 us  [the longest x1 3.87 us: body(): lax.ppermute(units(0, 1, 2, chips, place, [far], early)[0], 'grp', onward)]
    ppermute x2, waiting for transfers between devices: 6.81 us -> 4.74 us  [body(): first = lax.ppermute(add(first, mine[0]), 'grp', onward)]
    ppermute x1, starting transfers between devices: 4.28 us -> 2.74 us  [body(): second = lax.ppermute(mine[1], 'grp', onward)]
    ppermute x3 -> x4, waiting for transfers between devices: 6.15 us -> 4.63 us  [the longest x1 3.14 us: body(): lax.ppermute(units(0, 1, 2, chips, place, [far], early)[0], 'grp', onward)]
    convert_element_type x6 -> x5, other arithmetic: 2.37 us -> 0.93 us  [add(): return total.astype(jnp.bfloat16)]
    another operation x2 -> x1, other arithmetic: 1.5 us -> 0.08 us  [body(): place = jnp.stack([chip, core])]
    unnamed x18 -> x14, local copies, waits for them, and re-layouts: 2.38 us -> 3.6 us
    pallas_call x6 -> x8, Pallas kernels: 21.3 us -> 21.3 us  [the longest x6 20.5 us: units(): pl.pallas_call(functools.partial(unit_kernel, hop, lanes, chips, len(sour...]
  transfers between devices with their start and end apart: 10 -> 11, of which waited for: 6 -> 5; matrix products, arithmetic and copies ran while one was open for 3% -> 2% of each run, Pallas kernels for 15% -> 16%
where the time goes in v6:
time: 118 us; the launch traced here: 117 us
  blocking collectives  42.2 us (36%)
  starting transfers between devices  34 us (29%)
  Pallas kernels  22.7 us (19%)
  waiting for transfers between devices  11.4 us (10%)
  local copies, waits for them, and re-layouts  3.67 us (3%)
  other arithmetic  1.63 us (1%)
    all_to_all x1, blocking collectives, body(): got = lax.all_to_all(summed, 'ang', split_axis=0, concat_axis=0, tiled=True)  27.9 us
    pallas_call x6, Pallas kernels, units(): pl.pallas_call(functools.partial(unit_kernel, hop, lanes, chips, len(sour...  20.5 us
    all_to_all x1, blocking collectives, body(): lax.all_to_all(copies, 'ang', split_axis=0, concat_axis=0, tiled=True)  14.3 us
    ppermute x2, starting transfers between devices, body(): second = lax.ppermute(add(second, mine[1]), 'grp', onward)  10 us
    ppermute x2, starting transfers between devices, body(): first = lax.ppermute(add(first, mine[0]), 'grp', onward)  7.14 us
    ppermute x2, waiting for transfers between devices, body(): first = lax.ppermute(add(first, mine[0]), 'grp', onward)  4.74 us
    ppermute x1, starting transfers between devices, body(): lax.ppermute(units(0, 1, 2, chips, place, [far], early)[0], 'grp', onward)  3.87 us
    unnamed x14, local copies, waits for them, and re-layouts  3.6 us
  transfers between devices with their start and end apart: 11, of which 5 were waited for; matrix products, arithmetic and copies ran while one was open for 2% of the time, Pallas kernels for 16%

profile of v6, /device:TPU:8, one launch (start us, length us, event | category | flops | bytes accessed | tf_op | source)
XLA Modules:
  0.0 117.3 jit_solution(14091439349045822181)
XLA Ops:
  0.6 2.1 %collective-permute-start.1 = (bf16[32,32,1024]{2,1,0:T(8,128)(2,1)}, bf16[32,32,1024]{2,1,0:T(8,128)(2,1)S(1)}, u32[]{:S(2)}, u32[]{:S(2)}) collective-permute-start(bf16[32,32,1024]{2,1,0:T(8,128)(2,1)} %bitcast.26), channel_id=1, source_target_pairs={{0,32},{32,0},{64,96},{96,64},{128,160},{160,128},{192,224},{224,1... | collective-permute-start | bytes 6291464 | tf_op jit(solution)/shard_map/ppermute | solution.py:225
  4.7 2.4 %collective-permute-start = (f32[4,32]{1,0:T(4,128)S(1)}, f32[4,32]{1,0:T(4,128)S(1)}, u32[]{:S(2)}, u32[]{:S(2)}) collective-permute-start(f32[4,32]{1,0:T(4,128)S(1)} %shard_map.77.refs_0_), channel_id=1, source_target_pairs={{0,32},{32,0},{64,96},{96,64},{128,160},{160,128},{192,224},{224,1... | collective-permute-start | bytes 1544 | tf_op jit(solution)/shard_map/ppermute | solution.py:228
  7.2 1.6 %copy-done.5 = bf16[1,32,32,1024]{3,2,1,0:T(8,128)(2,1)S(1)} copy-done((bf16[1,32,32,1024]{3,2,1,0:T(8,128)(2,1)S(1)}, bf16[1,32,32,1024]{3,2,1,0:T(8,128)(2,1)}, u32[]{:S(2)}) %copy-start.5) | copy-done | bytes 2097176
  8.8 2.1 %shard_map.78.refs_2_ = f32[2,16,2,32,128]{4,3,2,1,0:T(8,128)S(1)} custom-call(s32[2]{0:T(128)S(1)} %pad_add_fusion.place, f32[4,32]{1,0:T(4,128)S(1)} %shard_map.77.refs_0_, bf16[32,32,1024]{2,1,0:T(8,128)(2,1)S(1)} %bitcast.27), custom_call_target="tpu_custom_call" | custom-call | flops 1200000000 | bytes 1000000 | tf_op jit(solution)/shard_map/pallas_call | solution.py:143
  11.0 2.1 %shard_map.79 = bf16[2,16,2,32,128]{4,3,2,1,0:T(8,128)(2,1)S(1)} custom-call(s32[2]{0:T(128)S(1)} %pad_add_fusion.place, f32[4,32]{1,0:T(4,128)S(1)} %collective-permute-done.refs_0_.refs_2_, bf16[32,32,1024]{2,1,0:T(8,128)(2,1)S(1)} %collective-permute-done.1.refs_1_.refs_3_, f32[2,16,2,32,128]{4,3,2,1,0:T(8,128)S(1)} %shard_map.78.refs_2_), custom_call_target="tpu_custom_call" | custom-call | flops 1200000000 | bytes 1000000 | tf_op jit(solution)/shard_map/pallas_call | solution.py:143
  13.1 3.9 %collective-permute-start.2 = (bf16[2,16,2,32,128]{4,3,2,1,0:T(8,128)(2,1)S(1)}, bf16[2,16,2,32,128]{4,3,2,1,0:T(8,128)(2,1)S(1)}, u32[]{:S(2)}, u32[]{:S(2)}) collective-permute-start(bf16[2,16,2,32,128]{4,3,2,1,0:T(8,128)(2,1)S(1)} %shard_map.79), channel_id=1, source_target_pairs={{0,64},{32,480},{64,128},{96,32},{128,192},{160,96},{192,256},{224... | collective-permute-start | bytes 1572872 | tf_op jit(solution)/shard_map/ppermute | solution.py:238
  17.0 5.3 %shard_map.80 = (bf16[2,16,2,32,128]{4,3,2,1,0:T(8,128)(2,1)S(1)}, bf16[2,16,2,32,128]{4,3,2,1,0:T(8,128)(2,1)S(1)}) custom-call(s32[2]{0:T(128)S(1)} %pad_add_fusion.place, f32[4,32]{1,0:T(4,128)S(1)} %shard_map.77.refs_0_, bf16[32,32,1024]{2,1,0:T(8,128)(2,1)S(1)} %bitcast.28, f32[4,32]{1,0:T(4,128)S(1)} %collective-permute-done.refs_0_.refs_2_, ...), custom_call_target="tpu_custom_call" | custom-call | flops 4800000000 | bytes 1000000 | tf_op jit(solution)/shard_map/pallas_call | solution.py:143
  22.3 2.7 %collective-permute-start.6 = (bf16[2,16,2,32,128]{4,3,2,1,0:T(8,128)(2,1)S(1)}, bf16[2,16,2,32,128]{4,3,2,1,0:T(8,128)(2,1)S(1)}, u32[]{:S(2)}, u32[]{:S(2)}) collective-permute-start(bf16[2,16,2,32,128]{4,3,2,1,0:T(8,128)(2,1)S(1)} %get-tuple-element.25), channel_id=1, source_target_pairs={{0,64},{32,480},{64,128},{96,32},{128,192},{160,96},{192,256},{224... | collective-permute-start | bytes 1572872 | tf_op jit(solution)/shard_map/ppermute | solution.py:240
  25.0 2.6 %shard_map.81 = (bf16[1,16,2,32,128]{4,3,2,1,0:T(8,128)(2,1)S(1)}, bf16[1,16,2,32,128]{4,3,2,1,0:T(8,128)(2,1)S(1)}) custom-call(s32[2]{0:T(128)S(1)} %pad_add_fusion.place, f32[4,32]{1,0:T(4,128)S(1)} %shard_map.77.refs_0_, bf16[32,32,1024]{2,1,0:T(8,128)(2,1)S(1)} %bitcast.29, f32[4,32]{1,0:T(4,128)S(1)} %collective-permute-done.refs_0_.refs_2_, ...), custom_call_target="tpu_custom_call" | custom-call | flops 4800000000 | bytes 1000000 | tf_op jit(solution)/shard_map/pallas_call | solution.py:143
  27.6 3.1 %collective-permute-done.2 = bf16[2,16,2,32,128]{4,3,2,1,0:T(8,128)(2,1)S(1)} collective-permute-done((bf16[2,16,2,32,128]{4,3,2,1,0:T(8,128)(2,1)S(1)}, bf16[2,16,2,32,128]{4,3,2,1,0:T(8,128)(2,1)S(1)}, u32[]{:S(2)}, u32[]{:S(2)}) %collective-permute-start.2) | collective-permute-done | bytes 524320 | tf_op jit(solution)/shard_map/ppermute | solution.py:238
  31.0 1.9 %collective-permute-start.3 = (bf16[2,16,2,32,128]{4,3,2,1,0:T(8,128)(2,1)S(1)}, bf16[2,16,2,32,128]{4,3,2,1,0:T(8,128)(2,1)S(1)}, u32[]{:S(2)}, u32[]{:S(2)}) collective-permute-start(bf16[2,16,2,32,128]{4,3,2,1,0:T(8,128)(2,1)S(1)} %add_convert_fusion.4), channel_id=1, source_target_pairs={{0,64},{32,480},{64,128},{96,32},{128,192},{160,96},{192,256},{224... | collective-permute-start | bytes 1572872 | tf_op jit(solution)/shard_map/ppermute | solution.py:244
  32.9 4.6 %shard_map.82 = (bf16[2,16,2,32,128]{4,3,2,1,0:T(8,128)(2,1)S(1)}, bf16[2,16,2,32,128]{4,3,2,1,0:T(8,128)(2,1)S(1)}) custom-call(s32[2]{0:T(128)S(1)} %pad_add_fusion.place, f32[4,32]{1,0:T(4,128)S(1)} %shard_map.77.refs_0_, bf16[32,32,1024]{2,1,0:T(8,128)(2,1)S(1)} %bitcast.30, f32[4,32]{1,0:T(4,128)S(1)} %collective-permute-done.refs_0_.refs_2_, ...), custom_call_target="tpu_custom_call" | custom-call | flops 4800000000 | bytes 1000000 | tf_op jit(solution)/shard_map/pallas_call | solution.py:143
  37.7 5.9 %collective-permute-start.7 = (bf16[2,16,2,32,128]{4,3,2,1,0:T(8,128)(2,1)S(1)}, bf16[2,16,2,32,128]{4,3,2,1,0:T(8,128)(2,1)S(1)}, u32[]{:S(2)}, u32[]{:S(2)}) collective-permute-start(bf16[2,16,2,32,128]{4,3,2,1,0:T(8,128)(2,1)S(1)} %add_convert_fusion.1), channel_id=1, source_target_pairs={{0,64},{32,480},{64,128},{96,32},{128,192},{160,96},{192,256},{224... | collective-permute-start | bytes 1572872 | tf_op jit(solution)/shard_map/ppermute | solution.py:246
  43.7 2.9 %collective-permute-start.4 = (bf16[2,16,2,32,128]{4,3,2,1,0:T(8,128)(2,1)S(1)}, bf16[2,16,2,32,128]{4,3,2,1,0:T(8,128)(2,1)S(1)}, u32[]{:S(2)}, u32[]{:S(2)}) collective-permute-start(bf16[2,16,2,32,128]{4,3,2,1,0:T(8,128)(2,1)S(1)} %add_convert_fusion.3), channel_id=1, source_target_pairs={{0,64},{32,480},{64,128},{96,32},{128,192},{160,96},{192,256},{224... | collective-permute-start | bytes 1572872 | tf_op jit(solution)/shard_map/ppermute | solution.py:247
  46.7 3.8 %shard_map.83 = (bf16[2,16,2,32,128]{4,3,2,1,0:T(8,128)(2,1)S(1)}, bf16[2,16,2,32,128]{4,3,2,1,0:T(8,128)(2,1)S(1)}) custom-call(s32[2]{0:T(128)S(1)} %pad_add_fusion.place, f32[4,32]{1,0:T(4,128)S(1)} %shard_map.77.refs_0_, bf16[32,32,1024]{2,1,0:T(8,128)(2,1)S(1)} %bitcast.31, f32[4,32]{1,0:T(4,128)S(1)} %collective-permute-done.refs_0_.refs_2_, ...), custom_call_target="tpu_custom_call" | custom-call | flops 4800000000 | bytes 1000000 | tf_op jit(solution)/shard_map/pallas_call | solution.py:143
  50.8 4.2 %collective-permute-start.8 = (bf16[2,16,2,32,128]{4,3,2,1,0:T(8,128)(2,1)S(1)}, bf16[2,16,2,32,128]{4,3,2,1,0:T(8,128)(2,1)S(1)}, u32[]{:S(2)}, u32[]{:S(2)}) collective-permute-start(bf16[2,16,2,32,128]{4,3,2,1,0:T(8,128)(2,1)S(1)} %add_convert_fusion), channel_id=1, source_target_pairs={{0,64},{32,480},{64,128},{96,32},{128,192},{160,96},{192,256},{224... | collective-permute-start | bytes 1572872 | tf_op jit(solution)/shard_map/ppermute | solution.py:249
  56.2 4.2 %collective-permute-start.5 = (bf16[2,16,2,32,128]{4,3,2,1,0:T(8,128)(2,1)S(1)}, bf16[2,16,2,32,128]{4,3,2,1,0:T(8,128)(2,1)S(1)}, u32[]{:S(2)}, u32[]{:S(2)}) collective-permute-start(bf16[2,16,2,32,128]{4,3,2,1,0:T(8,128)(2,1)S(1)} %add_convert_fusion.2), channel_id=1, source_target_pairs={{0,64},{32,480},{64,128},{96,32},{128,192},{160,96},{192,256},{224... | collective-permute-start | bytes 1572872 | tf_op jit(solution)/shard_map/ppermute | solution.py:250
  61.2 2.0 %collective-permute-done.8 = bf16[2,16,2,32,128]{4,3,2,1,0:T(8,128)(2,1)S(1)} collective-permute-done((bf16[2,16,2,32,128]{4,3,2,1,0:T(8,128)(2,1)S(1)}, bf16[2,16,2,32,128]{4,3,2,1,0:T(8,128)(2,1)S(1)}, u32[]{:S(2)}, u32[]{:S(2)}) %collective-permute-start.8) | collective-permute-done | bytes 524320 | tf_op jit(solution)/shard_map/ppermute | solution.py:249
  63.2 1.9 %collective-permute-start.9 = (bf16[16,2,32,128]{3,2,1,0:T(8,128)(2,1)S(1)}, bf16[16,2,32,128]{3,2,1,0:T(8,128)(2,1)S(1)}, u32[]{:S(2)}, u32[]{:S(2)}) collective-permute-start(bf16[16,2,32,128]{3,2,1,0:T(8,128)(2,1)S(1)} %get-tuple-element.37), channel_id=1, source_target_pairs={{0,32},{32,0},{64,96},{96,64},{128,160},{160,128},{192,224},{224,1... | collective-permute-start | bytes 786440 | tf_op jit(solution)/shard_map/ppermute | solution.py:251
  65.2 3.7 %collective-permute-done.5 = bf16[2,16,2,32,128]{4,3,2,1,0:T(8,128)(2,1)S(1)} collective-permute-done((bf16[2,16,2,32,128]{4,3,2,1,0:T(8,128)(2,1)S(1)}, bf16[2,16,2,32,128]{4,3,2,1,0:T(8,128)(2,1)S(1)}, u32[]{:S(2)}, u32[]{:S(2)}) %collective-permute-start.5) | collective-permute-done | bytes 524320 | tf_op jit(solution)/shard_map/ppermute | solution.py:250
  68.9 1.9 %collective-permute-start.10 = (bf16[16,2,32,128]{3,2,1,0:T(8,128)(2,1)S(1)}, bf16[16,2,32,128]{3,2,1,0:T(8,128)(2,1)S(1)}, u32[]{:S(2)}, u32[]{:S(2)}) collective-permute-start(bf16[16,2,32,128]{3,2,1,0:T(8,128)(2,1)S(1)} %get-tuple-element.29), channel_id=1, source_target_pairs={{0,32},{32,0},{64,96},{96,64},{128,160},{160,128},{192,224},{224,1... | collective-permute-start | bytes 786440 | tf_op jit(solution)/shard_map/ppermute | solution.py:253
  70.8 1.5 %collective-permute-done.10.other_there = bf16[16,2,32,128]{3,2,1,0:T(8,128)(2,1)S(1)} collective-permute-done((bf16[16,2,32,128]{3,2,1,0:T(8,128)(2,1)S(1)}, bf16[16,2,32,128]{3,2,1,0:T(8,128)(2,1)S(1)}, u32[]{:S(2)}, u32[]{:S(2)}) %collective-permute-start.10) | collective-permute-done | bytes 262176 | tf_op jit(solution)/shard_map/ppermute | solution.py:253
  73.0 27.9 %all_to_all.10.got = bf16[32,2,32,128]{3,2,1,0:T(8,128)(2,1)S(1)} all-to-all(bf16[32,2,32,128]{3,2,1,0:T(8,128)(2,1)S(1)} %shard_map.84), channel_id=1, replica_groups=mesh['grp'=16,'ang'=32] {'ang'}, dimensions={0} | all-to-all | bytes 1048576 | tf_op jit(solution)/shard_map/all_to_all | solution.py:256
  102.4 14.3 %all_to_all.11 = f32[32,8,128]{2,1,0:T(8,128)S(1)} all-to-all(f32[32,8,128]{2,1,0:T(8,128)S(1)} %get-tuple-element.33), channel_id=1, replica_groups=mesh['grp'=16,'ang'=32] {'ang'}, dimensions={0} | all-to-all | bytes 262144 | tf_op jit(solution)/shard_map/all_to_all | solution.py:258
  (34 shorter events, 7.7 us)
Async XLA Ops:
  0.6 59.8 %copy-start = (bf16[1,2,128,1024]{3,2,1,0:T(8,128)(2,1)S(1)}, bf16[1,2,128,1024]{3,2,1,0:T(8,128)(2,1)}, u32[]{:S(2)}) copy-start(bf16[1,2,128,1024]{3,2,1,0:T(8,128)(2,1)} %param.10) | copy-start | bytes 1572868
  0.6 10.4 %collective-permute-start.1 = (bf16[32,32,1024]{2,1,0:T(8,128)(2,1)}, bf16[32,32,1024]{2,1,0:T(8,128)(2,1)S(1)}, u32[]{:S(2)}, u32[]{:S(2)}) collective-permute-start(bf16[32,32,1024]{2,1,0:T(8,128)(2,1)} %bitcast.26), channel_id=1, source_target_pairs={{0,32},{32,0},{64,96},{96,64},{128,160},{160,128},{192,224},{224,1... | collective-permute-start | bytes 6291464 | tf_op jit(solution)/shard_map/ppermute | solution.py:225
  2.7 0.7 copy-start.2
  3.4 0.7 copy-start.3
  4.1 0.7 copy-start.4
  4.7 6.3 %collective-permute-start = (f32[4,32]{1,0:T(4,128)S(1)}, f32[4,32]{1,0:T(4,128)S(1)}, u32[]{:S(2)}, u32[]{:S(2)}) collective-permute-start(f32[4,32]{1,0:T(4,128)S(1)} %shard_map.77.refs_0_), channel_id=1, source_target_pairs={{0,32},{32,0},{64,96},{96,64},{128,160},{160,128},{192,224},{224,1... | collective-permute-start | bytes 1544 | tf_op jit(solution)/shard_map/ppermute | solution.py:228
  7.2 1.6 %copy-start.5 = (bf16[1,32,32,1024]{3,2,1,0:T(8,128)(2,1)S(1)}, bf16[1,32,32,1024]{3,2,1,0:T(8,128)(2,1)}, u32[]{:S(2)}) copy-start(bf16[1,32,32,1024]{3,2,1,0:T(8,128)(2,1)} %param.6) | copy-start | bytes 6291460
  11.0 6.0 %copy-start.6 = (bf16[1,32,32,1024]{3,2,1,0:T(8,128)(2,1)S(1)}, bf16[1,32,32,1024]{3,2,1,0:T(8,128)(2,1)}, u32[]{:S(2)}) copy-start(bf16[1,32,32,1024]{3,2,1,0:T(8,128)(2,1)} %param.6) | copy-start | bytes 6291460
  13.1 17.7 %collective-permute-start.2 = (bf16[2,16,2,32,128]{4,3,2,1,0:T(8,128)(2,1)S(1)}, bf16[2,16,2,32,128]{4,3,2,1,0:T(8,128)(2,1)S(1)}, u32[]{:S(2)}, u32[]{:S(2)}) collective-permute-start(bf16[2,16,2,32,128]{4,3,2,1,0:T(8,128)(2,1)S(1)} %shard_map.79), channel_id=1, source_target_pairs={{0,64},{32,480},{64,128},{96,32},{128,192},{160,96},{192,256},{224... | collective-permute-start | bytes 1572872 | tf_op jit(solution)/shard_map/ppermute | solution.py:238
  22.3 15.2 %collective-permute-start.6 = (bf16[2,16,2,32,128]{4,3,2,1,0:T(8,128)(2,1)S(1)}, bf16[2,16,2,32,128]{4,3,2,1,0:T(8,128)(2,1)S(1)}, u32[]{:S(2)}, u32[]{:S(2)}) collective-permute-start(bf16[2,16,2,32,128]{4,3,2,1,0:T(8,128)(2,1)S(1)} %get-tuple-element.25), channel_id=1, source_target_pairs={{0,64},{32,480},{64,128},{96,32},{128,192},{160,96},{192,256},{224... | collective-permute-start | bytes 1572872 | tf_op jit(solution)/shard_map/ppermute | solution.py:240
  31.0 12.6 %collective-permute-start.3 = (bf16[2,16,2,32,128]{4,3,2,1,0:T(8,128)(2,1)S(1)}, bf16[2,16,2,32,128]{4,3,2,1,0:T(8,128)(2,1)S(1)}, u32[]{:S(2)}, u32[]{:S(2)}) collective-permute-start(bf16[2,16,2,32,128]{4,3,2,1,0:T(8,128)(2,1)S(1)} %add_convert_fusion.4), channel_id=1, source_target_pairs={{0,64},{32,480},{64,128},{96,32},{128,192},{160,96},{192,256},{224... | collective-permute-start | bytes 1572872 | tf_op jit(solution)/shard_map/ppermute | solution.py:244
  37.7 12.9 %collective-permute-start.7 = (bf16[2,16,2,32,128]{4,3,2,1,0:T(8,128)(2,1)S(1)}, bf16[2,16,2,32,128]{4,3,2,1,0:T(8,128)(2,1)S(1)}, u32[]{:S(2)}, u32[]{:S(2)}) collective-permute-start(bf16[2,16,2,32,128]{4,3,2,1,0:T(8,128)(2,1)S(1)} %add_convert_fusion.1), channel_id=1, source_target_pairs={{0,64},{32,480},{64,128},{96,32},{128,192},{160,96},{192,256},{224... | collective-permute-start | bytes 1572872 | tf_op jit(solution)/shard_map/ppermute | solution.py:246
  43.7 12.3 %collective-permute-start.4 = (bf16[2,16,2,32,128]{4,3,2,1,0:T(8,128)(2,1)S(1)}, bf16[2,16,2,32,128]{4,3,2,1,0:T(8,128)(2,1)S(1)}, u32[]{:S(2)}, u32[]{:S(2)}) collective-permute-start(bf16[2,16,2,32,128]{4,3,2,1,0:T(8,128)(2,1)S(1)} %add_convert_fusion.3), channel_id=1, source_target_pairs={{0,64},{32,480},{64,128},{96,32},{128,192},{160,96},{192,256},{224... | collective-permute-start | bytes 1572872 | tf_op jit(solution)/shard_map/ppermute | solution.py:247
  50.6 9.9 %copy-start.1 = (bf16[1024,1024]{1,0:T(8,128)(2,1)S(1)}, bf16[1024,1024]{1,0:T(8,128)(2,1)}, u32[]{:S(2)}) copy-start(bf16[1024,1024]{1,0:T(8,128)(2,1)} %constant.36.clone.basis) | copy-start | bytes 6291460
  50.8 12.4 %collective-permute-start.8 = (bf16[2,16,2,32,128]{4,3,2,1,0:T(8,128)(2,1)S(1)}, bf16[2,16,2,32,128]{4,3,2,1,0:T(8,128)(2,1)S(1)}, u32[]{:S(2)}, u32[]{:S(2)}) collective-permute-start(bf16[2,16,2,32,128]{4,3,2,1,0:T(8,128)(2,1)S(1)} %add_convert_fusion), channel_id=1, source_target_pairs={{0,64},{32,480},{64,128},{96,32},{128,192},{160,96},{192,256},{224... | collective-permute-start | bytes 1572872 | tf_op jit(solution)/shard_map/ppermute | solution.py:249
  56.2 12.6 %collective-permute-start.5 = (bf16[2,16,2,32,128]{4,3,2,1,0:T(8,128)(2,1)S(1)}, bf16[2,16,2,32,128]{4,3,2,1,0:T(8,128)(2,1)S(1)}, u32[]{:S(2)}, u32[]{:S(2)}) collective-permute-start(bf16[2,16,2,32,128]{4,3,2,1,0:T(8,128)(2,1)S(1)} %add_convert_fusion.2), channel_id=1, source_target_pairs={{0,64},{32,480},{64,128},{96,32},{128,192},{160,96},{192,256},{224... | collective-permute-start | bytes 1572872 | tf_op jit(solution)/shard_map/ppermute | solution.py:250
  63.2 7.5 %collective-permute-start.9 = (bf16[16,2,32,128]{3,2,1,0:T(8,128)(2,1)S(1)}, bf16[16,2,32,128]{3,2,1,0:T(8,128)(2,1)S(1)}, u32[]{:S(2)}, u32[]{:S(2)}) collective-permute-start(bf16[16,2,32,128]{3,2,1,0:T(8,128)(2,1)S(1)} %get-tuple-element.37), channel_id=1, source_target_pairs={{0,32},{32,0},{64,96},{96,64},{128,160},{160,128},{192,224},{224,1... | collective-permute-start | bytes 786440 | tf_op jit(solution)/shard_map/ppermute | solution.py:251
  68.9 3.4 %collective-permute-start.10 = (bf16[16,2,32,128]{3,2,1,0:T(8,128)(2,1)S(1)}, bf16[16,2,32,128]{3,2,1,0:T(8,128)(2,1)S(1)}, u32[]{:S(2)}, u32[]{:S(2)}) collective-permute-start(bf16[16,2,32,128]{3,2,1,0:T(8,128)(2,1)S(1)} %get-tuple-element.29), channel_id=1, source_target_pairs={{0,32},{32,0},{64,96},{96,64},{128,160},{160,128},{192,224},{224,1... | collective-permute-start | bytes 786440 | tf_op jit(solution)/shard_map/ppermute | solution.py:253

commit v7 on v6

--- a/solution.py
+++ b/solution.py
@@ -27,23 +27,33 @@
     return np.concatenate([np.cos(phases), np.sin(phases)], axis=1).astype(jnp.bfloat16)
 
 
-def describe_kernel(lists, row_shift, stretch, meta):
-    count = jnp.sum((lists[...] >= 0).astype(jnp.float32), axis=0, keepdims=True)
-    meta[0:1] = lists[0:1].astype(jnp.float32)
+def describe_kernel(lists, row_shift, stretch, meta, *held):
+    held, arrived = held[:-1], held[-1]
+    fetches = [
+        pltpu.make_async_copy(source, target, arrived.at[n])
+        for n, (source, target) in enumerate(zip((lists, row_shift, stretch), held))
+    ]
+    for fetch in fetches:
+        fetch.start()
+    for fetch in fetches:
+        fetch.wait()
+    count = jnp.sum((held[0][...] >= 0).astype(jnp.float32), axis=0, keepdims=True)
+    meta[0:1] = held[0][0:1].astype(jnp.float32)
     meta[1:2] = count
-    meta[2:3] = row_shift[...]
-    meta[3:4] = 1.0 / (TR * count * stretch[...] / SZ)
-
-
-def describe(lists, row_shift, stretch):
-    vmem = pl.BlockSpec(memory_space=pltpu.VMEM)
+    meta[2:3] = held[1][...]
+    meta[3:4] = 1.0 / (TR * count * held[2][...] / SZ)
+
+
+def describe(*operands):
     return pl.pallas_call(
         describe_kernel,
-        out_shape=jax.ShapeDtypeStruct((4, lists.shape[1]), jnp.float32),
-        in_specs=[vmem] * 3,
-        out_specs=vmem,
+        out_shape=jax.ShapeDtypeStruct((4, operands[0].shape[1]), jnp.float32),
+        in_specs=[pl.BlockSpec(memory_space=pltpu.HBM)] * 3,
+        out_specs=pl.BlockSpec(memory_space=pltpu.VMEM),
+        scratch_shapes=[pltpu.VMEM(operand.shape, operand.dtype) for operand in operands]
+        + [pltpu.SemaphoreType.DMA((3,))],
         compiler_params=pltpu.CompilerParams(vmem_limit_bytes=1024 * 1024),
-    )(lists, row_shift, stretch)
+    )(*(pltpu.with_memory_space_constraint(operand, pltpu.HBM) for operand in operands))
 
 
 def unit_kernel(hop, lanes, chips, slabs, resumed, fetched, place, *refs):
@@ -130,12 +140,13 @@
     vmem = pl.BlockSpec(memory_space=pltpu.VMEM)
     shape = (lanes, HALF, TPO, narrow, TR)
     operands = [place] + [ref for source in sources for ref in source]
-    specs = [smem] + [smem, pl.BlockSpec(memory_space=pl.ANY) if fetched else vmem] * len(sources)
+    specs = [smem] + [smem, pl.BlockSpec(memory_space=pltpu.HBM) if fetched else vmem] * len(sources)
     scratch = [
         pltpu.VMEM((lanes, halves * HALF) + shape[2:], jnp.float32),
         pltpu.SMEM((len(sources), halves * HALF * lanes + 1), jnp.int32),
     ]
     if fetched:
+        operands[2] = pltpu.with_memory_space_constraint(operands[2], pltpu.HBM)
         scratch += [pltpu.VMEM((HALF,) + sources[0][1].shape[1:], jnp.bfloat16), pltpu.SemaphoreType.DMA]
     dtype = jnp.float32 if fetched else jnp.bfloat16
     if before is not None:

time: 118 us -> 116 us (0.983)
  waiting for transfers between devices: 11.4 us -> 15.2 us
  local copies, waits for them, and re-layouts: 3.67 us -> 0.09 us
  starting transfers between devices: 34 us -> 31.1 us
    unnamed x14 -> x6, local copies, waits for them, and re-layouts: 3.6 us -> 0.02 us
    ppermute x2, starting transfers between devices: 10 us -> 6.66 us  [body(): second = lax.ppermute(add(second, mine[1]), 'grp', onward)]
    ppermute x2, waiting for transfers between devices: 2.03 us -> 3.9 us  [body(): second = lax.ppermute(add(second, mine[1]), 'grp', onward)]
  transfers between devices with their start and end apart: 11 -> 11, of which waited for: 5 -> 6; matrix products, arithmetic and copies ran while one was open for 2% -> 2% of each run, Pallas kernels for 16% -> 17%
where the time goes in v7:
time: 116 us; the launch traced here: 115 us
  blocking collectives  42.2 us (36%)
  starting transfers between devices  31.1 us (27%)
  Pallas kernels  23.6 us (20%)
  waiting for transfers between devices  15.2 us (13%)
  other arithmetic  1.63 us (1%)
    all_to_all x1, blocking collectives, body(): got = lax.all_to_all(summed, 'ang', split_axis=0, concat_axis=0, tiled=True)  27.9 us
    pallas_call x6, Pallas kernels, units(): pl.pallas_call(functools.partial(unit_kernel, hop, lanes, chips, len(sour...  20.7 us
    all_to_all x1, blocking collectives, body(): lax.all_to_all(copies, 'ang', split_axis=0, concat_axis=0, tiled=True)  14.3 us
    ppermute x2, starting transfers between devices, body(): second = lax.ppermute(add(second, mine[1]), 'grp', onward)  6.66 us
    ppermute x2, starting transfers between devices, body(): first = lax.ppermute(add(first, mine[0]), 'grp', onward)  5.99 us
    ppermute x2, waiting for transfers between devices, body(): first = lax.ppermute(add(first, mine[0]), 'grp', onward)  5.87 us
    ppermute x1, starting transfers between devices, body(): lax.ppermute(units(0, 1, 2, chips, place, [far], early)[0], 'grp', onward)  4.28 us
    ppermute x2, waiting for transfers between devices, body(): second = lax.ppermute(add(second, mine[1]), 'grp', onward)  3.9 us
  transfers between devices with their start and end apart: 11, of which 6 were waited for; matrix products, arithmetic and copies ran while one was open for 2% of the time, Pallas kernels for 17%

profile of v7, /device:TPU:8, one launch (start us, length us, event | category | flops | bytes accessed | tf_op | source)
XLA Modules:
  0.0 115.4 jit_solution(7247657746596903781)
XLA Ops:
  0.6 2.1 %collective-permute-start.1 = (bf16[32,32,1024]{2,1,0:T(8,128)(2,1)}, bf16[32,32,1024]{2,1,0:T(8,128)(2,1)S(1)}, u32[]{:S(2)}, u32[]{:S(2)}) collective-permute-start(bf16[32,32,1024]{2,1,0:T(8,128)(2,1)} %bitcast.25), channel_id=1, source_target_pairs={{0,32},{32,0},{64,96},{96,64},{128,160},{160,128},{192,224},{224,1... | collective-permute-start | bytes 6291464 | tf_op jit(solution)/shard_map/ppermute | solution.py:236
  3.5 2.4 %collective-permute-start = (f32[4,32]{1,0:T(4,128)S(1)}, f32[4,32]{1,0:T(4,128)S(1)}, u32[]{:S(2)}, u32[]{:S(2)}) collective-permute-start(f32[4,32]{1,0:T(4,128)S(1)} %shard_map.77.refs_0_), channel_id=1, source_target_pairs={{0,32},{32,0},{64,96},{96,64},{128,160},{160,128},{192,224},{224,1... | collective-permute-start | bytes 1544 | tf_op jit(solution)/shard_map/ppermute | solution.py:239
  6.0 2.7 %shard_map.78.refs_2_ = f32[2,16,2,32,128]{4,3,2,1,0:T(8,128)S(1)} custom-call(s32[2]{0:T(128)S(1)} %pad_add_fusion.place, f32[4,32]{1,0:T(4,128)S(1)} %shard_map.77.refs_0_, bf16[32,32,1024]{2,1,0:T(8,128)(2,1)} %bitcast.26), custom_call_target="tpu_custom_call" | custom-call | flops 1200000000 | bytes 1000000 | tf_op jit(solution)/shard_map/pallas_call | solution.py:154
  8.7 1.6 %shard_map.79 = bf16[2,16,2,32,128]{4,3,2,1,0:T(8,128)(2,1)S(1)} custom-call(s32[2]{0:T(128)S(1)} %pad_add_fusion.place, f32[4,32]{1,0:T(4,128)S(1)} %collective-permute-done.refs_0_.refs_2_, bf16[32,32,1024]{2,1,0:T(8,128)(2,1)S(1)} %collective-permute-done.1.refs_1_.refs_3_, f32[2,16,2,32,128]{4,3,2,1,0:T(8,128)S(1)} %shard_map.78.refs_2_), custom_call_target="tpu_custom_call" | custom-call | flops 1200000000 | bytes 1000000 | tf_op jit(solution)/shard_map/pallas_call | solution.py:154
  10.3 4.3 %collective-permute-start.2 = (bf16[2,16,2,32,128]{4,3,2,1,0:T(8,128)(2,1)S(1)}, bf16[2,16,2,32,128]{4,3,2,1,0:T(8,128)(2,1)S(1)}, u32[]{:S(2)}, u32[]{:S(2)}) collective-permute-start(bf16[2,16,2,32,128]{4,3,2,1,0:T(8,128)(2,1)S(1)} %shard_map.79), channel_id=1, source_target_pairs={{0,64},{32,480},{64,128},{96,32},{128,192},{160,96},{192,256},{224... | collective-permute-start | bytes 1572872 | tf_op jit(solution)/shard_map/ppermute | solution.py:249
  14.6 4.6 %shard_map.80 = (bf16[2,16,2,32,128]{4,3,2,1,0:T(8,128)(2,1)S(1)}, bf16[2,16,2,32,128]{4,3,2,1,0:T(8,128)(2,1)S(1)}) custom-call(s32[2]{0:T(128)S(1)} %pad_add_fusion.place, f32[4,32]{1,0:T(4,128)S(1)} %shard_map.77.refs_0_, bf16[32,32,1024]{2,1,0:T(8,128)(2,1)S(1)} %bitcast.27, f32[4,32]{1,0:T(4,128)S(1)} %collective-permute-done.refs_0_.refs_2_, ...), custom_call_target="tpu_custom_call" | custom-call | flops 4800000000 | bytes 1000000 | tf_op jit(solution)/shard_map/pallas_call | solution.py:154
  19.2 3.9 %collective-permute-start.6 = (bf16[2,16,2,32,128]{4,3,2,1,0:T(8,128)(2,1)S(1)}, bf16[2,16,2,32,128]{4,3,2,1,0:T(8,128)(2,1)S(1)}, u32[]{:S(2)}, u32[]{:S(2)}) collective-permute-start(bf16[2,16,2,32,128]{4,3,2,1,0:T(8,128)(2,1)S(1)} %get-tuple-element.25), channel_id=1, source_target_pairs={{0,64},{32,480},{64,128},{96,32},{128,192},{160,96},{192,256},{224... | collective-permute-start | bytes 1572872 | tf_op jit(solution)/shard_map/ppermute | solution.py:251
  23.1 2.6 %shard_map.81 = (bf16[1,16,2,32,128]{4,3,2,1,0:T(8,128)(2,1)S(1)}, bf16[1,16,2,32,128]{4,3,2,1,0:T(8,128)(2,1)S(1)}) custom-call(s32[2]{0:T(128)S(1)} %pad_add_fusion.place, f32[4,32]{1,0:T(4,128)S(1)} %shard_map.77.refs_0_, bf16[32,32,1024]{2,1,0:T(8,128)(2,1)S(1)} %bitcast.28, f32[4,32]{1,0:T(4,128)S(1)} %collective-permute-done.refs_0_.refs_2_, ...), custom_call_target="tpu_custom_call" | custom-call | flops 4800000000 | bytes 1000000 | tf_op jit(solution)/shard_map/pallas_call | solution.py:154
  25.7 2.7 %collective-permute-done.2 = bf16[2,16,2,32,128]{4,3,2,1,0:T(8,128)(2,1)S(1)} collective-permute-done((bf16[2,16,2,32,128]{4,3,2,1,0:T(8,128)(2,1)S(1)}, bf16[2,16,2,32,128]{4,3,2,1,0:T(8,128)(2,1)S(1)}, u32[]{:S(2)}, u32[]{:S(2)}) %collective-permute-start.2) | collective-permute-done | bytes 524320 | tf_op jit(solution)/shard_map/ppermute | solution.py:249
  28.6 2.0 %collective-permute-start.3 = (bf16[2,16,2,32,128]{4,3,2,1,0:T(8,128)(2,1)S(1)}, bf16[2,16,2,32,128]{4,3,2,1,0:T(8,128)(2,1)S(1)}, u32[]{:S(2)}, u32[]{:S(2)}) collective-permute-start(bf16[2,16,2,32,128]{4,3,2,1,0:T(8,128)(2,1)S(1)} %add_convert_fusion.4), channel_id=1, source_target_pairs={{0,64},{32,480},{64,128},{96,32},{128,192},{160,96},{192,256},{224... | collective-permute-start | bytes 1572872 | tf_op jit(solution)/shard_map/ppermute | solution.py:255
  30.6 4.6 %shard_map.82 = (bf16[2,16,2,32,128]{4,3,2,1,0:T(8,128)(2,1)S(1)}, bf16[2,16,2,32,128]{4,3,2,1,0:T(8,128)(2,1)S(1)}) custom-call(s32[2]{0:T(128)S(1)} %pad_add_fusion.place, f32[4,32]{1,0:T(4,128)S(1)} %shard_map.77.refs_0_, bf16[32,32,1024]{2,1,0:T(8,128)(2,1)S(1)} %bitcast.29, f32[4,32]{1,0:T(4,128)S(1)} %collective-permute-done.refs_0_.refs_2_, ...), custom_call_target="tpu_custom_call" | custom-call | flops 4800000000 | bytes 1000000 | tf_op jit(solution)/shard_map/pallas_call | solution.py:154
  35.4 4.4 %collective-permute-start.7 = (bf16[2,16,2,32,128]{4,3,2,1,0:T(8,128)(2,1)S(1)}, bf16[2,16,2,32,128]{4,3,2,1,0:T(8,128)(2,1)S(1)}, u32[]{:S(2)}, u32[]{:S(2)}) collective-permute-start(bf16[2,16,2,32,128]{4,3,2,1,0:T(8,128)(2,1)S(1)} %add_convert_fusion.1), channel_id=1, source_target_pairs={{0,64},{32,480},{64,128},{96,32},{128,192},{160,96},{192,256},{224... | collective-permute-start | bytes 1572872 | tf_op jit(solution)/shard_map/ppermute | solution.py:257
  41.1 2.9 %collective-permute-start.4 = (bf16[2,16,2,32,128]{4,3,2,1,0:T(8,128)(2,1)S(1)}, bf16[2,16,2,32,128]{4,3,2,1,0:T(8,128)(2,1)S(1)}, u32[]{:S(2)}, u32[]{:S(2)}) collective-permute-start(bf16[2,16,2,32,128]{4,3,2,1,0:T(8,128)(2,1)S(1)} %add_convert_fusion.3), channel_id=1, source_target_pairs={{0,64},{32,480},{64,128},{96,32},{128,192},{160,96},{192,256},{224... | collective-permute-start | bytes 1572872 | tf_op jit(solution)/shard_map/ppermute | solution.py:258
  44.1 4.6 %shard_map.83 = (bf16[2,16,2,32,128]{4,3,2,1,0:T(8,128)(2,1)S(1)}, bf16[2,16,2,32,128]{4,3,2,1,0:T(8,128)(2,1)S(1)}) custom-call(s32[2]{0:T(128)S(1)} %pad_add_fusion.place, f32[4,32]{1,0:T(4,128)S(1)} %shard_map.77.refs_0_, bf16[32,32,1024]{2,1,0:T(8,128)(2,1)S(1)} %bitcast.30, f32[4,32]{1,0:T(4,128)S(1)} %collective-permute-done.refs_0_.refs_2_, ...), custom_call_target="tpu_custom_call" | custom-call | flops 4800000000 | bytes 1000000 | tf_op jit(solution)/shard_map/pallas_call | solution.py:154
  48.9 2.3 %collective-permute-start.8 = (bf16[2,16,2,32,128]{4,3,2,1,0:T(8,128)(2,1)S(1)}, bf16[2,16,2,32,128]{4,3,2,1,0:T(8,128)(2,1)S(1)}, u32[]{:S(2)}, u32[]{:S(2)}) collective-permute-start(bf16[2,16,2,32,128]{4,3,2,1,0:T(8,128)(2,1)S(1)} %add_convert_fusion), channel_id=1, source_target_pairs={{0,64},{32,480},{64,128},{96,32},{128,192},{160,96},{192,256},{224... | collective-permute-start | bytes 1572872 | tf_op jit(solution)/shard_map/ppermute | solution.py:260
  51.2 2.2 %collective-permute-done.4 = bf16[2,16,2,32,128]{4,3,2,1,0:T(8,128)(2,1)S(1)} collective-permute-done((bf16[2,16,2,32,128]{4,3,2,1,0:T(8,128)(2,1)S(1)}, bf16[2,16,2,32,128]{4,3,2,1,0:T(8,128)(2,1)S(1)}, u32[]{:S(2)}, u32[]{:S(2)}) %collective-permute-start.4) | collective-permute-done | bytes 524320 | tf_op jit(solution)/shard_map/ppermute | solution.py:258
  53.6 3.1 %collective-permute-start.5 = (bf16[2,16,2,32,128]{4,3,2,1,0:T(8,128)(2,1)S(1)}, bf16[2,16,2,32,128]{4,3,2,1,0:T(8,128)(2,1)S(1)}, u32[]{:S(2)}, u32[]{:S(2)}) collective-permute-start(bf16[2,16,2,32,128]{4,3,2,1,0:T(8,128)(2,1)S(1)} %add_convert_fusion.2), channel_id=1, source_target_pairs={{0,64},{32,480},{64,128},{96,32},{128,192},{160,96},{192,256},{224... | collective-permute-start | bytes 1572872 | tf_op jit(solution)/shard_map/ppermute | solution.py:261
  57.4 3.9 %collective-permute-done.8 = bf16[2,16,2,32,128]{4,3,2,1,0:T(8,128)(2,1)S(1)} collective-permute-done((bf16[2,16,2,32,128]{4,3,2,1,0:T(8,128)(2,1)S(1)}, bf16[2,16,2,32,128]{4,3,2,1,0:T(8,128)(2,1)S(1)}, u32[]{:S(2)}, u32[]{:S(2)}) %collective-permute-start.8) | collective-permute-done | bytes 524320 | tf_op jit(solution)/shard_map/ppermute | solution.py:260
  61.3 1.9 %collective-permute-start.9 = (bf16[16,2,32,128]{3,2,1,0:T(8,128)(2,1)S(1)}, bf16[16,2,32,128]{3,2,1,0:T(8,128)(2,1)S(1)}, u32[]{:S(2)}, u32[]{:S(2)}) collective-permute-start(bf16[16,2,32,128]{3,2,1,0:T(8,128)(2,1)S(1)} %get-tuple-element.37), channel_id=1, source_target_pairs={{0,32},{32,0},{64,96},{96,64},{128,160},{160,128},{192,224},{224,1... | collective-permute-start | bytes 786440 | tf_op jit(solution)/shard_map/ppermute | solution.py:262
  63.2 3.7 %collective-permute-done.5 = bf16[2,16,2,32,128]{4,3,2,1,0:T(8,128)(2,1)S(1)} collective-permute-done((bf16[2,16,2,32,128]{4,3,2,1,0:T(8,128)(2,1)S(1)}, bf16[2,16,2,32,128]{4,3,2,1,0:T(8,128)(2,1)S(1)}, u32[]{:S(2)}, u32[]{:S(2)}) %collective-permute-start.5) | collective-permute-done | bytes 524320 | tf_op jit(solution)/shard_map/ppermute | solution.py:261
  66.9 1.9 %collective-permute-start.10 = (bf16[16,2,32,128]{3,2,1,0:T(8,128)(2,1)S(1)}, bf16[16,2,32,128]{3,2,1,0:T(8,128)(2,1)S(1)}, u32[]{:S(2)}, u32[]{:S(2)}) collective-permute-start(bf16[16,2,32,128]{3,2,1,0:T(8,128)(2,1)S(1)} %get-tuple-element.29), channel_id=1, source_target_pairs={{0,32},{32,0},{64,96},{96,64},{128,160},{160,128},{192,224},{224,1... | collective-permute-start | bytes 786440 | tf_op jit(solution)/shard_map/ppermute | solution.py:264
  68.9 1.5 %collective-permute-done.10.other_there = bf16[16,2,32,128]{3,2,1,0:T(8,128)(2,1)S(1)} collective-permute-done((bf16[16,2,32,128]{3,2,1,0:T(8,128)(2,1)S(1)}, bf16[16,2,32,128]{3,2,1,0:T(8,128)(2,1)S(1)}, u32[]{:S(2)}, u32[]{:S(2)}) %collective-permute-start.10) | collective-permute-done | bytes 262176 | tf_op jit(solution)/shard_map/ppermute | solution.py:264
  71.1 27.9 %all_to_all.10.got = bf16[32,2,32,128]{3,2,1,0:T(8,128)(2,1)S(1)} all-to-all(bf16[32,2,32,128]{3,2,1,0:T(8,128)(2,1)S(1)} %shard_map.84), channel_id=1, replica_groups=mesh['grp'=16,'ang'=32] {'ang'}, dimensions={0} | all-to-all | bytes 1048576 | tf_op jit(solution)/shard_map/all_to_all | solution.py:267
  100.5 14.3 %all_to_all.11 = f32[32,8,128]{2,1,0:T(8,128)S(1)} all-to-all(f32[32,8,128]{2,1,0:T(8,128)S(1)} %get-tuple-element.33), channel_id=1, replica_groups=mesh['grp'=16,'ang'=32] {'ang'}, dimensions={0} | all-to-all | bytes 262144 | tf_op jit(solution)/shard_map/all_to_all | solution.py:269
  (26 shorter events, 6.5 us)
Async XLA Ops:
  0.6 56.0 %copy-start = (bf16[1,2,128,1024]{3,2,1,0:T(8,128)(2,1)S(1)}, bf16[1,2,128,1024]{3,2,1,0:T(8,128)(2,1)}, u32[]{:S(2)}) copy-start(bf16[1,2,128,1024]{3,2,1,0:T(8,128)(2,1)} %param.10) | copy-start | bytes 1572868
  0.6 8.0 %collective-permute-start.1 = (bf16[32,32,1024]{2,1,0:T(8,128)(2,1)}, bf16[32,32,1024]{2,1,0:T(8,128)(2,1)S(1)}, u32[]{:S(2)}, u32[]{:S(2)}) collective-permute-start(bf16[32,32,1024]{2,1,0:T(8,128)(2,1)} %bitcast.25), channel_id=1, source_target_pairs={{0,32},{32,0},{64,96},{96,64},{128,160},{160,128},{192,224},{224,1... | collective-permute-start | bytes 6291464 | tf_op jit(solution)/shard_map/ppermute | solution.py:236
  3.5 5.2 %collective-permute-start = (f32[4,32]{1,0:T(4,128)S(1)}, f32[4,32]{1,0:T(4,128)S(1)}, u32[]{:S(2)}, u32[]{:S(2)}) collective-permute-start(f32[4,32]{1,0:T(4,128)S(1)} %shard_map.77.refs_0_), channel_id=1, source_target_pairs={{0,32},{32,0},{64,96},{96,64},{128,160},{160,128},{192,224},{224,1... | collective-permute-start | bytes 1544 | tf_op jit(solution)/shard_map/ppermute | solution.py:239
  8.7 6.0 %copy-start.2 = (bf16[1,32,32,1024]{3,2,1,0:T(8,128)(2,1)S(1)}, bf16[1,32,32,1024]{3,2,1,0:T(8,128)(2,1)}, u32[]{:S(2)}) copy-start(bf16[1,32,32,1024]{3,2,1,0:T(8,128)(2,1)} %param.6) | copy-start | bytes 6291460
  10.3 18.1 %collective-permute-start.2 = (bf16[2,16,2,32,128]{4,3,2,1,0:T(8,128)(2,1)S(1)}, bf16[2,16,2,32,128]{4,3,2,1,0:T(8,128)(2,1)S(1)}, u32[]{:S(2)}, u32[]{:S(2)}) collective-permute-start(bf16[2,16,2,32,128]{4,3,2,1,0:T(8,128)(2,1)S(1)} %shard_map.79), channel_id=1, source_target_pairs={{0,64},{32,480},{64,128},{96,32},{128,192},{160,96},{192,256},{224... | collective-permute-start | bytes 1572872 | tf_op jit(solution)/shard_map/ppermute | solution.py:249
  19.2 16.0 %collective-permute-start.6 = (bf16[2,16,2,32,128]{4,3,2,1,0:T(8,128)(2,1)S(1)}, bf16[2,16,2,32,128]{4,3,2,1,0:T(8,128)(2,1)S(1)}, u32[]{:S(2)}, u32[]{:S(2)}) collective-permute-start(bf16[2,16,2,32,128]{4,3,2,1,0:T(8,128)(2,1)S(1)} %get-tuple-element.25), channel_id=1, source_target_pairs={{0,64},{32,480},{64,128},{96,32},{128,192},{160,96},{192,256},{224... | collective-permute-start | bytes 1572872 | tf_op jit(solution)/shard_map/ppermute | solution.py:251
  28.6 12.3 %collective-permute-start.3 = (bf16[2,16,2,32,128]{4,3,2,1,0:T(8,128)(2,1)S(1)}, bf16[2,16,2,32,128]{4,3,2,1,0:T(8,128)(2,1)S(1)}, u32[]{:S(2)}, u32[]{:S(2)}) collective-permute-start(bf16[2,16,2,32,128]{4,3,2,1,0:T(8,128)(2,1)S(1)} %add_convert_fusion.4), channel_id=1, source_target_pairs={{0,64},{32,480},{64,128},{96,32},{128,192},{160,96},{192,256},{224... | collective-permute-start | bytes 1572872 | tf_op jit(solution)/shard_map/ppermute | solution.py:255
  35.4 13.3 %collective-permute-start.7 = (bf16[2,16,2,32,128]{4,3,2,1,0:T(8,128)(2,1)S(1)}, bf16[2,16,2,32,128]{4,3,2,1,0:T(8,128)(2,1)S(1)}, u32[]{:S(2)}, u32[]{:S(2)}) collective-permute-start(bf16[2,16,2,32,128]{4,3,2,1,0:T(8,128)(2,1)S(1)} %add_convert_fusion.1), channel_id=1, source_target_pairs={{0,64},{32,480},{64,128},{96,32},{128,192},{160,96},{192,256},{224... | collective-permute-start | bytes 1572872 | tf_op jit(solution)/shard_map/ppermute | solution.py:257
  41.1 12.3 %collective-permute-start.4 = (bf16[2,16,2,32,128]{4,3,2,1,0:T(8,128)(2,1)S(1)}, bf16[2,16,2,32,128]{4,3,2,1,0:T(8,128)(2,1)S(1)}, u32[]{:S(2)}, u32[]{:S(2)}) collective-permute-start(bf16[2,16,2,32,128]{4,3,2,1,0:T(8,128)(2,1)S(1)} %add_convert_fusion.3), channel_id=1, source_target_pairs={{0,64},{32,480},{64,128},{96,32},{128,192},{160,96},{192,256},{224... | collective-permute-start | bytes 1572872 | tf_op jit(solution)/shard_map/ppermute | solution.py:258
  48.6 8.0 %copy-start.1 = (bf16[1024,1024]{1,0:T(8,128)(2,1)S(1)}, bf16[1024,1024]{1,0:T(8,128)(2,1)}, u32[]{:S(2)}) copy-start(bf16[1024,1024]{1,0:T(8,128)(2,1)} %constant.36.clone.basis) | copy-start | bytes 6291460
  48.9 12.4 %collective-permute-start.8 = (bf16[2,16,2,32,128]{4,3,2,1,0:T(8,128)(2,1)S(1)}, bf16[2,16,2,32,128]{4,3,2,1,0:T(8,128)(2,1)S(1)}, u32[]{:S(2)}, u32[]{:S(2)}) collective-permute-start(bf16[2,16,2,32,128]{4,3,2,1,0:T(8,128)(2,1)S(1)} %add_convert_fusion), channel_id=1, source_target_pairs={{0,64},{32,480},{64,128},{96,32},{128,192},{160,96},{192,256},{224... | collective-permute-start | bytes 1572872 | tf_op jit(solution)/shard_map/ppermute | solution.py:260
  53.6 13.3 %collective-permute-start.5 = (bf16[2,16,2,32,128]{4,3,2,1,0:T(8,128)(2,1)S(1)}, bf16[2,16,2,32,128]{4,3,2,1,0:T(8,128)(2,1)S(1)}, u32[]{:S(2)}, u32[]{:S(2)}) collective-permute-start(bf16[2,16,2,32,128]{4,3,2,1,0:T(8,128)(2,1)S(1)} %add_convert_fusion.2), channel_id=1, source_target_pairs={{0,64},{32,480},{64,128},{96,32},{128,192},{160,96},{192,256},{224... | collective-permute-start | bytes 1572872 | tf_op jit(solution)/shard_map/ppermute | solution.py:261
  61.3 7.5 %collective-permute-start.9 = (bf16[16,2,32,128]{3,2,1,0:T(8,128)(2,1)S(1)}, bf16[16,2,32,128]{3,2,1,0:T(8,128)(2,1)S(1)}, u32[]{:S(2)}, u32[]{:S(2)}) collective-permute-start(bf16[16,2,32,128]{3,2,1,0:T(8,128)(2,1)S(1)} %get-tuple-element.37), channel_id=1, source_target_pairs={{0,32},{32,0},{64,96},{96,64},{128,160},{160,128},{192,224},{224,1... | collective-permute-start | bytes 786440 | tf_op jit(solution)/shard_map/ppermute | solution.py:262
  66.9 3.4 %collective-permute-start.10 = (bf16[16,2,32,128]{3,2,1,0:T(8,128)(2,1)S(1)}, bf16[16,2,32,128]{3,2,1,0:T(8,128)(2,1)S(1)}, u32[]{:S(2)}, u32[]{:S(2)}) collective-permute-start(bf16[16,2,32,128]{3,2,1,0:T(8,128)(2,1)S(1)} %get-tuple-element.29), channel_id=1, source_target_pairs={{0,32},{32,0},{64,96},{96,64},{128,160},{160,128},{192,224},{224,1... | collective-permute-start | bytes 786440 | tf_op jit(solution)/shard_map/ppermute | solution.py:264

commit v8 on v7

--- a/solution.py
+++ b/solution.py
@@ -16,6 +16,7 @@
 WINDOW = 512
 HALF = 16
 BATCH = 8
+FEW = KF // 2
 UNROLL = 16
 PIECE = 16
 
@@ -71,65 +72,80 @@
     zero = jnp.zeros((PIECE, TR), jnp.bfloat16)
     owner = [(2 * target + (core ^ lane)).astype(jnp.float32) for lane in range(lanes)]
     first_angle = core * HALF
+    size = angles * lanes + 1
     if fetched:
         fetch = pltpu.make_async_copy(sources[0][1].at[pl.ds(first_angle, HALF)], brought, arrived)
         fetch.start()
     total[...] = refs[2 * slabs][...] if resumed else jnp.zeros_like(total)
 
-    def entry(meta, a, lane):
-        k = owner[lane] - meta[0, a]
+    def entry(meta, a, wanted):
+        k = wanted - meta[0, a]
         k = jnp.where(k < 0.0, k + owners, k)
         return jnp.where(k < 0.0, k + owners, k)
 
-    live = []
+    ends = []
     for s, (meta, _) in enumerate(sources):
 
         def note(i, found):
             a = (first_angle + i) & (2 * HALF - 1)
+            count = meta[1, a]
+            few = count < FEW + 1
+            wide, narrow = found
             for lane in range(lanes):
-                listed[s, found] = i * lanes + lane
-                found = found + jnp.where(entry(meta, a, lane) < meta[1, a], 1, 0)
-            return found
-
-        live.append(lax.fori_loop(0, angles, note, jnp.int32(0), unroll=UNROLL))
+                live = entry(meta, a, owner[lane]) < count
+                listed[s, jnp.where(few, size - wide, narrow)] = i * lanes + lane
+                wide = wide + jnp.where(live & few, 1, 0)
+                narrow = narrow + jnp.where(live & ~few, 1, 0)
+            return wide, narrow
+
+        ends.append(
+            lax.fori_loop(0, angles, note, (jnp.int32(0), jnp.int32(0)), unroll=UNROLL)
+        )
 
     if fetched:
         fetch.wait()
 
-    def some(at, carry):
-        for m in range(BATCH):
-            for s, (meta, views) in enumerate(sources):
-                place = at * BATCH + m
-                n = listed[s, jnp.clip(place, 0, jnp.maximum(live[s] - 1, 0))]
-                i, lane = n >> (lanes - 1), n & (lanes - 1)
-                a = (first_angle + i) & (2 * HALF - 1)
-                k = entry(meta, a, 0) if lanes == 1 else jnp.where(
-                    lane == 0, entry(meta, a, 0), entry(meta, a, 1)
-                )
-                slope = meta[3, a]
-                begin = (TR * k - meta[2, a]) * slope
-                block = jnp.clip((begin - 1.0).astype(jnp.int32) >> 7, 0, (SZ - WINDOW) // 128)
-                start = jnp.where(place < live[s], begin - (128 * block).astype(jnp.float32), -1e4)
-                cycle = jnp.where(meta[0, a] + k >= owners, 1, 0)
-                centre = row * slope + start
-                below = jnp.floor(centre)
-                above = centre - below
-                at_below = (1.0 - above).astype(jnp.bfloat16)
-                at_above = above.astype(jnp.bfloat16)
-                gap = (below.astype(jnp.int32) - depth).astype(jnp.int16)
-                pieces = []
-                for p in range(WINDOW // PIECE):
-                    hit = jnp.where(gap == jnp.int16(p * PIECE - 1), at_above, zero)
-                    pieces.append(jnp.where(gap == jnp.int16(p * PIECE), at_below, hit))
-                weights = jnp.concatenate(pieces, axis=0)
-                z0 = pl.multiple_of(block * 128, 128)
-                depths = pl.ds(z0, WINDOW)
-                view = brought[i, :, depths] if fetched else views[a, :, depths]
-                total[lane, i, cycle] += jnp.dot(view, weights, preferred_element_type=jnp.float32)
-        return carry
-
-    most = functools.reduce(jnp.maximum, live)
-    lax.fori_loop(0, lax.div(most + BATCH - 1, BATCH), some, 0)
+    def add_tiles(window, batch, live, at_place):
+        limits = [jnp.maximum(n - 1, 0) for n in live]
+
+        def some(at, carry):
+            for m in range(batch):
+                for s, (meta, views) in enumerate(sources):
+                    place = at * batch + m
+                    n = listed[s, at_place(jnp.minimum(place, limits[s]))]
+                    i, lane = n >> (lanes - 1), n & (lanes - 1)
+                    a = (first_angle + i) & (2 * HALF - 1)
+                    wanted = owner[0] if lanes == 1 else jnp.where(lane == 0, owner[0], owner[1])
+                    k = entry(meta, a, wanted)
+                    begin = (TR * k - meta[2, a]) * meta[3, a]
+                    block = jnp.clip((begin - 1.0).astype(jnp.int32) >> 7, 0, (SZ - window) // 128)
+                    start = jnp.where(
+                        place < live[s], begin - (128 * block).astype(jnp.float32), -1e4
+                    )
+                    cycle = jnp.where(meta[0, a] + k >= owners, 1, 0)
+                    centre = row * meta[3, a] + start
+                    below = jnp.floor(centre)
+                    above = centre - below
+                    at_below = (1.0 - above).astype(jnp.bfloat16)
+                    at_above = above.astype(jnp.bfloat16)
+                    gap = (below.astype(jnp.int32) - depth).astype(jnp.int16)
+                    pieces = []
+                    for p in range(window // PIECE):
+                        hit = jnp.where(gap == jnp.int16(p * PIECE - 1), at_above, zero)
+                        pieces.append(jnp.where(gap == jnp.int16(p * PIECE), at_below, hit))
+                    weights = jnp.concatenate(pieces, axis=0)
+                    depths = pl.ds(pl.multiple_of(block * 128, 128), window)
+                    view = brought[i, :, depths] if fetched else views[a, :, depths]
+                    total[lane, i, cycle] += jnp.dot(
+                        view, weights, preferred_element_type=jnp.float32
+                    )
+            return carry
+
+        most = functools.reduce(jnp.maximum, live)
+        lax.fori_loop(0, lax.div(most + batch - 1, batch), some, 0)
+
+    add_tiles(WINDOW, BATCH // 4, [wide for wide, _ in ends], lambda n: size - n)
+    add_tiles(WINDOW - 128, BATCH, [narrow for _, narrow in ends], lambda n: n)
     for half, out in enumerate(outs):
         out[...] = total[:, half * HALF : (half + 1) * HALF].astype(out.dtype)
 
@@ -143,7 +159,7 @@
     specs = [smem] + [smem, pl.BlockSpec(memory_space=pltpu.HBM) if fetched else vmem] * len(sources)
     scratch = [
         pltpu.VMEM((lanes, halves * HALF) + shape[2:], jnp.float32),
-        pltpu.SMEM((len(sources), halves * HALF * lanes + 1), jnp.int32),
+        pltpu.SMEM((len(sources), halves * HALF * lanes + 2), jnp.int32),
     ]
     if fetched:
         operands[2] = pltpu.with_memory_space_constraint(operands[2], pltpu.HBM)

time: 116 us -> 115 us (level)
  waiting for transfers between devices: 15.2 us -> 17.3 us
  Pallas kernels: 23.6 us -> 22 us
  starting transfers between devices: 31.1 us -> 29.9 us
    pallas_call x6, Pallas kernels: 20.7 us -> 19.1 us  [units(): pl.pallas_call(functools.partial(unit_kernel, hop, lanes, chips, len(sour...]
    ppermute x2, starting transfers between devices: 5.99 us -> 4.54 us  [body(): first = lax.ppermute(add(first, mine[0]), 'grp', onward)]
  transfers between devices with their start and end apart: 11 -> 11, of which waited for: 6 -> 6; matrix products, arithmetic and copies ran while one was open for 2% -> 2% of each run, Pallas kernels for 17% -> 16%
where the time goes in v8:
time: 115 us
  blocking collectives  42.2 us (37%)
  starting transfers between devices  29.9 us (26%)
  Pallas kernels  22 us (19%)
  waiting for transfers between devices  17.3 us (15%)
  other arithmetic  1.63 us (1%)
    all_to_all x1, blocking collectives, body(): got = lax.all_to_all(summed, 'ang', split_axis=0, concat_axis=0, tiled=True)  27.9 us
    pallas_call x6, Pallas kernels, units(): pl.pallas_call(functools.partial(unit_kernel, hop, lanes, chips, len(sour...  19.1 us
    all_to_all x1, blocking collectives, body(): lax.all_to_all(copies, 'ang', split_axis=0, concat_axis=0, tiled=True)  14.3 us
    ppermute x2, waiting for transfers between devices, body(): first = lax.ppermute(add(first, mine[0]), 'grp', onward)  6.69 us
    ppermute x2, starting transfers between devices, body(): second = lax.ppermute(add(second, mine[1]), 'grp', onward)  6.68 us
    ppermute x1, starting transfers between devices, body(): lax.ppermute(units(0, 1, 2, chips, place, [far], early)[0], 'grp', onward)  4.66 us
    ppermute x2, starting transfers between devices, body(): first = lax.ppermute(add(first, mine[0]), 'grp', onward)  4.54 us
    ppermute x1, starting transfers between devices, body(): second = lax.ppermute(mine[1], 'grp', onward)  3.76 us
  transfers between devices with their start and end apart: 11, of which 6 were waited for; matrix products, arithmetic and copies ran while one was open for 2% of the time, Pallas kernels for 16%

profile of v8, /device:TPU:8, one launch (start us, length us, event | category | flops | bytes accessed | tf_op | source)
XLA Modules:
  0.0 114.7 jit_solution(5300949627122251962)
XLA Ops:
  0.6 2.1 %collective-permute-start.1 = (bf16[32,32,1024]{2,1,0:T(8,128)(2,1)}, bf16[32,32,1024]{2,1,0:T(8,128)(2,1)S(1)}, u32[]{:S(2)}, u32[]{:S(2)}) collective-permute-start(bf16[32,32,1024]{2,1,0:T(8,128)(2,1)} %bitcast.25), channel_id=1, source_target_pairs={{0,32},{32,0},{64,96},{96,64},{128,160},{160,128},{192,224},{224,1... | collective-permute-start | bytes 6291464 | tf_op jit(solution)/shard_map/ppermute | solution.py:252
  3.5 2.4 %collective-permute-start = (f32[4,32]{1,0:T(4,128)S(1)}, f32[4,32]{1,0:T(4,128)S(1)}, u32[]{:S(2)}, u32[]{:S(2)}) collective-permute-start(f32[4,32]{1,0:T(4,128)S(1)} %shard_map.77.refs_0_), channel_id=1, source_target_pairs={{0,32},{32,0},{64,96},{96,64},{128,160},{160,128},{192,224},{224,1... | collective-permute-start | bytes 1544 | tf_op jit(solution)/shard_map/ppermute | solution.py:255
  6.0 2.7 %shard_map.78.refs_2_ = f32[2,16,2,32,128]{4,3,2,1,0:T(8,128)S(1)} custom-call(s32[2]{0:T(128)S(1)} %pad_add_fusion.place, f32[4,32]{1,0:T(4,128)S(1)} %shard_map.77.refs_0_, bf16[32,32,1024]{2,1,0:T(8,128)(2,1)} %bitcast.26), custom_call_target="tpu_custom_call" | custom-call | flops 1200000000 | bytes 1000000 | tf_op jit(solution)/shard_map/pallas_call | solution.py:170
  10.2 4.7 %collective-permute-start.2 = (bf16[2,16,2,32,128]{4,3,2,1,0:T(8,128)(2,1)S(1)}, bf16[2,16,2,32,128]{4,3,2,1,0:T(8,128)(2,1)S(1)}, u32[]{:S(2)}, u32[]{:S(2)}) collective-permute-start(bf16[2,16,2,32,128]{4,3,2,1,0:T(8,128)(2,1)S(1)} %shard_map.79), channel_id=1, source_target_pairs={{0,64},{32,480},{64,128},{96,32},{128,192},{160,96},{192,256},{224... | collective-permute-start | bytes 1572872 | tf_op jit(solution)/shard_map/ppermute | solution.py:265
  14.9 4.1 %shard_map.80 = (bf16[2,16,2,32,128]{4,3,2,1,0:T(8,128)(2,1)S(1)}, bf16[2,16,2,32,128]{4,3,2,1,0:T(8,128)(2,1)S(1)}) custom-call(s32[2]{0:T(128)S(1)} %pad_add_fusion.place, f32[4,32]{1,0:T(4,128)S(1)} %shard_map.77.refs_0_, bf16[32,32,1024]{2,1,0:T(8,128)(2,1)S(1)} %bitcast.27, f32[4,32]{1,0:T(4,128)S(1)} %collective-permute-done.refs_0_.refs_2_, ...), custom_call_target="tpu_custom_call" | custom-call | flops 4800000000 | bytes 1000000 | tf_op jit(solution)/shard_map/pallas_call | solution.py:170
  19.0 3.8 %collective-permute-start.6 = (bf16[2,16,2,32,128]{4,3,2,1,0:T(8,128)(2,1)S(1)}, bf16[2,16,2,32,128]{4,3,2,1,0:T(8,128)(2,1)S(1)}, u32[]{:S(2)}, u32[]{:S(2)}) collective-permute-start(bf16[2,16,2,32,128]{4,3,2,1,0:T(8,128)(2,1)S(1)} %get-tuple-element.25), channel_id=1, source_target_pairs={{0,64},{32,480},{64,128},{96,32},{128,192},{160,96},{192,256},{224... | collective-permute-start | bytes 1572872 | tf_op jit(solution)/shard_map/ppermute | solution.py:267
  22.8 2.3 %shard_map.81 = (bf16[1,16,2,32,128]{4,3,2,1,0:T(8,128)(2,1)S(1)}, bf16[1,16,2,32,128]{4,3,2,1,0:T(8,128)(2,1)S(1)}) custom-call(s32[2]{0:T(128)S(1)} %pad_add_fusion.place, f32[4,32]{1,0:T(4,128)S(1)} %shard_map.77.refs_0_, bf16[32,32,1024]{2,1,0:T(8,128)(2,1)S(1)} %bitcast.28, f32[4,32]{1,0:T(4,128)S(1)} %collective-permute-done.refs_0_.refs_2_, ...), custom_call_target="tpu_custom_call" | custom-call | flops 4800000000 | bytes 1000000 | tf_op jit(solution)/shard_map/pallas_call | solution.py:170
  25.1 3.7 %collective-permute-done.2 = bf16[2,16,2,32,128]{4,3,2,1,0:T(8,128)(2,1)S(1)} collective-permute-done((bf16[2,16,2,32,128]{4,3,2,1,0:T(8,128)(2,1)S(1)}, bf16[2,16,2,32,128]{4,3,2,1,0:T(8,128)(2,1)S(1)}, u32[]{:S(2)}, u32[]{:S(2)}) %collective-permute-start.2) | collective-permute-done | bytes 524320 | tf_op jit(solution)/shard_map/ppermute | solution.py:265
  29.0 1.9 %collective-permute-start.3 = (bf16[2,16,2,32,128]{4,3,2,1,0:T(8,128)(2,1)S(1)}, bf16[2,16,2,32,128]{4,3,2,1,0:T(8,128)(2,1)S(1)}, u32[]{:S(2)}, u32[]{:S(2)}) collective-permute-start(bf16[2,16,2,32,128]{4,3,2,1,0:T(8,128)(2,1)S(1)} %add_convert_fusion.4), channel_id=1, source_target_pairs={{0,64},{32,480},{64,128},{96,32},{128,192},{160,96},{192,256},{224... | collective-permute-start | bytes 1572872 | tf_op jit(solution)/shard_map/ppermute | solution.py:271
  30.9 4.1 %shard_map.82 = (bf16[2,16,2,32,128]{4,3,2,1,0:T(8,128)(2,1)S(1)}, bf16[2,16,2,32,128]{4,3,2,1,0:T(8,128)(2,1)S(1)}) custom-call(s32[2]{0:T(128)S(1)} %pad_add_fusion.place, f32[4,32]{1,0:T(4,128)S(1)} %shard_map.77.refs_0_, bf16[32,32,1024]{2,1,0:T(8,128)(2,1)S(1)} %bitcast.29, f32[4,32]{1,0:T(4,128)S(1)} %collective-permute-done.refs_0_.refs_2_, ...), custom_call_target="tpu_custom_call" | custom-call | flops 4800000000 | bytes 1000000 | tf_op jit(solution)/shard_map/pallas_call | solution.py:170
  35.2 4.2 %collective-permute-start.7 = (bf16[2,16,2,32,128]{4,3,2,1,0:T(8,128)(2,1)S(1)}, bf16[2,16,2,32,128]{4,3,2,1,0:T(8,128)(2,1)S(1)}, u32[]{:S(2)}, u32[]{:S(2)}) collective-permute-start(bf16[2,16,2,32,128]{4,3,2,1,0:T(8,128)(2,1)S(1)} %add_convert_fusion.1), channel_id=1, source_target_pairs={{0,64},{32,480},{64,128},{96,32},{128,192},{160,96},{192,256},{224... | collective-permute-start | bytes 1572872 | tf_op jit(solution)/shard_map/ppermute | solution.py:273
  39.4 1.8 %collective-permute-done.3 = bf16[2,16,2,32,128]{4,3,2,1,0:T(8,128)(2,1)S(1)} collective-permute-done((bf16[2,16,2,32,128]{4,3,2,1,0:T(8,128)(2,1)S(1)}, bf16[2,16,2,32,128]{4,3,2,1,0:T(8,128)(2,1)S(1)}, u32[]{:S(2)}, u32[]{:S(2)}) %collective-permute-start.3) | collective-permute-done | bytes 524320 | tf_op jit(solution)/shard_map/ppermute | solution.py:271
  41.5 2.2 %collective-permute-start.4 = (bf16[2,16,2,32,128]{4,3,2,1,0:T(8,128)(2,1)S(1)}, bf16[2,16,2,32,128]{4,3,2,1,0:T(8,128)(2,1)S(1)}, u32[]{:S(2)}, u32[]{:S(2)}) collective-permute-start(bf16[2,16,2,32,128]{4,3,2,1,0:T(8,128)(2,1)S(1)} %add_convert_fusion.3), channel_id=1, source_target_pairs={{0,64},{32,480},{64,128},{96,32},{128,192},{160,96},{192,256},{224... | collective-permute-start | bytes 1572872 | tf_op jit(solution)/shard_map/ppermute | solution.py:274
  43.6 4.4 %shard_map.83 = (bf16[2,16,2,32,128]{4,3,2,1,0:T(8,128)(2,1)S(1)}, bf16[2,16,2,32,128]{4,3,2,1,0:T(8,128)(2,1)S(1)}) custom-call(s32[2]{0:T(128)S(1)} %pad_add_fusion.place, f32[4,32]{1,0:T(4,128)S(1)} %shard_map.77.refs_0_, bf16[32,32,1024]{2,1,0:T(8,128)(2,1)S(1)} %bitcast.30, f32[4,32]{1,0:T(4,128)S(1)} %collective-permute-done.refs_0_.refs_2_, ...), custom_call_target="tpu_custom_call" | custom-call | flops 4800000000 | bytes 1000000 | tf_op jit(solution)/shard_map/pallas_call | solution.py:170
  48.2 2.5 %collective-permute-start.8 = (bf16[2,16,2,32,128]{4,3,2,1,0:T(8,128)(2,1)S(1)}, bf16[2,16,2,32,128]{4,3,2,1,0:T(8,128)(2,1)S(1)}, u32[]{:S(2)}, u32[]{:S(2)}) collective-permute-start(bf16[2,16,2,32,128]{4,3,2,1,0:T(8,128)(2,1)S(1)} %add_convert_fusion), channel_id=1, source_target_pairs={{0,64},{32,480},{64,128},{96,32},{128,192},{160,96},{192,256},{224... | collective-permute-start | bytes 1572872 | tf_op jit(solution)/shard_map/ppermute | solution.py:276
  50.7 3.0 %collective-permute-done.4 = bf16[2,16,2,32,128]{4,3,2,1,0:T(8,128)(2,1)S(1)} collective-permute-done((bf16[2,16,2,32,128]{4,3,2,1,0:T(8,128)(2,1)S(1)}, bf16[2,16,2,32,128]{4,3,2,1,0:T(8,128)(2,1)S(1)}, u32[]{:S(2)}, u32[]{:S(2)}) %collective-permute-start.4) | collective-permute-done | bytes 524320 | tf_op jit(solution)/shard_map/ppermute | solution.py:274
  53.9 2.4 %collective-permute-start.5 = (bf16[2,16,2,32,128]{4,3,2,1,0:T(8,128)(2,1)S(1)}, bf16[2,16,2,32,128]{4,3,2,1,0:T(8,128)(2,1)S(1)}, u32[]{:S(2)}, u32[]{:S(2)}) collective-permute-start(bf16[2,16,2,32,128]{4,3,2,1,0:T(8,128)(2,1)S(1)} %add_convert_fusion.2), channel_id=1, source_target_pairs={{0,64},{32,480},{64,128},{96,32},{128,192},{160,96},{192,256},{224... | collective-permute-start | bytes 1572872 | tf_op jit(solution)/shard_map/ppermute | solution.py:277
  57.1 3.6 %collective-permute-done.8 = bf16[2,16,2,32,128]{4,3,2,1,0:T(8,128)(2,1)S(1)} collective-permute-done((bf16[2,16,2,32,128]{4,3,2,1,0:T(8,128)(2,1)S(1)}, bf16[2,16,2,32,128]{4,3,2,1,0:T(8,128)(2,1)S(1)}, u32[]{:S(2)}, u32[]{:S(2)}) %collective-permute-start.8) | collective-permute-done | bytes 524320 | tf_op jit(solution)/shard_map/ppermute | solution.py:276
  60.7 1.9 %collective-permute-start.9 = (bf16[16,2,32,128]{3,2,1,0:T(8,128)(2,1)S(1)}, bf16[16,2,32,128]{3,2,1,0:T(8,128)(2,1)S(1)}, u32[]{:S(2)}, u32[]{:S(2)}) collective-permute-start(bf16[16,2,32,128]{3,2,1,0:T(8,128)(2,1)S(1)} %get-tuple-element.37), channel_id=1, source_target_pairs={{0,32},{32,0},{64,96},{96,64},{128,160},{160,128},{192,224},{224,1... | collective-permute-start | bytes 786440 | tf_op jit(solution)/shard_map/ppermute | solution.py:278
  62.6 3.7 %collective-permute-done.5 = bf16[2,16,2,32,128]{4,3,2,1,0:T(8,128)(2,1)S(1)} collective-permute-done((bf16[2,16,2,32,128]{4,3,2,1,0:T(8,128)(2,1)S(1)}, bf16[2,16,2,32,128]{4,3,2,1,0:T(8,128)(2,1)S(1)}, u32[]{:S(2)}, u32[]{:S(2)}) %collective-permute-start.5) | collective-permute-done | bytes 524320 | tf_op jit(solution)/shard_map/ppermute | solution.py:277
  66.3 1.9 %collective-permute-start.10 = (bf16[16,2,32,128]{3,2,1,0:T(8,128)(2,1)S(1)}, bf16[16,2,32,128]{3,2,1,0:T(8,128)(2,1)S(1)}, u32[]{:S(2)}, u32[]{:S(2)}) collective-permute-start(bf16[16,2,32,128]{3,2,1,0:T(8,128)(2,1)S(1)} %get-tuple-element.29), channel_id=1, source_target_pairs={{0,32},{32,0},{64,96},{96,64},{128,160},{160,128},{192,224},{224,1... | collective-permute-start | bytes 786440 | tf_op jit(solution)/shard_map/ppermute | solution.py:280
  68.2 1.5 %collective-permute-done.10.other_there = bf16[16,2,32,128]{3,2,1,0:T(8,128)(2,1)S(1)} collective-permute-done((bf16[16,2,32,128]{3,2,1,0:T(8,128)(2,1)S(1)}, bf16[16,2,32,128]{3,2,1,0:T(8,128)(2,1)S(1)}, u32[]{:S(2)}, u32[]{:S(2)}) %collective-permute-start.10) | collective-permute-done | bytes 262176 | tf_op jit(solution)/shard_map/ppermute | solution.py:280
  70.5 27.9 %all_to_all.10.got = bf16[32,2,32,128]{3,2,1,0:T(8,128)(2,1)S(1)} all-to-all(bf16[32,2,32,128]{3,2,1,0:T(8,128)(2,1)S(1)} %shard_map.84), channel_id=1, replica_groups=mesh['grp'=16,'ang'=32] {'ang'}, dimensions={0} | all-to-all | bytes 1048576 | tf_op jit(solution)/shard_map/all_to_all | solution.py:283
  99.8 14.3 %all_to_all.11 = f32[32,8,128]{2,1,0:T(8,128)S(1)} all-to-all(f32[32,8,128]{2,1,0:T(8,128)S(1)} %get-tuple-element.33), channel_id=1, replica_groups=mesh['grp'=16,'ang'=32] {'ang'}, dimensions={0} | all-to-all | bytes 262144 | tf_op jit(solution)/shard_map/all_to_all | solution.py:285
  (26 shorter events, 6.8 us)
Async XLA Ops:
  0.6 55.7 %copy-start = (bf16[1,2,128,1024]{3,2,1,0:T(8,128)(2,1)S(1)}, bf16[1,2,128,1024]{3,2,1,0:T(8,128)(2,1)}, u32[]{:S(2)}) copy-start(bf16[1,2,128,1024]{3,2,1,0:T(8,128)(2,1)} %param.10) | copy-start | bytes 1572868
  0.6 8.1 %collective-permute-start.1 = (bf16[32,32,1024]{2,1,0:T(8,128)(2,1)}, bf16[32,32,1024]{2,1,0:T(8,128)(2,1)S(1)}, u32[]{:S(2)}, u32[]{:S(2)}) collective-permute-start(bf16[32,32,1024]{2,1,0:T(8,128)(2,1)} %bitcast.25), channel_id=1, source_target_pairs={{0,32},{32,0},{64,96},{96,64},{128,160},{160,128},{192,224},{224,1... | collective-permute-start | bytes 6291464 | tf_op jit(solution)/shard_map/ppermute | solution.py:252
  3.5 5.3 %collective-permute-start = (f32[4,32]{1,0:T(4,128)S(1)}, f32[4,32]{1,0:T(4,128)S(1)}, u32[]{:S(2)}, u32[]{:S(2)}) collective-permute-start(f32[4,32]{1,0:T(4,128)S(1)} %shard_map.77.refs_0_), channel_id=1, source_target_pairs={{0,32},{32,0},{64,96},{96,64},{128,160},{160,128},{192,224},{224,1... | collective-permute-start | bytes 1544 | tf_op jit(solution)/shard_map/ppermute | solution.py:255
  8.7 6.2 %copy-start.2 = (bf16[1,32,32,1024]{3,2,1,0:T(8,128)(2,1)S(1)}, bf16[1,32,32,1024]{3,2,1,0:T(8,128)(2,1)}, u32[]{:S(2)}) copy-start(bf16[1,32,32,1024]{3,2,1,0:T(8,128)(2,1)} %param.6) | copy-start | bytes 6291460
  10.2 18.6 %collective-permute-start.2 = (bf16[2,16,2,32,128]{4,3,2,1,0:T(8,128)(2,1)S(1)}, bf16[2,16,2,32,128]{4,3,2,1,0:T(8,128)(2,1)S(1)}, u32[]{:S(2)}, u32[]{:S(2)}) collective-permute-start(bf16[2,16,2,32,128]{4,3,2,1,0:T(8,128)(2,1)S(1)} %shard_map.79), channel_id=1, source_target_pairs={{0,64},{32,480},{64,128},{96,32},{128,192},{160,96},{192,256},{224... | collective-permute-start | bytes 1572872 | tf_op jit(solution)/shard_map/ppermute | solution.py:265
  19.0 16.0 %collective-permute-start.6 = (bf16[2,16,2,32,128]{4,3,2,1,0:T(8,128)(2,1)S(1)}, bf16[2,16,2,32,128]{4,3,2,1,0:T(8,128)(2,1)S(1)}, u32[]{:S(2)}, u32[]{:S(2)}) collective-permute-start(bf16[2,16,2,32,128]{4,3,2,1,0:T(8,128)(2,1)S(1)} %get-tuple-element.25), channel_id=1, source_target_pairs={{0,64},{32,480},{64,128},{96,32},{128,192},{160,96},{192,256},{224... | collective-permute-start | bytes 1572872 | tf_op jit(solution)/shard_map/ppermute | solution.py:267
  29.0 12.3 %collective-permute-start.3 = (bf16[2,16,2,32,128]{4,3,2,1,0:T(8,128)(2,1)S(1)}, bf16[2,16,2,32,128]{4,3,2,1,0:T(8,128)(2,1)S(1)}, u32[]{:S(2)}, u32[]{:S(2)}) collective-permute-start(bf16[2,16,2,32,128]{4,3,2,1,0:T(8,128)(2,1)S(1)} %add_convert_fusion.4), channel_id=1, source_target_pairs={{0,64},{32,480},{64,128},{96,32},{128,192},{160,96},{192,256},{224... | collective-permute-start | bytes 1572872 | tf_op jit(solution)/shard_map/ppermute | solution.py:271
  35.2 12.8 %collective-permute-start.7 = (bf16[2,16,2,32,128]{4,3,2,1,0:T(8,128)(2,1)S(1)}, bf16[2,16,2,32,128]{4,3,2,1,0:T(8,128)(2,1)S(1)}, u32[]{:S(2)}, u32[]{:S(2)}) collective-permute-start(bf16[2,16,2,32,128]{4,3,2,1,0:T(8,128)(2,1)S(1)} %add_convert_fusion.1), channel_id=1, source_target_pairs={{0,64},{32,480},{64,128},{96,32},{128,192},{160,96},{192,256},{224... | collective-permute-start | bytes 1572872 | tf_op jit(solution)/shard_map/ppermute | solution.py:273
  41.5 12.3 %collective-permute-start.4 = (bf16[2,16,2,32,128]{4,3,2,1,0:T(8,128)(2,1)S(1)}, bf16[2,16,2,32,128]{4,3,2,1,0:T(8,128)(2,1)S(1)}, u32[]{:S(2)}, u32[]{:S(2)}) collective-permute-start(bf16[2,16,2,32,128]{4,3,2,1,0:T(8,128)(2,1)S(1)} %add_convert_fusion.3), channel_id=1, source_target_pairs={{0,64},{32,480},{64,128},{96,32},{128,192},{160,96},{192,256},{224... | collective-permute-start | bytes 1572872 | tf_op jit(solution)/shard_map/ppermute | solution.py:274
  48.0 8.3 %copy-start.1 = (bf16[1024,1024]{1,0:T(8,128)(2,1)S(1)}, bf16[1024,1024]{1,0:T(8,128)(2,1)}, u32[]{:S(2)}) copy-start(bf16[1024,1024]{1,0:T(8,128)(2,1)} %constant.36.clone.basis) | copy-start | bytes 6291460
  48.2 12.4 %collective-permute-start.8 = (bf16[2,16,2,32,128]{4,3,2,1,0:T(8,128)(2,1)S(1)}, bf16[2,16,2,32,128]{4,3,2,1,0:T(8,128)(2,1)S(1)}, u32[]{:S(2)}, u32[]{:S(2)}) collective-permute-start(bf16[2,16,2,32,128]{4,3,2,1,0:T(8,128)(2,1)S(1)} %add_convert_fusion), channel_id=1, source_target_pairs={{0,64},{32,480},{64,128},{96,32},{128,192},{160,96},{192,256},{224... | collective-permute-start | bytes 1572872 | tf_op jit(solution)/shard_map/ppermute | solution.py:276
  53.9 12.3 %collective-permute-start.5 = (bf16[2,16,2,32,128]{4,3,2,1,0:T(8,128)(2,1)S(1)}, bf16[2,16,2,32,128]{4,3,2,1,0:T(8,128)(2,1)S(1)}, u32[]{:S(2)}, u32[]{:S(2)}) collective-permute-start(bf16[2,16,2,32,128]{4,3,2,1,0:T(8,128)(2,1)S(1)} %add_convert_fusion.2), channel_id=1, source_target_pairs={{0,64},{32,480},{64,128},{96,32},{128,192},{160,96},{192,256},{224... | collective-permute-start | bytes 1572872 | tf_op jit(solution)/shard_map/ppermute | solution.py:277
  60.7 7.5 %collective-permute-start.9 = (bf16[16,2,32,128]{3,2,1,0:T(8,128)(2,1)S(1)}, bf16[16,2,32,128]{3,2,1,0:T(8,128)(2,1)S(1)}, u32[]{:S(2)}, u32[]{:S(2)}) collective-permute-start(bf16[16,2,32,128]{3,2,1,0:T(8,128)(2,1)S(1)} %get-tuple-element.37), channel_id=1, source_target_pairs={{0,32},{32,0},{64,96},{96,64},{128,160},{160,128},{192,224},{224,1... | collective-permute-start | bytes 786440 | tf_op jit(solution)/shard_map/ppermute | solution.py:278
  66.3 3.4 %collective-permute-start.10 = (bf16[16,2,32,128]{3,2,1,0:T(8,128)(2,1)S(1)}, bf16[16,2,32,128]{3,2,1,0:T(8,128)(2,1)S(1)}, u32[]{:S(2)}, u32[]{:S(2)}) collective-permute-start(bf16[16,2,32,128]{3,2,1,0:T(8,128)(2,1)S(1)} %get-tuple-element.29), channel_id=1, source_target_pairs={{0,32},{32,0},{64,96},{96,64},{128,160},{160,128},{192,224},{224,1... | collective-permute-start | bytes 786440 | tf_op jit(solution)/shard_map/ppermute | solution.py:280

commit v9 on v8

--- a/solution.py
+++ b/solution.py
@@ -113,6 +113,7 @@
                 for s, (meta, views) in enumerate(sources):
                     place = at * batch + m
                     n = listed[s, at_place(jnp.minimum(place, limits[s]))]
+                    n = jnp.where(place < live[s], n, 0)
                     i, lane = n >> (lanes - 1), n & (lanes - 1)
                     a = (first_angle + i) & (2 * HALF - 1)
                     wanted = owner[0] if lanes == 1 else jnp.where(lane == 0, owner[0], owner[1])

time: 115 us -> 115 us (level)
  waiting for transfers between devices: 17.3 us -> 12.1 us
  starting transfers between devices: 29.9 us -> 34.2 us
    ppermute x2, starting transfers between devices: 6.68 us -> 9.21 us  [body(): second = lax.ppermute(add(second, mine[1]), 'grp', onward)]
    ppermute x2, waiting for transfers between devices: 6.69 us -> 5.18 us  [body(): first = lax.ppermute(add(first, mine[0]), 'grp', onward)]
    ppermute x1, waiting for transfers between devices: 1.82 us -> 0.45 us  [body(): first = lax.ppermute(sending, 'grp', onward)]
    ppermute x2, waiting for transfers between devices: 3.58 us -> 2.26 us  [body(): second = lax.ppermute(add(second, mine[1]), 'grp', onward)]
  transfers between devices with their start and end apart: 11 -> 11, of which waited for: 6 -> 6; matrix products, arithmetic and copies ran while one was open for 2% -> 2% of each run, Pallas kernels for 16% -> 17%
where the time goes in v9:
time: 115 us
  blocking collectives  42.2 us (37%)
  starting transfers between devices  34.2 us (30%)
  Pallas kernels  22.8 us (20%)
  waiting for transfers between devices  12.1 us (11%)
  other arithmetic  1.64 us (1%)
    all_to_all x1, blocking collectives, body(): got = lax.all_to_all(summed, 'ang', split_axis=0, concat_axis=0, tiled=True)  27.9 us
    pallas_call x6, Pallas kernels, units(): pl.pallas_call(functools.partial(unit_kernel, hop, lanes, chips, len(sour...  19.9 us
    all_to_all x1, blocking collectives, body(): lax.all_to_all(copies, 'ang', split_axis=0, concat_axis=0, tiled=True)  14.3 us
    ppermute x2, starting transfers between devices, body(): second = lax.ppermute(add(second, mine[1]), 'grp', onward)  9.21 us
    ppermute x2, starting transfers between devices, body(): first = lax.ppermute(add(first, mine[0]), 'grp', onward)  5.67 us
    ppermute x1, starting transfers between devices, body(): lax.ppermute(units(0, 1, 2, chips, place, [far], early)[0], 'grp', onward)  5.24 us
    ppermute x2, waiting for transfers between devices, body(): first = lax.ppermute(add(first, mine[0]), 'grp', onward)  5.18 us
    ppermute x1, starting transfers between devices, body(): second = lax.ppermute(mine[1], 'grp', onward)  3.9 us
  transfers between devices with their start and end apart: 11, of which 6 were waited for; matrix products, arithmetic and copies ran while one was open for 2% of the time, Pallas kernels for 17%

profile of v9, /device:TPU:8, one launch (start us, length us, event | category | flops | bytes accessed | tf_op | source)
XLA Modules:
  0.0 114.7 jit_solution(3832462518024072990)
XLA Ops:
  0.6 2.1 %collective-permute-start.1 = (bf16[32,32,1024]{2,1,0:T(8,128)(2,1)}, bf16[32,32,1024]{2,1,0:T(8,128)(2,1)S(1)}, u32[]{:S(2)}, u32[]{:S(2)}) collective-permute-start(bf16[32,32,1024]{2,1,0:T(8,128)(2,1)} %bitcast.25), channel_id=1, source_target_pairs={{0,32},{32,0},{64,96},{96,64},{128,160},{160,128},{192,224},{224,1... | collective-permute-start | bytes 6291464 | tf_op jit(solution)/shard_map/ppermute | solution.py:253
  3.5 2.4 %collective-permute-start = (f32[4,32]{1,0:T(4,128)S(1)}, f32[4,32]{1,0:T(4,128)S(1)}, u32[]{:S(2)}, u32[]{:S(2)}) collective-permute-start(f32[4,32]{1,0:T(4,128)S(1)} %shard_map.77.refs_0_), channel_id=1, source_target_pairs={{0,32},{32,0},{64,96},{96,64},{128,160},{160,128},{192,224},{224,1... | collective-permute-start | bytes 1544 | tf_op jit(solution)/shard_map/ppermute | solution.py:256
  6.0 2.6 %shard_map.78.refs_2_ = f32[2,16,2,32,128]{4,3,2,1,0:T(8,128)S(1)} custom-call(s32[2]{0:T(128)S(1)} %pad_add_fusion.place, f32[4,32]{1,0:T(4,128)S(1)} %shard_map.77.refs_0_, bf16[32,32,1024]{2,1,0:T(8,128)(2,1)} %bitcast.26), custom_call_target="tpu_custom_call" | custom-call | flops 1200000000 | bytes 1000000 | tf_op jit(solution)/shard_map/pallas_call | solution.py:171
  9.8 5.2 %collective-permute-start.2 = (bf16[2,16,2,32,128]{4,3,2,1,0:T(8,128)(2,1)S(1)}, bf16[2,16,2,32,128]{4,3,2,1,0:T(8,128)(2,1)S(1)}, u32[]{:S(2)}, u32[]{:S(2)}) collective-permute-start(bf16[2,16,2,32,128]{4,3,2,1,0:T(8,128)(2,1)S(1)} %shard_map.79), channel_id=1, source_target_pairs={{0,64},{32,480},{64,128},{96,32},{128,192},{160,96},{192,256},{224... | collective-permute-start | bytes 1572872 | tf_op jit(solution)/shard_map/ppermute | solution.py:266
  15.1 4.4 %shard_map.80 = (bf16[2,16,2,32,128]{4,3,2,1,0:T(8,128)(2,1)S(1)}, bf16[2,16,2,32,128]{4,3,2,1,0:T(8,128)(2,1)S(1)}) custom-call(s32[2]{0:T(128)S(1)} %pad_add_fusion.place, f32[4,32]{1,0:T(4,128)S(1)} %shard_map.77.refs_0_, bf16[32,32,1024]{2,1,0:T(8,128)(2,1)S(1)} %bitcast.27, f32[4,32]{1,0:T(4,128)S(1)} %collective-permute-done.refs_0_.refs_2_, ...), custom_call_target="tpu_custom_call" | custom-call | flops 4800000000 | bytes 1000000 | tf_op jit(solution)/shard_map/pallas_call | solution.py:171
  19.5 3.9 %collective-permute-start.6 = (bf16[2,16,2,32,128]{4,3,2,1,0:T(8,128)(2,1)S(1)}, bf16[2,16,2,32,128]{4,3,2,1,0:T(8,128)(2,1)S(1)}, u32[]{:S(2)}, u32[]{:S(2)}) collective-permute-start(bf16[2,16,2,32,128]{4,3,2,1,0:T(8,128)(2,1)S(1)} %get-tuple-element.25), channel_id=1, source_target_pairs={{0,64},{32,480},{64,128},{96,32},{128,192},{160,96},{192,256},{224... | collective-permute-start | bytes 1572872 | tf_op jit(solution)/shard_map/ppermute | solution.py:268
  23.4 2.5 %shard_map.81 = (bf16[1,16,2,32,128]{4,3,2,1,0:T(8,128)(2,1)S(1)}, bf16[1,16,2,32,128]{4,3,2,1,0:T(8,128)(2,1)S(1)}) custom-call(s32[2]{0:T(128)S(1)} %pad_add_fusion.place, f32[4,32]{1,0:T(4,128)S(1)} %shard_map.77.refs_0_, bf16[32,32,1024]{2,1,0:T(8,128)(2,1)S(1)} %bitcast.28, f32[4,32]{1,0:T(4,128)S(1)} %collective-permute-done.refs_0_.refs_2_, ...), custom_call_target="tpu_custom_call" | custom-call | flops 4800000000 | bytes 1000000 | tf_op jit(solution)/shard_map/pallas_call | solution.py:171
  26.0 2.7 %collective-permute-done.2 = bf16[2,16,2,32,128]{4,3,2,1,0:T(8,128)(2,1)S(1)} collective-permute-done((bf16[2,16,2,32,128]{4,3,2,1,0:T(8,128)(2,1)S(1)}, bf16[2,16,2,32,128]{4,3,2,1,0:T(8,128)(2,1)S(1)}, u32[]{:S(2)}, u32[]{:S(2)}) %collective-permute-start.2) | collective-permute-done | bytes 524320 | tf_op jit(solution)/shard_map/ppermute | solution.py:266
  28.9 1.9 %collective-permute-start.3 = (bf16[2,16,2,32,128]{4,3,2,1,0:T(8,128)(2,1)S(1)}, bf16[2,16,2,32,128]{4,3,2,1,0:T(8,128)(2,1)S(1)}, u32[]{:S(2)}, u32[]{:S(2)}) collective-permute-start(bf16[2,16,2,32,128]{4,3,2,1,0:T(8,128)(2,1)S(1)} %add_convert_fusion.4), channel_id=1, source_target_pairs={{0,64},{32,480},{64,128},{96,32},{128,192},{160,96},{192,256},{224... | collective-permute-start | bytes 1572872 | tf_op jit(solution)/shard_map/ppermute | solution.py:272
  30.8 4.4 %shard_map.82 = (bf16[2,16,2,32,128]{4,3,2,1,0:T(8,128)(2,1)S(1)}, bf16[2,16,2,32,128]{4,3,2,1,0:T(8,128)(2,1)S(1)}) custom-call(s32[2]{0:T(128)S(1)} %pad_add_fusion.place, f32[4,32]{1,0:T(4,128)S(1)} %shard_map.77.refs_0_, bf16[32,32,1024]{2,1,0:T(8,128)(2,1)S(1)} %bitcast.29, f32[4,32]{1,0:T(4,128)S(1)} %collective-permute-done.refs_0_.refs_2_, ...), custom_call_target="tpu_custom_call" | custom-call | flops 4800000000 | bytes 1000000 | tf_op jit(solution)/shard_map/pallas_call | solution.py:171
  35.4 5.3 %collective-permute-start.7 = (bf16[2,16,2,32,128]{4,3,2,1,0:T(8,128)(2,1)S(1)}, bf16[2,16,2,32,128]{4,3,2,1,0:T(8,128)(2,1)S(1)}, u32[]{:S(2)}, u32[]{:S(2)}) collective-permute-start(bf16[2,16,2,32,128]{4,3,2,1,0:T(8,128)(2,1)S(1)} %add_convert_fusion.1), channel_id=1, source_target_pairs={{0,64},{32,480},{64,128},{96,32},{128,192},{160,96},{192,256},{224... | collective-permute-start | bytes 1572872 | tf_op jit(solution)/shard_map/ppermute | solution.py:274
  41.4 1.9 %collective-permute-start.4 = (bf16[2,16,2,32,128]{4,3,2,1,0:T(8,128)(2,1)S(1)}, bf16[2,16,2,32,128]{4,3,2,1,0:T(8,128)(2,1)S(1)}, u32[]{:S(2)}, u32[]{:S(2)}) collective-permute-start(bf16[2,16,2,32,128]{4,3,2,1,0:T(8,128)(2,1)S(1)} %add_convert_fusion.3), channel_id=1, source_target_pairs={{0,64},{32,480},{64,128},{96,32},{128,192},{160,96},{192,256},{224... | collective-permute-start | bytes 1572872 | tf_op jit(solution)/shard_map/ppermute | solution.py:275
  43.3 4.7 %shard_map.83 = (bf16[2,16,2,32,128]{4,3,2,1,0:T(8,128)(2,1)S(1)}, bf16[2,16,2,32,128]{4,3,2,1,0:T(8,128)(2,1)S(1)}) custom-call(s32[2]{0:T(128)S(1)} %pad_add_fusion.place, f32[4,32]{1,0:T(4,128)S(1)} %shard_map.77.refs_0_, bf16[32,32,1024]{2,1,0:T(8,128)(2,1)S(1)} %bitcast.30, f32[4,32]{1,0:T(4,128)S(1)} %collective-permute-done.refs_0_.refs_2_, ...), custom_call_target="tpu_custom_call" | custom-call | flops 4800000000 | bytes 1000000 | tf_op jit(solution)/shard_map/pallas_call | solution.py:171
  48.2 3.9 %collective-permute-start.8 = (bf16[2,16,2,32,128]{4,3,2,1,0:T(8,128)(2,1)S(1)}, bf16[2,16,2,32,128]{4,3,2,1,0:T(8,128)(2,1)S(1)}, u32[]{:S(2)}, u32[]{:S(2)}) collective-permute-start(bf16[2,16,2,32,128]{4,3,2,1,0:T(8,128)(2,1)S(1)} %add_convert_fusion), channel_id=1, source_target_pairs={{0,64},{32,480},{64,128},{96,32},{128,192},{160,96},{192,256},{224... | collective-permute-start | bytes 1572872 | tf_op jit(solution)/shard_map/ppermute | solution.py:277
  52.1 1.5 %collective-permute-done.4 = bf16[2,16,2,32,128]{4,3,2,1,0:T(8,128)(2,1)S(1)} collective-permute-done((bf16[2,16,2,32,128]{4,3,2,1,0:T(8,128)(2,1)S(1)}, bf16[2,16,2,32,128]{4,3,2,1,0:T(8,128)(2,1)S(1)}, u32[]{:S(2)}, u32[]{:S(2)}) %collective-permute-start.4) | collective-permute-done | bytes 524320 | tf_op jit(solution)/shard_map/ppermute | solution.py:275
  53.9 3.8 %collective-permute-start.5 = (bf16[2,16,2,32,128]{4,3,2,1,0:T(8,128)(2,1)S(1)}, bf16[2,16,2,32,128]{4,3,2,1,0:T(8,128)(2,1)S(1)}, u32[]{:S(2)}, u32[]{:S(2)}) collective-permute-start(bf16[2,16,2,32,128]{4,3,2,1,0:T(8,128)(2,1)S(1)} %add_convert_fusion.2), channel_id=1, source_target_pairs={{0,64},{32,480},{64,128},{96,32},{128,192},{160,96},{192,256},{224... | collective-permute-start | bytes 1572872 | tf_op jit(solution)/shard_map/ppermute | solution.py:278
  58.3 2.3 %collective-permute-done.8 = bf16[2,16,2,32,128]{4,3,2,1,0:T(8,128)(2,1)S(1)} collective-permute-done((bf16[2,16,2,32,128]{4,3,2,1,0:T(8,128)(2,1)S(1)}, bf16[2,16,2,32,128]{4,3,2,1,0:T(8,128)(2,1)S(1)}, u32[]{:S(2)}, u32[]{:S(2)}) %collective-permute-start.8) | collective-permute-done | bytes 524320 | tf_op jit(solution)/shard_map/ppermute | solution.py:277
  60.6 1.9 %collective-permute-start.9 = (bf16[16,2,32,128]{3,2,1,0:T(8,128)(2,1)S(1)}, bf16[16,2,32,128]{3,2,1,0:T(8,128)(2,1)S(1)}, u32[]{:S(2)}, u32[]{:S(2)}) collective-permute-start(bf16[16,2,32,128]{3,2,1,0:T(8,128)(2,1)S(1)} %get-tuple-element.37), channel_id=1, source_target_pairs={{0,32},{32,0},{64,96},{96,64},{128,160},{160,128},{192,224},{224,1... | collective-permute-start | bytes 786440 | tf_op jit(solution)/shard_map/ppermute | solution.py:279
  62.6 3.7 %collective-permute-done.5 = bf16[2,16,2,32,128]{4,3,2,1,0:T(8,128)(2,1)S(1)} collective-permute-done((bf16[2,16,2,32,128]{4,3,2,1,0:T(8,128)(2,1)S(1)}, bf16[2,16,2,32,128]{4,3,2,1,0:T(8,128)(2,1)S(1)}, u32[]{:S(2)}, u32[]{:S(2)}) %collective-permute-start.5) | collective-permute-done | bytes 524320 | tf_op jit(solution)/shard_map/ppermute | solution.py:278
  66.3 1.9 %collective-permute-start.10 = (bf16[16,2,32,128]{3,2,1,0:T(8,128)(2,1)S(1)}, bf16[16,2,32,128]{3,2,1,0:T(8,128)(2,1)S(1)}, u32[]{:S(2)}, u32[]{:S(2)}) collective-permute-start(bf16[16,2,32,128]{3,2,1,0:T(8,128)(2,1)S(1)} %get-tuple-element.29), channel_id=1, source_target_pairs={{0,32},{32,0},{64,96},{96,64},{128,160},{160,128},{192,224},{224,1... | collective-permute-start | bytes 786440 | tf_op jit(solution)/shard_map/ppermute | solution.py:281
  68.2 1.5 %collective-permute-done.10.other_there = bf16[16,2,32,128]{3,2,1,0:T(8,128)(2,1)S(1)} collective-permute-done((bf16[16,2,32,128]{3,2,1,0:T(8,128)(2,1)S(1)}, bf16[16,2,32,128]{3,2,1,0:T(8,128)(2,1)S(1)}, u32[]{:S(2)}, u32[]{:S(2)}) %collective-permute-start.10) | collective-permute-done | bytes 262176 | tf_op jit(solution)/shard_map/ppermute | solution.py:281
  70.4 27.9 %all_to_all.10.got = bf16[32,2,32,128]{3,2,1,0:T(8,128)(2,1)S(1)} all-to-all(bf16[32,2,32,128]{3,2,1,0:T(8,128)(2,1)S(1)} %shard_map.84), channel_id=1, replica_groups=mesh['grp'=16,'ang'=32] {'ang'}, dimensions={0} | all-to-all | bytes 1048576 | tf_op jit(solution)/shard_map/all_to_all | solution.py:284
  98.3 1.4 %shard_map.85 = (bf16[1,2,128,1024]{3,2,1,0:T(8,128)(2,1)}, f32[32,8,128]{2,1,0:T(8,128)S(1)}) custom-call(bf16[32,2,32,128]{3,2,1,0:T(8,128)(2,1)S(1)} %all_to_all.10.got, bf16[1024,1024]{1,0:T(8,128)(2,1)S(1)} %copy-done.1, f32[256,1024]{1,0:T(8,128)S(1)} %convolution_bitcast_fusion.spec_proj), custom_call_target="tpu_custom_call" | custom-call | flops 1000000000 | bytes 1000000 | tf_op jit(solution)/shard_map/pallas_call | solution.py:229
  99.8 14.3 %all_to_all.11 = f32[32,8,128]{2,1,0:T(8,128)S(1)} all-to-all(f32[32,8,128]{2,1,0:T(8,128)S(1)} %get-tuple-element.33), channel_id=1, replica_groups=mesh['grp'=16,'ang'=32] {'ang'}, dimensions={0} | all-to-all | bytes 262144 | tf_op jit(solution)/shard_map/all_to_all | solution.py:286
  (26 shorter events, 5.6 us)
Async XLA Ops:
  0.6 57.0 %copy-start = (bf16[1,2,128,1024]{3,2,1,0:T(8,128)(2,1)S(1)}, bf16[1,2,128,1024]{3,2,1,0:T(8,128)(2,1)}, u32[]{:S(2)}) copy-start(bf16[1,2,128,1024]{3,2,1,0:T(8,128)(2,1)} %param.10) | copy-start | bytes 1572868
  0.6 8.0 %collective-permute-start.1 = (bf16[32,32,1024]{2,1,0:T(8,128)(2,1)}, bf16[32,32,1024]{2,1,0:T(8,128)(2,1)S(1)}, u32[]{:S(2)}, u32[]{:S(2)}) collective-permute-start(bf16[32,32,1024]{2,1,0:T(8,128)(2,1)} %bitcast.25), channel_id=1, source_target_pairs={{0,32},{32,0},{64,96},{96,64},{128,160},{160,128},{192,224},{224,1... | collective-permute-start | bytes 6291464 | tf_op jit(solution)/shard_map/ppermute | solution.py:253
  3.5 5.2 %collective-permute-start = (f32[4,32]{1,0:T(4,128)S(1)}, f32[4,32]{1,0:T(4,128)S(1)}, u32[]{:S(2)}, u32[]{:S(2)}) collective-permute-start(f32[4,32]{1,0:T(4,128)S(1)} %shard_map.77.refs_0_), channel_id=1, source_target_pairs={{0,32},{32,0},{64,96},{96,64},{128,160},{160,128},{192,224},{224,1... | collective-permute-start | bytes 1544 | tf_op jit(solution)/shard_map/ppermute | solution.py:256
  8.6 6.5 %copy-start.2 = (bf16[1,32,32,1024]{3,2,1,0:T(8,128)(2,1)S(1)}, bf16[1,32,32,1024]{3,2,1,0:T(8,128)(2,1)}, u32[]{:S(2)}) copy-start(bf16[1,32,32,1024]{3,2,1,0:T(8,128)(2,1)} %param.6) | copy-start | bytes 6291460
  9.8 18.9 %collective-permute-start.2 = (bf16[2,16,2,32,128]{4,3,2,1,0:T(8,128)(2,1)S(1)}, bf16[2,16,2,32,128]{4,3,2,1,0:T(8,128)(2,1)S(1)}, u32[]{:S(2)}, u32[]{:S(2)}) collective-permute-start(bf16[2,16,2,32,128]{4,3,2,1,0:T(8,128)(2,1)S(1)} %shard_map.79), channel_id=1, source_target_pairs={{0,64},{32,480},{64,128},{96,32},{128,192},{160,96},{192,256},{224... | collective-permute-start | bytes 1572872 | tf_op jit(solution)/shard_map/ppermute | solution.py:266
  19.5 15.7 %collective-permute-start.6 = (bf16[2,16,2,32,128]{4,3,2,1,0:T(8,128)(2,1)S(1)}, bf16[2,16,2,32,128]{4,3,2,1,0:T(8,128)(2,1)S(1)}, u32[]{:S(2)}, u32[]{:S(2)}) collective-permute-start(bf16[2,16,2,32,128]{4,3,2,1,0:T(8,128)(2,1)S(1)} %get-tuple-element.25), channel_id=1, source_target_pairs={{0,64},{32,480},{64,128},{96,32},{128,192},{160,96},{192,256},{224... | collective-permute-start | bytes 1572872 | tf_op jit(solution)/shard_map/ppermute | solution.py:268
  28.9 12.3 %collective-permute-start.3 = (bf16[2,16,2,32,128]{4,3,2,1,0:T(8,128)(2,1)S(1)}, bf16[2,16,2,32,128]{4,3,2,1,0:T(8,128)(2,1)S(1)}, u32[]{:S(2)}, u32[]{:S(2)}) collective-permute-start(bf16[2,16,2,32,128]{4,3,2,1,0:T(8,128)(2,1)S(1)} %add_convert_fusion.4), channel_id=1, source_target_pairs={{0,64},{32,480},{64,128},{96,32},{128,192},{160,96},{192,256},{224... | collective-permute-start | bytes 1572872 | tf_op jit(solution)/shard_map/ppermute | solution.py:272
  35.4 12.5 %collective-permute-start.7 = (bf16[2,16,2,32,128]{4,3,2,1,0:T(8,128)(2,1)S(1)}, bf16[2,16,2,32,128]{4,3,2,1,0:T(8,128)(2,1)S(1)}, u32[]{:S(2)}, u32[]{:S(2)}) collective-permute-start(bf16[2,16,2,32,128]{4,3,2,1,0:T(8,128)(2,1)S(1)} %add_convert_fusion.1), channel_id=1, source_target_pairs={{0,64},{32,480},{64,128},{96,32},{128,192},{160,96},{192,256},{224... | collective-permute-start | bytes 1572872 | tf_op jit(solution)/shard_map/ppermute | solution.py:274
  41.4 12.3 %collective-permute-start.4 = (bf16[2,16,2,32,128]{4,3,2,1,0:T(8,128)(2,1)S(1)}, bf16[2,16,2,32,128]{4,3,2,1,0:T(8,128)(2,1)S(1)}, u32[]{:S(2)}, u32[]{:S(2)}) collective-permute-start(bf16[2,16,2,32,128]{4,3,2,1,0:T(8,128)(2,1)S(1)} %add_convert_fusion.3), channel_id=1, source_target_pairs={{0,64},{32,480},{64,128},{96,32},{128,192},{160,96},{192,256},{224... | collective-permute-start | bytes 1572872 | tf_op jit(solution)/shard_map/ppermute | solution.py:275
  48.0 9.7 %copy-start.1 = (bf16[1024,1024]{1,0:T(8,128)(2,1)S(1)}, bf16[1024,1024]{1,0:T(8,128)(2,1)}, u32[]{:S(2)}) copy-start(bf16[1024,1024]{1,0:T(8,128)(2,1)} %constant.36.clone.basis) | copy-start | bytes 6291460
  48.2 12.4 %collective-permute-start.8 = (bf16[2,16,2,32,128]{4,3,2,1,0:T(8,128)(2,1)S(1)}, bf16[2,16,2,32,128]{4,3,2,1,0:T(8,128)(2,1)S(1)}, u32[]{:S(2)}, u32[]{:S(2)}) collective-permute-start(bf16[2,16,2,32,128]{4,3,2,1,0:T(8,128)(2,1)S(1)} %add_convert_fusion), channel_id=1, source_target_pairs={{0,64},{32,480},{64,128},{96,32},{128,192},{160,96},{192,256},{224... | collective-permute-start | bytes 1572872 | tf_op jit(solution)/shard_map/ppermute | solution.py:277
  53.9 12.4 %collective-permute-start.5 = (bf16[2,16,2,32,128]{4,3,2,1,0:T(8,128)(2,1)S(1)}, bf16[2,16,2,32,128]{4,3,2,1,0:T(8,128)(2,1)S(1)}, u32[]{:S(2)}, u32[]{:S(2)}) collective-permute-start(bf16[2,16,2,32,128]{4,3,2,1,0:T(8,128)(2,1)S(1)} %add_convert_fusion.2), channel_id=1, source_target_pairs={{0,64},{32,480},{64,128},{96,32},{128,192},{160,96},{192,256},{224... | collective-permute-start | bytes 1572872 | tf_op jit(solution)/shard_map/ppermute | solution.py:278
  60.6 7.5 %collective-permute-start.9 = (bf16[16,2,32,128]{3,2,1,0:T(8,128)(2,1)S(1)}, bf16[16,2,32,128]{3,2,1,0:T(8,128)(2,1)S(1)}, u32[]{:S(2)}, u32[]{:S(2)}) collective-permute-start(bf16[16,2,32,128]{3,2,1,0:T(8,128)(2,1)S(1)} %get-tuple-element.37), channel_id=1, source_target_pairs={{0,32},{32,0},{64,96},{96,64},{128,160},{160,128},{192,224},{224,1... | collective-permute-start | bytes 786440 | tf_op jit(solution)/shard_map/ppermute | solution.py:279
  66.3 3.4 %collective-permute-start.10 = (bf16[16,2,32,128]{3,2,1,0:T(8,128)(2,1)S(1)}, bf16[16,2,32,128]{3,2,1,0:T(8,128)(2,1)S(1)}, u32[]{:S(2)}, u32[]{:S(2)}) collective-permute-start(bf16[16,2,32,128]{3,2,1,0:T(8,128)(2,1)S(1)} %get-tuple-element.29), channel_id=1, source_target_pairs={{0,32},{32,0},{64,96},{96,64},{128,160},{160,128},{192,224},{224,1... | collective-permute-start | bytes 786440 | tf_op jit(solution)/shard_map/ppermute | solution.py:281
